TPU v7x, 32 devices: a whole 2x2x4 slice. The times are simulated.
32 devices in a mesh: seq: 8 (over z, x), tp: 4 (over y, core).
Axes of the slice: x: 2, y: 2, z: 4, core: 2. Of those that a mesh axis runs over, the one named last changes fastest.
Arguments:
- queries: bfloat16 [8192, 8192], P('seq', 'tp'), may hold values from -0.29882812 to 0.29882812
- key_vectors: bfloat16 [8192, 8192], P('seq', 'tp'), may hold values from -0.29882812 to 0.29882812
- value_vectors: bfloat16 [8192, 8192], P('seq', 'tp'), may hold values from -0.29882812 to 0.29882812
- log_decay: float32 [64, 8192], P('tp', 'seq'), may hold values from -1 to 0
- grad_output: bfloat16 [8192, 6144], P('seq', 'tp'), may hold values from -6 to 6
- out_weight: bfloat16 [8192, 6144], P('tp'), may hold values from -0.0625 to 0.0625
Outputs:
- grad_queries: bfloat16 [8192, 8192], P('seq', 'tp')
- grad_keys: bfloat16 [8192, 8192], P('seq', 'tp')
- grad_values: bfloat16 [8192, 8192], P('seq', 'tp')
All inputs are finite; a program needn't handle non-finite values.
Results may differ from a plain program's by a relative error of at most 0.0063.
Values may be sent and summed in bfloat16 or wider, within the bound.
No kernel may reach another device: no remote copies, remote signals or barrier semaphores. Data moves between devices by JAX's collectives and lax.ppermute only.
A program may use at most 192 MiB of HBM per device.

v0:
```python
import jax
import jax.numpy as jnp
from jax import lax
from jax.sharding import PartitionSpec as P

HD = 128
BLK = 256


def prefix(x, axis, combine, identity, reverse):
    devices, place = (lax.axis_size(axis), lax.axis_index(axis))
    everything = jax.tree.map(lambda part: lax.all_gather(part, axis), x)
    start = jax.tree.map(
        lambda part, zero: jnp.broadcast_to(jnp.asarray(zero, part.dtype), part.shape), x, identity
    )

    def hop(k, before):
        at = devices - 1 - k if reverse else k
        reached = at > place if reverse else at < place
        new = combine(before, jax.tree.map(lambda part: part[at], everything))
        return jax.tree.map(lambda a, b: jnp.where(reached, a, b), new, before)

    return lax.fori_loop(0, devices, hop, start)


def contract(form, left, right):
    return jnp.einsum(form, left, right, preferred_element_type=jnp.float32)


def key_sums(key_blk, value_blk, decay_blk):
    cum_decay = jnp.cumsum(decay_blk, axis=1)
    end_decay = cum_decay[:, -1]
    key_weight = jnp.exp(end_decay[:, None] - cum_decay).T
    key_scaled = (key_blk * key_weight[:, :, None]).astype(jnp.bfloat16)
    return (contract("sha,shb->hab", key_scaled, value_blk), end_decay)


def query_sums(query_blk, grad_blk, decay_blk):
    cum_decay = jnp.cumsum(decay_blk, axis=1)
    query_weight = jnp.exp(cum_decay).T
    query_scaled = (query_blk * query_weight[:, :, None]).astype(jnp.bfloat16)
    return contract("tha,thb->hab", query_scaled, grad_blk)


def block_terms(query_blk, key_blk, value_blk, grad_blk, decay_blk, enter_fwd, enter_bwd):
    blk_len = query_blk.shape[0]
    cum_decay = jnp.cumsum(decay_blk, axis=1)
    end_decay = cum_decay[:, -1]
    causal = (jnp.arange(blk_len)[:, None] >= jnp.arange(blk_len)[None, :])[None]
    gap_decay = jnp.where(causal, cum_decay[:, :, None] - cum_decay[:, None, :], 0.0)
    mask_mat = jnp.where(causal, jnp.exp(gap_decay), 0.0)
    grad_scores = (contract("thd,shd->hts", grad_blk, value_blk) * mask_mat).astype(jnp.bfloat16)
    attn_scores = (contract("thd,shd->hts", query_blk, key_blk) * mask_mat).astype(jnp.bfloat16)
    fwd_round = enter_fwd.astype(jnp.bfloat16)
    bwd_round = enter_bwd.astype(jnp.bfloat16)
    head_decay = jnp.exp(cum_decay).T[:, :, None]
    tail_decay = jnp.exp(end_decay[:, None] - cum_decay).T[:, :, None]
    grad_query = (
        contract("hts,shd->thd", grad_scores, key_blk)
        + contract("thb,hab->tha", grad_blk, fwd_round) * head_decay
    )
    grad_key = (
        contract("hts,thd->shd", grad_scores, query_blk)
        + contract("shb,hab->sha", value_blk, bwd_round) * tail_decay
    )
    grad_value = (
        contract("hts,thd->shd", attn_scores, grad_blk)
        + contract("sha,hab->shb", key_blk, bwd_round) * tail_decay
    )
    return (
        grad_query.astype(jnp.bfloat16),
        grad_key.astype(jnp.bfloat16),
        grad_value.astype(jnp.bfloat16),
    )


def advance(memory, inputs):
    block_state, block_end = inputs
    return (jnp.exp(block_end)[:, None, None] * memory + block_state, memory)


def chain(earlier, latter):
    return (earlier[0] + latter[0], earlier[1] * jnp.exp(latter[0])[:, None, None] + latter[1])


def local(queries, key_vectors, value_vectors, log_decay, grad_output, out_weight):
    row_count = queries.shape[0]
    head_count = queries.shape[1] // HD
    blk_count = row_count // BLK

    def split_rows(matrix):
        return matrix.reshape(blk_count, BLK, head_count, HD)

    decay_blks = log_decay.reshape(head_count, blk_count, BLK).transpose(1, 0, 2)
    key_value, end_decay = jax.vmap(key_sums)(
        split_rows(key_vectors), split_rows(value_vectors), decay_blks
    )
    zero_state = jnp.zeros((head_count, HD, HD), jnp.float32)
    local_fwd_total, local_enter_fwd = lax.scan(advance, zero_state, (key_value, end_decay))
    span_total = jnp.sum(end_decay, axis=0)
    head_grads = lax.dot_general(
        lax.all_gather(grad_output, "tp", axis=1, tiled=True),
        out_weight,
        (((1,), (1,)), ((), ())),
        preferred_element_type=jnp.float32,
    ).astype(jnp.bfloat16)
    query_grad = jax.vmap(query_sums)(split_rows(queries), split_rows(head_grads), decay_blks)
    local_bwd_total, local_enter_bwd = lax.scan(
        advance, zero_state, (query_grad, end_decay), reverse=True
    )
    identity = (jnp.zeros_like(span_total), zero_state)
    _, state_in = prefix((span_total, local_fwd_total), "seq", chain, identity, False)
    _, grad_in = prefix((span_total, local_bwd_total), "seq", chain, identity, True)
    prior_decay = jnp.cumsum(end_decay, axis=0) - end_decay
    after_decay = span_total[None, :] - jnp.cumsum(end_decay, axis=0)
    enter_fwd = local_enter_fwd + jnp.exp(prior_decay)[:, :, None, None] * state_in[None]
    enter_bwd = local_enter_bwd + jnp.exp(after_decay)[:, :, None, None] * grad_in[None]
    grad_q, grad_k, grad_v = jax.vmap(block_terms)(
        split_rows(queries),
        split_rows(key_vectors),
        split_rows(value_vectors),
        split_rows(head_grads),
        decay_blks,
        enter_fwd,
        enter_bwd,
    )

    def join_rows(blocks):
        return blocks.reshape(row_count, head_count * HD)

    return (join_rows(grad_q), join_rows(grad_k), join_rows(grad_v))


def solution(mesh):
    in_specs = (
        P("seq", "tp"),
        P("seq", "tp"),
        P("seq", "tp"),
        P("tp", "seq"),
        P("seq", "tp"),
        P("tp", None),
    )
    out_specs = (P("seq", "tp"), P("seq", "tp"), P("seq", "tp"))
    return jax.shard_map(local, mesh=mesh, in_specs=in_specs, out_specs=out_specs, check_vma=False)
```

profile of v0, /device:TPU:0, one launch (start us, length us, event | category | flops | bytes accessed | tf_op | source)
XLA Modules:
  0.0 419.4 jit_solution(11142400511651923431)
XLA Ops:
  8.8 2.3 reduce-window.6
  11.3 3.7 copy.131
  17.4 8.5 %fusion.12 = f32[4,16,128,128]{3,2,1,0:T(8,128)} fusion(f32[4,256,16]{1,2,0:T(8,128)S(1)} %get-tuple-element.482, bf16[4,256,16,128]{3,2,1,0:T(8,128)(2,1)S(1)} %bitcast.140, bf16[4,256,16,128]{3,2,1,0:T(8,128)(2,1)S(1)} %bitcast.133), kind=kOutput, calls=%fused_computation.30 | convolution fusion | flops 543162368 | bytes 12648448 | tf_op jit(solution)/shard_map/vmap(sha,shb->hab)/dot_general | solution.py:27
  25.9 2.5 broadcast.26.clone
  28.5 10.0 %while.60 = (s32[]{:T(128)}, f32[16,128,128]{2,1,0:T(8,128)S(1)}, f32[4,16,128,128]{3,2,1,0:T(8,128)}, f32[4,16]{1,0:T(4,128)S(1)}, f32[4,16,128,128]{3,2,1,0:T(8,128)}, /*index=5*/s32[]{:T(128)}, s32[]{:T(128)}) while((s32[]{:T(128)}, f32[16,128,128]{2,1,0:T(8,128)S(1)}, f32[4,16,128,128]{3,2,1,0:T(8,128)}, ...), condition=%wide.region_3.4_spmd.clone, body=%wide.region_2.3_spmd.clone.sunk | while | flops 1048579 | bytes 5243180 | solution.py:99
  39.7 5.5 %copy.133 = bf16[128,8,16,128]{3,2,1,0:T(8,128)(2,1)} copy(bf16[128,8,16,128]{3,1,2,0:T(8,128)(2,1)} %bitcast.149) | data formatting | bytes 8388608
  45.3 49.2 %all-gather.7.cloned.1.call-done = bf16[1024,6144]{1,0:T(8,128)(2,1)} async-done(((bf16[1024,1536]{1,0:T(8,128)(2,1)}), bf16[1024,6144]{1,0:T(8,128)(2,1)}) %all-gather.7.cloned.1.call-update) | async-done | bytes 12582928 | tf_op jit(solution)/shard_map/all_gather | solution.py:102
  94.4 33.2 %convert_bitcast_fusion = bf16[128,8,16,128]{3,1,2,0:T(8,128)(2,1)S(1)} fusion(bf16[1024,6144]{1,0:T(8,128)(2,1)} %all-gather.7.cloned.1.call-done, bf16[2048,6144]{1,0:T(8,128)(2,1)} %param.19), kind=kOutput, calls=%fused_computation.39 | convolution fusion | flops 25771900928 | bytes 41943040 | tf_op jit(solution)/shard_map/dot_general | solution.py:101
  127.6 3.4 copy.129
  131.0 7.5 %copy.112 = bf16[4,256,16,128]{1,3,2,0:T(8,128)(2,1)} copy(bf16[4,256,16,128]{3,2,1,0:T(8,128)(2,1)} %bitcast.143) | data formatting | bytes 8388608 | tf_op jit(solution)/shard_map/reshape | solution.py:92
  138.5 8.5 %fusion.13 = f32[4,16,128,128]{3,2,1,0:T(8,128)} fusion(bf16[4,256,16,128]{1,3,2,0:T(8,128)(2,1)} %copy.112, f32[4,256,16]{1,2,0:T(8,128)S(1)} %get-tuple-element.481, bf16[4,256,16,128]{3,2,1,0:T(8,128)(2,1)} %bitcast.137), kind=kOutput, calls=%fused_computation.31 | convolution fusion | flops 543162368 | bytes 12648448 | tf_op jit(solution)/shard_map/vmap(tha,thb->hab)/dot_general | solution.py:27
  147.0 2.7 broadcast.26.clone.1
  149.7 10.0 %while.62 = (s32[]{:T(128)}, f32[16,128,128]{2,1,0:T(8,128)S(1)}, f32[4,16,128,128]{3,2,1,0:T(8,128)}, f32[4,16]{1,0:T(4,128)S(1)}, f32[4,16,128,128]{3,2,1,0:T(8,128)}, /*index=5*/s32[]{:T(128)}, s32[]{:T(128)}, s32[]{:T(128)}) while((s32[]{:T(128)}, f32[16,128,128]{2,1,0:T(8,128)S(1)}, f32[4,16,128,128]{3,2,1,0:T(8,128)}, ...), condition=%wide.region_9.10_spmd.clone, body=%wide.region_8.9_spmd.clone.sunk | while | flops 1048580 | bytes 5243200 | solution.py:108
  162.2 22.4 %all-reduce = f32[128]{0:T(128)S(1)} all-reduce(f32[128]{0:T(128)S(1)} %dynamic-update-slice), channel_id=2, replica_groups=mesh['seq'=8,'tp'=4] {'seq'}, use_global_device_ids=true, to_apply=%add | all-reduce | flops 128 | bytes 1024
  184.8 37.4 %all-gather.9.cloned.1.call-done = f32[128,128,128]{2,1,0:T(8,128)} async-done(((f32[16,128,128]{2,1,0:T(8,128)}), f32[128,128,128]{2,1,0:T(8,128)}) %all-gather.9.cloned.1.call-update) | async-done | bytes 8388624 | tf_op jit(solution)/shard_map/all_gather | solution.py:12
  222.1 12.2 %while.61 = (s32[]{:T(128)}, f32[16,128,128]{2,1,0:T(8,128)S(1)}, s32[]{:T(128)}, f32[8,16]{1,0:T(8,128)S(1)}, f32[8,16,128,128]{3,2,1,0:T(8,128)}, /*index=5*/s32[]{:T(128)}, s32[]{:T(128)}) while((s32[]{:T(128)}, f32[16,128,128]{2,1,0:T(8,128)S(1)}, s32[]{:T(128)}, f32[8,16]{1,0:T(8,128)S(1)}, f32[8,16,128,128]{3,2,1,0:T(8,128)}, ...), condition=%wide.region_7.8_spmd.clone, body=%wide.region_6.7_spmd.clone.sunk | while | flops 1048580 | bytes 3146033 | solution.py:23
  229.7 1.6 fusion.55
  231.3 1.5 fusion.55
  234.3 8.3 %fusion.28 = f32[4,16,128,256]{2,3,1,0:T(8,128)} fusion(bf16[4,256,16,128]{1,3,2,0:T(8,128)(2,1)} %copy.112, f32[4,16,128,128]{3,2,1,0:T(8,128)} %get-tuple-element.361, f32[16,128,128]{2,1,0:T(8,128)S(1)} %get-tuple-element.363, f32[4,16]{1,0:T(4,128)S(1)} %get-tuple-element.484), kind=kOutput, calls=%fused_computation.52 | convolution fusion | flops 540016640 | bytes 17826048 | tf_op jit(solution)/shard_map/vmap(thb,hab->tha)/dot_general | solution.py:27
  242.7 7.6 %multiply_convert_fusion.1 = bf16[4,16,256,256]{3,2,1,0:T(8,128)(2,1)} fusion(bf16[4,256,16,128]{1,3,2,0:T(8,128)(2,1)S(1)} %copy-done.2, f32[4,16,256]{2,1,0:T(8,128)S(1)} %copy_bitcast_fusion.3, pred[256,256]{1,0:T(8,128)(4,1)S(1)} %iota_compare_fusion, bf16[4,256,16,128]{3,2,1,0:T(8,128)(2,1)S(1)} %bitcast.142), kind=kOutput, calls=%fused_computation.17 | convolution fusion | flops 1094713344 | bytes 16908288 | tf_op jit(solution)/shard_map/vmap(thd,shd->hts)/dot_general | solution.py:27
  250.2 7.2 %fusion.11 = bf16[4,256,16,128]{3,1,2,0:T(8,128)(2,1)S(1)} fusion(f32[4,16,128,256]{2,3,1,0:T(8,128)} %fusion.28, f32[4,256,16]{1,2,0:T(8,128)S(1)} %get-tuple-element.481, bf16[4,16,256,256]{3,2,1,0:T(8,128)(2,1)} %multiply_convert_fusion.1, bf16[4,256,16,128]{3,2,1,0:T(8,128)(2,1)S(1)} %bitcast.135), kind=kOutput, calls=%fused_computation.27 | convolution fusion | flops 1080033280 | bytes 25231360 | tf_op jit(solution)/shard_map/vmap(hts,shd->thd)/dot_general | solution.py:27
  257.5 2.7 copy.101
  260.2 4.1 copy.179
  264.3 83.1 %all-gather.11.cloned.1.call-done = f32[128,128,128]{2,1,0:T(8,128)} async-done(((f32[16,128,128]{2,1,0:T(8,128)}), f32[128,128,128]{2,1,0:T(8,128)}) %all-gather.11.cloned.1.call-update) | async-done | bytes 8388624 | tf_op jit(solution)/shard_map/all_gather | solution.py:12
  347.4 12.4 %while.63 = (s32[]{:T(128)}, f32[16,128,128]{2,1,0:T(8,128)S(1)}, s32[]{:T(128)}, f32[8,16]{1,0:T(8,128)S(1)}, f32[8,16,128,128]{3,2,1,0:T(8,128)}, /*index=5*/s32[]{:T(128)}, s32[]{:T(128)}, s32[]{:T(128)}, s32[]{:T(128)}) while((s32[]{:T(128)}, f32[16,128,128]{2,1,0:T(8,128)S(1)}, s32[]{:T(128)}, f32[8,16]{1,0:T(8,128)S(1)}, ...), condition=%wide.region_11.12_spmd.clone, body=%wide.region_10.11_spmd.clone.sunk | while | flops 1048584 | bytes 3146095 | solution.py:23
  359.9 8.4 %fusion.19 = f32[4,16,128,256]{2,3,1,0:T(8,128)} fusion(bf16[4,256,16,128]{3,2,1,0:T(8,128)(2,1)} %bitcast.141, f32[4,16,128,128]{3,2,1,0:T(8,128)} %get-tuple-element.364, f32[16,128,128]{2,1,0:T(8,128)S(1)} %get-tuple-element.366, f32[4,16]{1,0:T(4,128)S(1)} %get-tuple-element.483), kind=kOutput, calls=%fused_computation.43 | convolution fusion | flops 540016640 | bytes 17826048 | tf_op jit(solution)/shard_map/vmap(shb,hab->sha)/dot_general | solution.py:27
  368.2 4.9 %fusion.23 = f32[4,16,128,256]{2,3,1,0:T(8,128)} fusion(bf16[4,256,16,128]{3,2,1,0:T(8,128)(2,1)S(1)} %bitcast.136, f32[4,16,128,128]{3,2,1,0:T(8,128)S(1)} %copy-done.3, f32[16,128,128]{2,1,0:T(8,128)S(1)} %get-tuple-element.366, f32[4,16]{1,0:T(4,128)S(1)} %get-tuple-element.483), kind=kOutput, calls=%fused_computation.47 | convolution fusion | flops 540016640 | bytes 17826048 | tf_op jit(solution)/shard_map/vmap(sha,hab->shb)/dot_general | solution.py:27
  373.1 8.5 %fusion.9 = bf16[4,256,16,128]{3,1,2,0:T(8,128)(2,1)S(1)} fusion(f32[4,16,128,256]{2,3,1,0:T(8,128)} %fusion.19, f32[4,256,16]{1,2,0:T(8,128)S(1)} %get-tuple-element.482, bf16[4,16,256,256]{3,2,1,0:T(8,128)(2,1)} %multiply_convert_fusion.1, bf16[4,256,16,128]{3,2,1,0:T(8,128)(2,1)S(1)} %bitcast.139), kind=kOutput, calls=%fused_computation.24 | convolution fusion | flops 1080033280 | bytes 25231360 | tf_op jit(solution)/shard_map/vmap(hts,thd->shd)/dot_general | solution.py:27
  381.6 4.7 %copy.109 = bf16[4,256,16,128]{3,2,1,0:T(8,128)(2,1)} copy(bf16[4,256,16,128]{3,1,2,0:T(8,128)(2,1)S(1)} %fusion.9) | data formatting | bytes 8388608 | tf_op jit(solution)/shard_map/vmap()/convert_element_type | solution.py:72
  386.3 14.8 %fusion.7 = bf16[4,256,16,128]{3,1,2,0:T(8,128)(2,1)} fusion(f32[4,16,128,256]{2,3,1,0:T(8,128)} %fusion.23, f32[4,256,16]{1,2,0:T(8,128)S(1)} %get-tuple-element.482, bf16[4,256,16,128]{1,3,2,0:T(8,128)(2,1)} %copy.112, f32[4,16,256]{2,1,0:T(8,128)S(1)} %copy_bitcast_fusion.3, pred[256,256]{1,0:T(8,128)(4,1)S(1)} %iota_compare_fusion, ...), kind=kOutput, calls=%fused_computation.21 | convolution fusion | flops 2174746624 | bytes 25362432 | tf_op jit(solution)/shard_map/vmap(hts,thd->shd)/dot_general | solution.py:27
  401.1 5.0 %copy.117 = bf16[4,256,16,128]{3,2,1,0:T(8,128)(2,1)S(1)} copy(bf16[4,256,16,128]{3,1,2,0:T(8,128)(2,1)} %fusion.7) | data formatting | bytes 8388608 | tf_op jit(solution)/shard_map/vmap()/convert_element_type | solution.py:73
  406.1 6.6 %copy_bitcast_fusion = (bf16[1024,2048]{1,0:T(8,128)(2,1)}, bf16[1024,2048]{1,0:T(8,128)(2,1)}) fusion(bf16[128,8,16,128]{3,2,1,0:T(8,128)(2,1)S(1)} %bitcast.146, bf16[128,8,16,128]{3,2,1,0:T(8,128)(2,1)S(1)} %bitcast.145), kind=kLoop, calls=%fused_computation.32 | loop fusion | bytes 16777216 | tf_op jit(solution)/shard_map/reshape | solution.py:129
  (107 shorter events, 47.8 us)
Async XLA Ops:
  7.2 87.3 %all-gather.7.cloned.1.call-start = ((), (), s32[]{:S(2)}) async-start(), calls=%async_computation | async-start | bytes 15728640 | tf_op jit(solution)/shard_map/all_gather | solution.py:102
  7.9 214.2 %all-gather.9.cloned.1.call-start = ((), (), s32[]{:S(2)}) async-start(), calls=%async_computation.1 | async-start | bytes 9437184 | tf_op jit(solution)/shard_map/all_gather | solution.py:12
  11.3 3.8 copy-start.11
  15.0 2.3 copy-start.4
  16.5 9.4 %copy-start.8 = (bf16[128,8,16,128]{3,2,1,0:T(8,128)(2,1)}, bf16[128,8,16,128]{3,2,1,0:T(8,128)(2,1)S(1)}, u32[]{:S(2)}) copy-start(bf16[128,8,16,128]{3,2,1,0:T(8,128)(2,1)S(1)} %copy.130) | copy-start | bytes 12582916
  38.5 1.0 copy-start
  39.5 307.9 %all-gather.11.cloned.1.call-start = ((), (), s32[]{:S(2)}) async-start(), calls=%async_computation.2 | async-start | bytes 9437184 | tf_op jit(solution)/shard_map/all_gather | solution.py:12
  149.7 11.1 %copy-start.12 = (u32[32]{0:T(128)S(1)}, u32[32]{0:T(128)}, u32[]{:S(2)}) copy-start(u32[32]{0:T(128)} %constant.134) | copy-start | bytes 388
  159.7 0.9 copy-start.1
  234.3 8.3 %copy-start.2 = (bf16[4,256,16,128]{1,3,2,0:T(8,128)(2,1)S(1)}, bf16[4,256,16,128]{1,3,2,0:T(8,128)(2,1)}, u32[]{:S(2)}) copy-start(bf16[4,256,16,128]{1,3,2,0:T(8,128)(2,1)} %copy.112) | copy-start | bytes 12582916
  234.3 8.3 %copy-start.9 = (bf16[128,8,16,128]{3,2,1,0:T(8,128)(2,1)S(1)}, bf16[128,8,16,128]{3,2,1,0:T(8,128)(2,1)}, u32[]{:S(2)}) copy-start(bf16[128,8,16,128]{3,2,1,0:T(8,128)(2,1)} %copy-done.8) | copy-start | bytes 12582916
  242.7 7.6 %copy-start.5 = (bf16[128,8,16,128]{3,2,1,0:T(8,128)(2,1)S(1)}, bf16[128,8,16,128]{3,2,1,0:T(8,128)(2,1)}, u32[]{:S(2)}) copy-start(bf16[128,8,16,128]{3,2,1,0:T(8,128)(2,1)} %copy-done.4) | copy-start | bytes 12582916
  359.8 8.4 %copy-start.3 = (f32[4,16,128,128]{3,2,1,0:T(8,128)S(1)}, f32[4,16,128,128]{3,2,1,0:T(8,128)}, u32[]{:S(2)}) copy-start(f32[4,16,128,128]{3,2,1,0:T(8,128)} %get-tuple-element.364) | copy-start | bytes 12582916
  359.9 8.4 %copy-start.6 = (bf16[128,8,16,128]{3,2,1,0:T(8,128)(2,1)S(1)}, bf16[128,8,16,128]{3,2,1,0:T(8,128)(2,1)}, u32[]{:S(2)}) copy-start(bf16[128,8,16,128]{3,2,1,0:T(8,128)(2,1)} %copy-done.4) | copy-start | bytes 12582916
  368.2 4.9 %copy-start.7 = (bf16[128,8,16,128]{3,2,1,0:T(8,128)(2,1)S(1)}, bf16[128,8,16,128]{3,2,1,0:T(8,128)(2,1)}, u32[]{:S(2)}) copy-start(bf16[128,8,16,128]{3,2,1,0:T(8,128)(2,1)} %copy.133) | copy-start | bytes 12582916
  401.1 5.1 %copy-start.10 = (bf16[4,256,16,128]{3,2,1,0:T(8,128)(2,1)S(1)}, bf16[4,256,16,128]{3,2,1,0:T(8,128)(2,1)}, u32[]{:S(2)}) copy-start(bf16[4,256,16,128]{3,2,1,0:T(8,128)(2,1)} %copy.109) | copy-start | bytes 12582916
Sparse Core Ops, SparseCore 0:
  9.6 84.8 all-gather.6
  96.5 125.5 all-gather.8
  224.3 123.1 all-gather.10
where the time goes:
time: 424 us; the launch traced here: 419 us
  waiting for transfers between devices  170 us (40%)
  matrix products  110 us (26%)
  local copies, waits for them, and re-layouts  54.6 us (13%)
  other arithmetic  46.1 us (11%)
  blocking collectives  22.4 us (5%)
  between operations  14.9 us (4%)
    all_gather x2, waiting for transfers between devices, prefix(): everything = jax.tree.map(lambda part: lax.all_gather(part, axis), x)  120 us
    dot_general x9, matrix products, contract(): return jnp.einsum(form, left, right, preferred_element_type=jnp.float32)  76.7 us
    all_gather x1, waiting for transfers between devices, local(): lax.all_gather(grad_output, 'tp', axis=1, tiled=True)  49.2 us
    dot_general x1, matrix products, local(): lax.dot_general(lax.all_gather(grad_output, 'tp', axis=1, tiled=True), ou...  33.2 us
    select_n x16, other arithmetic, hop(): return jax.tree.map(lambda a, b: jnp.where(reached, a, b), new, before)  23.5 us
    unnamed x1, blocking collectives  22.4 us
    unnamed x34, local copies, waits for them, and re-layouts  21.6 us
    add x8, other arithmetic, advance(): return (jnp.exp(block_end)[:, None, None] * memory + block_state, memory)  11.4 us
  transfers between devices with their start and end apart: 3, of which 3 were waited for; matrix products, arithmetic and copies ran while one was open for 34% of the time, Pallas kernels for 0%

commit v1 on v0

v1 whole, which is shorter than its diff:
```python
import functools

import jax
import jax.numpy as jnp
from jax import lax
from jax.experimental import pallas as pl
from jax.experimental.pallas import tpu as pltpu
from jax.sharding import PartitionSpec as P

HD = 128
BLK = 256
VMEM_BYTES = 56 * 2**20

NN = (((1,), (0,)), ((), ()))
NT = (((1,), (1,)), ((), ()))
TN = (((0,), (0,)), ((), ()))


def mm(left, right, form):
    return lax.dot_general(left, right, form, preferred_element_type=jnp.float32)


def params(grid_dims):
    return pltpu.CompilerParams(
        dimension_semantics=("arbitrary",) * grid_dims, vmem_limit_bytes=VMEM_BYTES
    )


def cost(flops, nbytes, exps=0):
    return pl.CostEstimate(flops=int(flops), bytes_accessed=int(nbytes), transcendentals=int(exps))


def head_lanes(h):
    return slice(h * HD, (h + 1) * HD)


def key_body(group, k_ref, v_ref, cum_ref, kv_ref, total_ref, carry_ref):
    blk, blk_count = pl.program_id(1), pl.num_programs(1)
    cum = cum_ref[0].T
    end = cum[BLK - 1 : BLK, :]
    weight = jnp.exp(end - cum)
    end_weight = jnp.exp(end)

    @pl.when(blk == 0)
    def _():
        carry_ref[...] = jnp.zeros_like(carry_ref)

    for h in range(group):
        lanes = head_lanes(h)
        scaled = (k_ref[:, lanes].astype(jnp.float32) * weight[:, h : h + 1]).astype(jnp.bfloat16)
        kv = mm(scaled, v_ref[:, lanes], TN)
        kv_ref[0, h] = kv
        carry_ref[h] = carry_ref[h] * end_weight[:, h : h + 1] + kv

    @pl.when(blk == blk_count - 1)
    def _():
        total_ref[...] = carry_ref[...].astype(total_ref.dtype)


def key_totals(keys, values, cum, group):
    rows, width = keys.shape
    heads, blk_count = width // HD, rows // BLK
    tokens = pl.BlockSpec((BLK, group * HD), lambda g, j: (j, g))
    return pl.pallas_call(
        functools.partial(key_body, group),
        grid=(heads // group, blk_count),
        in_specs=[tokens, tokens, pl.BlockSpec((1, group, BLK), lambda g, j: (g, 0, j))],
        out_specs=[
            pl.BlockSpec((1, group, HD, HD), lambda g, j: (j, g, 0, 0)),
            pl.BlockSpec((group, HD, HD), lambda g, j: (g, 0, 0)),
        ],
        out_shape=[
            jax.ShapeDtypeStruct((blk_count, heads, HD, HD), jnp.float32),
            jax.ShapeDtypeStruct((heads, HD, HD), jnp.bfloat16),
        ],
        scratch_shapes=[pltpu.VMEM((group, HD, HD), jnp.float32)],
        compiler_params=params(2),
        cost_estimate=cost(2 * rows * width * HD, 4 * rows * width + 4 * blk_count * width * HD),
        name="key_totals",
    )(keys, values, cum)


def near_body(count, ids_ref, *refs):
    total = mm(refs[0][...], refs[count][...], NT)
    for piece in range(1, count):
        total += mm(refs[piece][...], refs[count + piece][...], NT)
    refs[2 * count][...] = total


def near_product(ids, pieces, weight, wide):
    rows, depth = pieces[0].shape
    width, count = weight.shape[0], len(pieces)
    held = pl.BlockSpec((rows, depth), lambda g, ids: (0, 0))
    columns = [pl.BlockSpec((wide, depth), lambda g, ids, n=n: (g, ids[n])) for n in range(count)]
    return pl.pallas_call(
        functools.partial(near_body, count),
        grid_spec=pltpu.PrefetchScalarGridSpec(
            num_scalar_prefetch=1,
            grid=(width // wide,),
            in_specs=[held] * count + columns,
            out_specs=pl.BlockSpec((rows, wide), lambda g, ids: (0, g)),
        ),
        out_shape=jax.ShapeDtypeStruct((rows, width), jnp.float32),
        compiler_params=params(1),
        cost_estimate=cost(
            2 * rows * width * depth * count,
            2 * count * depth * (rows + width) + 4 * rows * width,
        ),
        name="near_product",
    )(ids, *pieces, *([weight] * count))


def far_body(count, group, ids_ref, before_ref, *refs):
    near_ref, q_ref, cum_ref, prior_ref, grad_ref, sums_ref, total_ref = refs[2 * count :]
    total = near_ref[...]
    for piece in range(count):
        total += mm(refs[piece][...], refs[count + piece][...], NT)
    grad_ref[...] = total.astype(jnp.bfloat16)
    cum = cum_ref[0].T
    weight = jnp.exp(cum)
    for h in range(group):
        lanes = head_lanes(h)
        scaled = (q_ref[:, lanes].astype(jnp.float32) * weight[:, h : h + 1]).astype(jnp.bfloat16)
        sums = mm(scaled, grad_ref[:, lanes], TN)
        sums_ref[h] = sums
        prior = prior_ref[pl.program_id(0) * group + h]
        total_ref[h] = (before_ref[h] + prior * sums).astype(total_ref.dtype)


def far_product(ids, before, pieces, weight, near, queries, cum, prior, blk, last):
    rows, depth = pieces[0].shape
    width, count = weight.shape[0], len(pieces)
    groups, group = cum.shape[0], cum.shape[1]
    wide, heads = group * HD, width // HD
    held = pl.BlockSpec((rows, depth), lambda g, ids: (0, 0))
    columns = [pl.BlockSpec((wide, depth), lambda g, ids, n=n: (g, ids[n])) for n in range(count)]
    tokens = pl.BlockSpec((rows, wide), lambda g, ids: (blk, g))
    states = pl.BlockSpec((group, HD, HD), lambda g, ids: (g, 0, 0))
    return pl.pallas_call(
        functools.partial(far_body, count, group),
        grid_spec=pltpu.PrefetchScalarGridSpec(
            num_scalar_prefetch=1,
            grid=(groups,),
            in_specs=[states]
            + [held] * count
            + columns
            + [
                tokens,
                tokens,
                pl.BlockSpec((1, group, rows), lambda g, ids: (g, 0, blk)),
                pl.BlockSpec(memory_space=pltpu.SMEM),
            ],
            out_specs=[pl.BlockSpec((rows, wide), lambda g, ids: (0, g)), states, states],
        ),
        out_shape=[
            jax.ShapeDtypeStruct((rows, width), jnp.bfloat16),
            jax.ShapeDtypeStruct((heads, HD, HD), jnp.float32),
            jax.ShapeDtypeStruct((heads, HD, HD), jnp.bfloat16 if last else jnp.float32),
        ],
        compiler_params=params(1),
        cost_estimate=cost(
            2 * rows * width * (depth * count + HD),
            2 * count * depth * (rows + width) + 8 * rows * width + 12 * width * HD,
        ),
        name="far_product",
    )(ids, before, *pieces, *([weight] * count), near, queries, cum, prior)


def block_body(group, blk_count, *refs):
    q_ref, k_ref, v_ref = refs[:3]
    grad_refs = refs[3 : 3 + blk_count]
    cum_ref, kv_ref, enter_ref, gq_ref, gk_ref, gv_ref, carry_ref, grad_ref = refs[3 + blk_count :]
    blk = pl.program_id(1)

    @pl.when(blk == 0)
    def _():
        carry_ref[...] = enter_ref[...].astype(jnp.float32)

    for j in range(blk_count):

        @pl.when(blk == j)
        def _(j=j):
            grad_ref[...] = grad_refs[j][...]

    rows = cum_ref[0]
    cum = rows.T
    head_weight = jnp.exp(cum)
    end_weight = head_weight[BLK - 1 : BLK, :]
    causal = lax.broadcasted_iota(jnp.int32, (BLK, BLK), 0) >= lax.broadcasted_iota(
        jnp.int32, (BLK, BLK), 1
    )
    for h in range(group):
        lanes = head_lanes(h)
        q, k, v, grad = q_ref[:, lanes], k_ref[:, lanes], v_ref[:, lanes], grad_ref[:, lanes]
        gap = jnp.where(causal, cum[:, h : h + 1] - rows[h : h + 1, :], -1e30)
        mask = jnp.exp(gap)
        grad_scores = (mm(grad, v, NT) * mask).astype(jnp.bfloat16)
        attn_scores = (mm(q, k, NT) * mask).astype(jnp.bfloat16)
        enter = carry_ref[h]
        gq = mm(grad_scores, k, NN)
        gq += mm(grad, enter.astype(jnp.bfloat16), NT) * head_weight[:, h : h + 1]
        gq_ref[:, lanes] = gq.astype(jnp.bfloat16)
        gk_ref[:, lanes] = mm(grad_scores, q, TN).astype(jnp.bfloat16)
        gv_ref[:, lanes] = mm(attn_scores, grad, TN).astype(jnp.bfloat16)
        carry_ref[h] = enter * end_weight[:, h : h + 1] + kv_ref[0, h]


def block_terms(queries, keys, values, grads, cum, kv, enter):
    rows, width = queries.shape
    heads, blk_count = width // HD, rows // BLK
    groups, group = cum.shape[0], cum.shape[1]
    tokens = pl.BlockSpec((BLK, group * HD), lambda g, j: (j, g))
    part = pl.BlockSpec((BLK, group * HD), lambda g, j: (0, g))
    out = jax.ShapeDtypeStruct((rows, width), jnp.bfloat16)
    return pl.pallas_call(
        functools.partial(block_body, group, blk_count),
        grid=(groups, blk_count),
        in_specs=[tokens] * 3
        + [part] * blk_count
        + [
            pl.BlockSpec((1, group, BLK), lambda g, j: (g, 0, j)),
            pl.BlockSpec((1, group, HD, HD), lambda g, j: (j, g, 0, 0)),
            pl.BlockSpec((group, HD, HD), lambda g, j: (g, 0, 0)),
        ],
        out_specs=[tokens] * 3,
        out_shape=[out] * 3,
        scratch_shapes=[
            pltpu.VMEM((group, HD, HD), jnp.float32),
            pltpu.VMEM((BLK, group * HD), jnp.bfloat16),
        ],
        compiler_params=params(2),
        cost_estimate=cost(
            rows * width * (10 * BLK + 2 * HD),
            14 * rows * width + 4 * blk_count * width * HD,
            rows * heads * BLK,
        ),
        name="block_terms",
    )(queries, keys, values, *grads, cum, kv, enter)


def later_body(group, blk_count, *refs):
    k_ref, v_ref, gk_in_ref, gv_in_ref = refs[:4]
    sums_refs = refs[4 : 4 + blk_count]
    cum_ref, enter_ref, gk_ref, gv_ref, carry_ref = refs[4 + blk_count :]
    blk = blk_count - 1 - pl.program_id(1)

    @pl.when(blk == blk_count - 1)
    def _():
        carry_ref[...] = enter_ref[...].astype(jnp.float32)

    cum = cum_ref[0].T
    end = cum[BLK - 1 : BLK, :]
    weight = jnp.exp(end - cum)
    end_weight = jnp.exp(end)
    for h in range(group):
        lanes = head_lanes(h)
        tail = weight[:, h : h + 1]
        enter = carry_ref[h].astype(jnp.bfloat16)
        gk = gk_in_ref[:, lanes].astype(jnp.float32) + mm(v_ref[:, lanes], enter, NT) * tail
        gv = gv_in_ref[:, lanes].astype(jnp.float32) + mm(k_ref[:, lanes], enter, NN) * tail
        gk_ref[:, lanes] = gk.astype(jnp.bfloat16)
        gv_ref[:, lanes] = gv.astype(jnp.bfloat16)
    for j in range(1, blk_count):

        @pl.when(blk == j)
        def _(j=j):
            for h in range(group):
                carry_ref[h] = carry_ref[h] * end_weight[:, h : h + 1] + sums_refs[j][h]


def later_terms(keys, values, gk, gv, sums, cum, enter):
    rows, width = keys.shape
    blk_count = rows // BLK
    groups, group = cum.shape[0], cum.shape[1]
    tokens = pl.BlockSpec((BLK, group * HD), lambda g, j: (blk_count - 1 - j, g))
    states = pl.BlockSpec((group, HD, HD), lambda g, j: (g, 0, 0))
    out = jax.ShapeDtypeStruct((rows, width), jnp.bfloat16)
    return pl.pallas_call(
        functools.partial(later_body, group, blk_count),
        grid=(groups, blk_count),
        in_specs=[tokens] * 4
        + [states] * blk_count
        + [pl.BlockSpec((1, group, BLK), lambda g, j: (g, 0, blk_count - 1 - j)), states],
        out_specs=[tokens] * 2,
        out_shape=[out] * 2,
        scratch_shapes=[pltpu.VMEM((group, HD, HD), jnp.float32)],
        input_output_aliases={2: 0, 3: 1},
        compiler_params=params(2),
        cost_estimate=cost(
            rows * width * 4 * HD, 12 * rows * width + 4 * blk_count * width * HD
        ),
        name="later_terms",
    )(keys, values, gk, gv, *sums, cum, enter)


def span_states(totals, spans, reverse):
    devices = lax.axis_size("seq")
    heads = totals.shape[0]
    share = heads * HD // devices
    flat = totals.reshape(heads * HD, HD)
    got = lax.all_to_all(flat, "seq", 0, 0, tiled=True).reshape(devices, share, HD)
    by_row = jnp.repeat(jnp.exp(spans), HD, axis=1)
    mine = lax.dynamic_slice_in_dim(by_row, lax.axis_index("seq") * share, share, axis=1)
    carry = jnp.zeros((share, HD), jnp.float32)
    out = [None] * devices
    for place in reversed(range(devices)) if reverse else range(devices):
        out[place] = carry.astype(jnp.bfloat16)
        carry = mine[place][:, None] * carry + got[place].astype(jnp.float32)
    back = lax.all_to_all(jnp.concatenate(out, axis=0), "seq", 0, 0, tiled=True)
    return back.reshape(heads, HD, HD)


def local(queries, key_vectors, value_vectors, log_decay, grad_output, out_weight):
    rows, width = queries.shape
    heads, blk_count = width // HD, rows // BLK
    tp, me = lax.axis_size("tp"), lax.axis_index("tp")
    chips = tp // 2
    core = [(i, i ^ 1) for i in range(tp)]

    def from_chip(hops):
        return [(i, (i + 2 * hops) % tp) for i in range(tp)]

    ids = jnp.stack(
        [lax.rem(me + tp - 2 * d, tp) ^ e for d in range(chips) for e in range(2)]
    ).astype(jnp.int32)
    own = grad_output
    far = []
    for j in range(blk_count):
        piece = own[j * BLK : (j + 1) * BLK]
        arrived = []
        for d in range(1, chips):
            first = lax.ppermute(piece, "tp", from_chip(d))
            arrived += [first, lax.ppermute(first, "tp", core)]
        far.append(arrived)
    sibling = lax.ppermute(own, "tp", core)

    cum = jnp.cumsum(log_decay.reshape(heads, blk_count, BLK), axis=2)
    end = cum[:, :, -1]
    spans = lax.all_gather(jnp.sum(end, axis=1), "seq")
    prior = jnp.exp(jnp.cumsum(end, axis=1) - end)
    group = 4
    cum4 = cum.reshape(heads // group, group, rows)

    kv, fwd_total = key_totals(key_vectors, value_vectors, cum4, group)
    enter_fwd = span_states(fwd_total, spans, False)

    near = near_product(ids[:2], [own, sibling], out_weight, 256)
    total = jnp.zeros((heads, HD, HD), jnp.float32)
    grads, sums = [], []
    for j in range(blk_count):
        grad, part, total = far_product(
            ids[2:],
            total,
            far[j],
            out_weight,
            near,
            queries,
            cum4,
            prior[:, j],
            j,
            j == blk_count - 1,
        )
        grads.append(grad)
        sums.append(part)
    enter_bwd = span_states(total, spans, True)
    gq, gk, gv = block_terms(queries, key_vectors, value_vectors, grads, cum4, kv, enter_fwd)
    gk, gv = later_terms(key_vectors, value_vectors, gk, gv, sums, cum4, enter_bwd)
    return gq, gk, gv


def solution(mesh):
    in_specs = (
        P("seq", "tp"),
        P("seq", "tp"),
        P("seq", "tp"),
        P("tp", "seq"),
        P("seq", "tp"),
        P("tp", None),
    )
    out_specs = (P("seq", "tp"), P("seq", "tp"), P("seq", "tp"))
    return jax.shard_map(local, mesh=mesh, in_specs=in_specs, out_specs=out_specs, check_vma=False)
```

time: 424 us -> 252 us (0.59)
  Pallas kernels: 0 us -> 130 us
  waiting for transfers between devices: 170 us -> 48.4 us
  matrix products: 110 us -> 0 us
  local copies, waits for them, and re-layouts: 54.6 us -> 12.1 us
  other arithmetic: 46.1 us -> 11.3 us
  starting transfers between devices: 0.29 us -> 24.7 us
  between operations: 14.9 us -> 1.51 us
    all_gather x3 -> x0, waiting for transfers between devices: 170 us -> none  [the longest x2 120 us: prefix(): everything = jax.tree.map(lambda part: lax.all_gather(part, axis), x)]
    pallas_call x0 -> x8, Pallas kernels: none -> 130 us  [the longest x4 45 us: far_product(): pl.pallas_call(functools.partial(far_body, count, group), grid_spec=pltpu...]
    dot_general x10 -> x0, matrix products: 110 us -> none  [the longest x9 76.7 us: contract(): return jnp.einsum(form, left, right, preferred_element_type=jnp.float32)]
    ppermute x0 -> x9, waiting for transfers between devices: none -> 38.8 us  [the longest x4 38.8 us: local(): first = lax.ppermute(piece, 'tp', from_chip(d))]
    select_n x16 -> x0, other arithmetic: 23.5 us -> none  [hop(): return jax.tree.map(lambda a, b: jnp.where(reached, a, b), new, before)]
    all_to_all x0 -> x4, starting transfers between devices: none -> 19.5 us  [the longest x2 12.3 us: span_states(): lax.all_to_all(flat, 'seq', 0, 0, tiled=True).reshape(devices, share, HD)]
    unnamed x34 -> x28, local copies, waits for them, and re-layouts: 21.6 us -> 5.03 us
    reshape x3 -> x2, local copies, waits for them, and re-layouts: 14.9 us -> 0.08 us  [the longest x1 7.46 us: split_rows(): return matrix.reshape(blk_count, BLK, head_count, HD)]
  transfers between devices with their start and end apart: 3 -> 13, of which waited for: 3 -> 4; matrix products, arithmetic and copies ran while one was open for 34% -> 6% of each run, Pallas kernels for 0% -> 44%
where the time goes in v1:
time: 252 us; the launch traced here: 250 us
  Pallas kernels  130 us (52%)
  waiting for transfers between devices  48.4 us (19%)
  starting transfers between devices  24.7 us (10%)
  blocking collectives  22.7 us (9%)
  local copies, waits for them, and re-layouts  12.1 us (5%)
  other arithmetic  11.3 us (4%)
    pallas_call x4, Pallas kernels, far_product(): pl.pallas_call(functools.partial(far_body, count, group), grid_spec=pltpu...  45 us
    ppermute x4, waiting for transfers between devices, local(): first = lax.ppermute(piece, 'tp', from_chip(d))  38.8 us
    pallas_call x1, Pallas kernels, block_terms(): pl.pallas_call(functools.partial(block_body, group, blk_count), grid=(gro...  29.7 us
    unnamed x1, blocking collectives  22.7 us
    pallas_call x1, Pallas kernels, near_product(): pl.pallas_call(functools.partial(near_body, count), grid_spec=pltpu.Prefe...  20 us
    pallas_call x1, Pallas kernels, later_terms(): pl.pallas_call(functools.partial(later_body, group, blk_count), grid=(gro...  18.8 us
    pallas_call x1, Pallas kernels, key_totals(): pl.pallas_call(functools.partial(key_body, group), grid=(heads // group,...  16.2 us
    all_to_all x2, starting transfers between devices, span_states(): lax.all_to_all(flat, 'seq', 0, 0, tiled=True).reshape(devices, share, HD)  12.3 us
  transfers between devices with their start and end apart: 13, of which 4 were waited for; matrix products, arithmetic and copies ran while one was open for 6% of the time, Pallas kernels for 44%

profile of v1, /device:TPU:0, one launch (start us, length us, event | category | flops | bytes accessed | tf_op | source)
XLA Modules:
  0.0 250.4 jit_solution(14007005785717766728)
XLA Ops:
  1.2 3.6 %fusion.22 = (bf16[256,1536]{1,0:T(8,128)(2,1)}, bf16[256,1536]{1,0:T(8,128)(2,1)}, bf16[256,1536]{1,0:T(8,128)(2,1)}, bf16[256,1536]{1,0:T(8,128)(2,1)}) fusion(bf16[1024,1536]{1,0:T(8,128)(2,1)} %refs_0_.3), kind=kLoop, calls=%fused_computation.72 | loop fusion | bytes 6291456 | tf_op jit(solution)/shard_map/slice | solution.py:329
  4.7 2.5 %collective-permute-start.7 = (bf16[256,1536]{1,0:T(8,128)(2,1)}, bf16[256,1536]{1,0:T(8,128)(2,1)S(1)}, u32[]{:S(2)}, u32[]{:S(2)}) collective-permute-start(bf16[256,1536]{1,0:T(8,128)(2,1)} %get-tuple-element.47), channel_id=1, source_target_pairs={{0,2},{1,3},{2,0},{3,1},{4,6},{5,7},{6,4},{7,5},{8,10},{9,11},{10,... | collective-permute-start | bytes 2359304 | tf_op jit(solution)/shard_map/ppermute | solution.py:332
  7.3 2.0 collective-permute-start
  9.4 2.3 reduce-window.6
  12.7 16.2 %key_totals.1 = (f32[4,16,128,128]{3,2,1,0:T(8,128)}, bf16[16,128,128]{2,1,0:T(8,128)(2,1)}) custom-call(bf16[1024,2048]{1,0:T(8,128)(2,1)} %refs_0_.5, bf16[1024,2048]{1,0:T(8,128)(2,1)} %refs_1_.3, f32[4,4,1024]{2,1,0:T(4,128)} %reduce_window_sum.31.refs_6_.cum_ref.refs_7_.refs_8_), custom_call_target="tpu_custom_call" | custom-call | flops 536870912 | bytes 12582912 | tf_op jit(solution)/shard_map/key_totals/pallas_call | solution.py:64
  29.0 6.3 %all-to-all-start = ((bf16[8,256,128]{2,1,0:T(8,128)(2,1)}), bf16[8,256,128]{2,1,0:T(8,128)(2,1)S(1)}, u32[]{:S(2)}, u32[]{:S(2)}) async-start(bf16[8,256,128]{2,1,0:T(8,128)(2,1)} %bitcast.175), calls=%async_computation | async-start | bytes 1048576 | tf_op jit(solution)/shard_map/all_to_all | solution.py:301
  37.5 5.3 %collective-permute-done.3.refs_0_ = bf16[256,1536]{1,0:T(8,128)(2,1)S(1)} collective-permute-done((bf16[256,1536]{1,0:T(8,128)(2,1)}, bf16[256,1536]{1,0:T(8,128)(2,1)S(1)}, u32[]{:S(2)}, u32[]{:S(2)}) %collective-permute-start.3) | collective-permute-done | bytes 786464 | tf_op jit(solution)/shard_map/ppermute | solution.py:332
  42.7 17.0 %collective-permute-done.refs_0_ = bf16[256,1536]{1,0:T(8,128)(2,1)} collective-permute-done((bf16[256,1536]{1,0:T(8,128)(2,1)}, bf16[256,1536]{1,0:T(8,128)(2,1)}, u32[]{:S(2)}, u32[]{:S(2)}) %collective-permute-start) | collective-permute-done | bytes 786464 | tf_op jit(solution)/shard_map/ppermute | solution.py:332
  59.7 16.5 %collective-permute-done.5.refs_0_ = bf16[256,1536]{1,0:T(8,128)(2,1)S(1)} collective-permute-done((bf16[256,1536]{1,0:T(8,128)(2,1)}, bf16[256,1536]{1,0:T(8,128)(2,1)S(1)}, u32[]{:S(2)}, u32[]{:S(2)}) %collective-permute-start.5) | collective-permute-done | bytes 786464 | tf_op jit(solution)/shard_map/ppermute | solution.py:332
  76.2 20.0 %near_product.1.refs_4_ = f32[1024,2048]{1,0:T(8,128)} custom-call(s32[2]{0:T(128)} %pad_add_fusion.1.ids_ref, bf16[1024,1536]{1,0:T(8,128)(2,1)} %refs_0_.3, bf16[1024,1536]{1,0:T(8,128)(2,1)} %collective-permute-done.2.refs_1_, bf16[2048,6144]{1,0:T(8,128)(2,1)} %refs_3_.9, bf16[2048,6144]{1,0:T(8,128)(2,1)} %refs_3_.9), custom_call_target="tpu_custom_call" | custom-call | flops 12884901888 | bytes 27262976 | tf_op jit(solution)/shard_map/near_product/pallas_call | solution.py:95
  96.2 1.2 broadcast_in_dim.7.before_ref
  97.5 11.2 %far_product.4 = (bf16[256,2048]{1,0:T(8,128)(2,1)}, f32[16,128,128]{2,1,0:T(8,128)}, f32[16,128,128]{2,1,0:T(8,128)}) custom-call(s32[2]{0:T(128)} %pad_add_fusion.ids_ref, f32[16,128,128]{2,1,0:T(8,128)} %broadcast_in_dim.7.before_ref, bf16[256,1536]{1,0:T(8,128)(2,1)} %collective-permute-done.refs_0_, bf16[256,1536]{1,0:T(8,128)(2,1)} %copy-done.7, ...), custom_call_target="tpu_custom_call" | custom-call | flops 3355443200 | bytes 21495808 | tf_op jit(solution)/shard_map/far_product/pallas_call | solution.py:139
  108.7 0.9 copy-done.5
  109.6 11.2 %far_product.5 = (bf16[256,2048]{1,0:T(8,128)(2,1)}, f32[16,128,128]{2,1,0:T(8,128)}, f32[16,128,128]{2,1,0:T(8,128)}) custom-call(s32[2]{0:T(128)} %pad_add_fusion.ids_ref, f32[16,128,128]{2,1,0:T(8,128)} %get-tuple-element.23.before_ref, bf16[256,1536]{1,0:T(8,128)(2,1)} %copy-done.3, bf16[256,1536]{1,0:T(8,128)(2,1)} %copy-done.5, ...), custom_call_target="tpu_custom_call" | custom-call | flops 3355443200 | bytes 21495808 | tf_op jit(solution)/shard_map/far_product/pallas_call | solution.py:139
  120.9 0.9 copy-done.6
  121.7 11.3 %far_product.6 = (bf16[256,2048]{1,0:T(8,128)(2,1)}, f32[16,128,128]{2,1,0:T(8,128)}, f32[16,128,128]{2,1,0:T(8,128)}) custom-call(s32[2]{0:T(128)} %pad_add_fusion.ids_ref, f32[16,128,128]{2,1,0:T(8,128)} %get-tuple-element.25.before_ref, bf16[256,1536]{1,0:T(8,128)(2,1)} %copy-done.2, bf16[256,1536]{1,0:T(8,128)(2,1)} %copy-done.6, ...), custom_call_target="tpu_custom_call" | custom-call | flops 3355443200 | bytes 21495808 | tf_op jit(solution)/shard_map/far_product/pallas_call | solution.py:139
  133.0 0.9 copy-done.4
  133.9 11.2 %far_product.7 = (bf16[256,2048]{1,0:T(8,128)(2,1)}, f32[16,128,128]{2,1,0:T(8,128)}, bf16[16,128,128]{2,1,0:T(8,128)(2,1)}) custom-call(s32[2]{0:T(128)} %pad_add_fusion.ids_ref, f32[16,128,128]{2,1,0:T(8,128)} %get-tuple-element.27.before_ref, bf16[256,1536]{1,0:T(8,128)(2,1)} %copy-done.1, bf16[256,1536]{1,0:T(8,128)(2,1)} %copy-done.4, ...), custom_call_target="tpu_custom_call" | custom-call | flops 3355443200 | bytes 21495808 | tf_op jit(solution)/shard_map/far_product/pallas_call | solution.py:139
  145.1 6.0 %all-to-all-start.2 = ((bf16[8,256,128]{2,1,0:T(8,128)(2,1)}), bf16[8,256,128]{2,1,0:T(8,128)(2,1)S(1)}, u32[]{:S(2)}, u32[]{:S(2)}) async-start(bf16[8,256,128]{2,1,0:T(8,128)(2,1)} %bitcast.176), calls=%async_computation.2 | async-start | bytes 1048576 | tf_op jit(solution)/shard_map/all_to_all | solution.py:301
  152.7 22.7 %all-reduce = f32[128]{0:T(128)S(1)} all-reduce(f32[128]{0:T(128)S(1)} %dynamic-update-slice), channel_id=2, replica_groups=mesh['seq'=8,'tp'=4] {'seq'}, use_global_device_ids=true, to_apply=%add | all-reduce | flops 128 | bytes 1024
  177.0 0.8 fusion.17
  177.8 1.0 fusion.21
  178.8 0.8 fusion.12
  179.6 0.9 convert_dynamic-update-slice_fusion.2
  180.5 0.8 fusion.13
  181.3 0.8 convert_dynamic-update-slice_fusion
  182.2 3.5 %all-to-all-start.1 = ((bf16[8,256,128]{2,1,0:T(8,128)(2,1)}), bf16[8,256,128]{2,1,0:T(8,128)(2,1)S(1)}, u32[]{:S(2)}, u32[]{:S(2)}) async-start(bf16[8,256,128]{2,1,0:T(8,128)(2,1)} %bitcast.24), calls=%async_computation.1 | async-start | bytes 1048576 | tf_op jit(solution)/shard_map/all_to_all | solution.py:309
  187.7 9.7 %all-to-all-done.1 = bf16[8,256,128]{2,1,0:T(8,128)(2,1)S(1)} async-done(((bf16[8,256,128]{2,1,0:T(8,128)(2,1)}), bf16[8,256,128]{2,1,0:T(8,128)(2,1)S(1)}, u32[]{:S(2)}, u32[]{:S(2)}) %all-to-all-start.1) | async-done | bytes 524320 | tf_op jit(solution)/shard_map/all_to_all | solution.py:309
  197.4 3.7 %all-to-all-start.3 = ((bf16[8,256,128]{2,1,0:T(8,128)(2,1)}), bf16[8,256,128]{2,1,0:T(8,128)(2,1)S(1)}, u32[]{:S(2)}, u32[]{:S(2)}) async-start(bf16[8,256,128]{2,1,0:T(8,128)(2,1)} %bitcast.35), calls=%async_computation.3 | async-start | bytes 1048576 | tf_op jit(solution)/shard_map/all_to_all | solution.py:309
  201.1 29.7 %block_terms.1 = (bf16[1024,2048]{1,0:T(8,128)(2,1)}, bf16[1024,2048]{1,0:T(8,128)(2,1)}, bf16[1024,2048]{1,0:T(8,128)(2,1)}) custom-call(bf16[1024,2048]{1,0:T(8,128)(2,1)} %refs_0_.4, bf16[1024,2048]{1,0:T(8,128)(2,1)} %refs_0_.5, bf16[1024,2048]{1,0:T(8,128)(2,1)} %refs_1_.3, bf16[256,2048]{1,0:T(8,128)(2,1)} %get-tuple-element.22.refs_3_, ...), custom_call_target="tpu_custom_call" | custom-call | flops 5905580032 | bytes 33554432 | tf_op jit(solution)/shard_map/block_terms/pallas_call | solution.py:215
  230.8 0.8 copy-done
  231.5 18.8 %later_terms.1 = (bf16[1024,2048]{1,0:T(8,128)(2,1)}, bf16[1024,2048]{1,0:T(8,128)(2,1)}) custom-call(bf16[1024,2048]{1,0:T(8,128)(2,1)} %refs_0_.5, bf16[1024,2048]{1,0:T(8,128)(2,1)} %refs_1_.3, bf16[1024,2048]{1,0:T(8,128)(2,1)} %get-tuple-element.32.refs_2_, ...), custom_call_target="tpu_custom_call", output_to_operand_aliasing={{0}: (2, {}), {1}: (3, {})} | custom-call | flops 1073741824 | bytes 29360128 | tf_op jit(solution)/shard_map/later_terms/pallas_call | solution.py:278
  (62 shorter events, 8.5 us)
Async XLA Ops:
  0.6 8.7 %copy-start.9 = (f32[16,1024]{1,0:T(8,128)S(1)}, f32[16,1024]{1,0:T(8,128)}, u32[]{:S(2)}) copy-start(f32[16,1024]{1,0:T(8,128)} %param.9) | copy-start | bytes 196612
  0.6 75.6 %collective-permute-start.2 = (bf16[1024,1536]{1,0:T(8,128)(2,1)}, bf16[1024,1536]{1,0:T(8,128)(2,1)}, u32[]{:S(2)}, u32[]{:S(2)}) collective-permute-start(bf16[1024,1536]{1,0:T(8,128)(2,1)} %refs_0_.3), channel_id=1, source_target_pairs={{0,1},{1,0},{2,3},{3,2},{4,5},{5,4},{6,7},{7,6},{8,9},{9,8},{10,11... | collective-permute-start | bytes 9437192 | tf_op jit(solution)/shard_map/ppermute | solution.py:335
  4.7 32.6 %collective-permute-start.7 = (bf16[256,1536]{1,0:T(8,128)(2,1)}, bf16[256,1536]{1,0:T(8,128)(2,1)S(1)}, u32[]{:S(2)}, u32[]{:S(2)}) collective-permute-start(bf16[256,1536]{1,0:T(8,128)(2,1)} %get-tuple-element.47), channel_id=1, source_target_pairs={{0,2},{1,3},{2,0},{3,1},{4,6},{5,7},{6,4},{7,5},{8,10},{9,11},{10,... | collective-permute-start | bytes 2359304 | tf_op jit(solution)/shard_map/ppermute | solution.py:332
  7.3 35.5 %collective-permute-start.3 = (bf16[256,1536]{1,0:T(8,128)(2,1)}, bf16[256,1536]{1,0:T(8,128)(2,1)S(1)}, u32[]{:S(2)}, u32[]{:S(2)}) collective-permute-start(bf16[256,1536]{1,0:T(8,128)(2,1)} %get-tuple-element.48), channel_id=1, source_target_pairs={{0,2},{1,3},{2,0},{3,1},{4,6},{5,7},{6,4},{7,5},{8,10},{9,11},{10,... | collective-permute-start | bytes 2359304 | tf_op jit(solution)/shard_map/ppermute | solution.py:332
  7.3 52.4 %collective-permute-start = (bf16[256,1536]{1,0:T(8,128)(2,1)}, bf16[256,1536]{1,0:T(8,128)(2,1)}, u32[]{:S(2)}, u32[]{:S(2)}) collective-permute-start(bf16[256,1536]{1,0:T(8,128)(2,1)} %get-tuple-element.49), channel_id=1, source_target_pairs={{0,2},{1,3},{2,0},{3,1},{4,6},{5,7},{6,4},{7,5},{8,10},{9,11},{10,... | collective-permute-start | bytes 2359304 | tf_op jit(solution)/shard_map/ppermute | solution.py:332
  9.3 66.9 %collective-permute-start.5 = (bf16[256,1536]{1,0:T(8,128)(2,1)}, bf16[256,1536]{1,0:T(8,128)(2,1)S(1)}, u32[]{:S(2)}, u32[]{:S(2)}) collective-permute-start(bf16[256,1536]{1,0:T(8,128)(2,1)} %get-tuple-element.50), channel_id=1, source_target_pairs={{0,2},{1,3},{2,0},{3,1},{4,6},{5,7},{6,4},{7,5},{8,10},{9,11},{10,... | collective-permute-start | bytes 2359304 | tf_op jit(solution)/shard_map/ppermute | solution.py:332
  29.0 116.1 %all-to-all-start = ((bf16[8,256,128]{2,1,0:T(8,128)(2,1)}), bf16[8,256,128]{2,1,0:T(8,128)(2,1)S(1)}, u32[]{:S(2)}, u32[]{:S(2)}) async-start(bf16[8,256,128]{2,1,0:T(8,128)(2,1)} %bitcast.175), calls=%async_computation | async-start | bytes 1048576 | tf_op jit(solution)/shard_map/all_to_all | solution.py:301
  37.4 58.8 %copy-start.1 = (bf16[256,1536]{1,0:T(8,128)(2,1)}, bf16[256,1536]{1,0:T(8,128)(2,1)S(1)}, u32[]{:S(2)}) copy-start(bf16[256,1536]{1,0:T(8,128)(2,1)S(1)} %collective-permute-done.7.refs_0_) | copy-start | bytes 2359300
  37.4 95.6 %collective-permute-start.8 = (bf16[256,1536]{1,0:T(8,128)(2,1)S(1)}, bf16[256,1536]{1,0:T(8,128)(2,1)S(1)}, u32[]{:S(2)}, u32[]{:S(2)}) collective-permute-start(bf16[256,1536]{1,0:T(8,128)(2,1)S(1)} %collective-permute-done.7.refs_0_), channel_id=1, source_target_pairs={{0,1},{1,0},{2,3},{3,2},{4,5},{5,4},{6,7},{7,6},{8,9},{9,8},{10,11... | collective-permute-start | bytes 2359304 | tf_op jit(solution)/shard_map/ppermute | solution.py:333
  42.7 53.5 %copy-start.3 = (bf16[256,1536]{1,0:T(8,128)(2,1)}, bf16[256,1536]{1,0:T(8,128)(2,1)S(1)}, u32[]{:S(2)}) copy-start(bf16[256,1536]{1,0:T(8,128)(2,1)S(1)} %collective-permute-done.3.refs_0_) | copy-start | bytes 2359300
  42.7 66.0 %collective-permute-start.4 = (bf16[256,1536]{1,0:T(8,128)(2,1)S(1)}, bf16[256,1536]{1,0:T(8,128)(2,1)S(1)}, u32[]{:S(2)}, u32[]{:S(2)}) collective-permute-start(bf16[256,1536]{1,0:T(8,128)(2,1)S(1)} %collective-permute-done.3.refs_0_), channel_id=1, source_target_pairs={{0,1},{1,0},{2,3},{3,2},{4,5},{5,4},{6,7},{7,6},{8,9},{9,8},{10,11... | collective-permute-start | bytes 2359304 | tf_op jit(solution)/shard_map/ppermute | solution.py:333
  59.7 36.5 %collective-permute-start.1 = (bf16[256,1536]{1,0:T(8,128)(2,1)}, bf16[256,1536]{1,0:T(8,128)(2,1)S(1)}, u32[]{:S(2)}, u32[]{:S(2)}) collective-permute-start(bf16[256,1536]{1,0:T(8,128)(2,1)} %collective-permute-done.refs_0_), channel_id=1, source_target_pairs={{0,1},{1,0},{2,3},{3,2},{4,5},{5,4},{6,7},{7,6},{8,9},{9,8},{10,11... | collective-permute-start | bytes 2359304 | tf_op jit(solution)/shard_map/ppermute | solution.py:333
  76.2 20.0 %copy-start.2 = (bf16[256,1536]{1,0:T(8,128)(2,1)}, bf16[256,1536]{1,0:T(8,128)(2,1)S(1)}, u32[]{:S(2)}) copy-start(bf16[256,1536]{1,0:T(8,128)(2,1)S(1)} %collective-permute-done.5.refs_0_) | copy-start | bytes 2359300
  76.2 44.6 %collective-permute-start.6 = (bf16[256,1536]{1,0:T(8,128)(2,1)S(1)}, bf16[256,1536]{1,0:T(8,128)(2,1)S(1)}, u32[]{:S(2)}, u32[]{:S(2)}) collective-permute-start(bf16[256,1536]{1,0:T(8,128)(2,1)S(1)} %collective-permute-done.5.refs_0_), channel_id=1, source_target_pairs={{0,1},{1,0},{2,3},{3,2},{4,5},{5,4},{6,7},{7,6},{8,9},{9,8},{10,11... | collective-permute-start | bytes 2359304 | tf_op jit(solution)/shard_map/ppermute | solution.py:333
  96.2 1.2 copy-start.7
  108.7 0.9 copy-start.5
  120.8 0.9 copy-start.6
  133.0 0.9 copy-start.4
  133.9 17.3 %copy-start.10 = (u32[32]{0:T(128)S(1)}, u32[32]{0:T(128)}, u32[]{:S(2)}) copy-start(u32[32]{0:T(128)} %constant.42) | copy-start | bytes 388
  145.1 32.7 %all-to-all-start.2 = ((bf16[8,256,128]{2,1,0:T(8,128)(2,1)}), bf16[8,256,128]{2,1,0:T(8,128)(2,1)S(1)}, u32[]{:S(2)}, u32[]{:S(2)}) async-start(bf16[8,256,128]{2,1,0:T(8,128)(2,1)} %bitcast.176), calls=%async_computation.2 | async-start | bytes 1048576 | tf_op jit(solution)/shard_map/all_to_all | solution.py:301
  182.2 15.3 %all-to-all-start.1 = ((bf16[8,256,128]{2,1,0:T(8,128)(2,1)}), bf16[8,256,128]{2,1,0:T(8,128)(2,1)S(1)}, u32[]{:S(2)}, u32[]{:S(2)}) async-start(bf16[8,256,128]{2,1,0:T(8,128)(2,1)} %bitcast.24), calls=%async_computation.1 | async-start | bytes 1048576 | tf_op jit(solution)/shard_map/all_to_all | solution.py:309
  197.4 3.7 %copy-start.8 = (bf16[8,256,128]{2,1,0:T(8,128)(2,1)}, bf16[8,256,128]{2,1,0:T(8,128)(2,1)S(1)}, u32[]{:S(2)}) copy-start(bf16[8,256,128]{2,1,0:T(8,128)(2,1)S(1)} %all-to-all-done.1) | copy-start | bytes 1572868
  197.4 33.3 %all-to-all-start.3 = ((bf16[8,256,128]{2,1,0:T(8,128)(2,1)}), bf16[8,256,128]{2,1,0:T(8,128)(2,1)S(1)}, u32[]{:S(2)}, u32[]{:S(2)}) async-start(bf16[8,256,128]{2,1,0:T(8,128)(2,1)} %bitcast.35), calls=%async_computation.3 | async-start | bytes 1048576 | tf_op jit(solution)/shard_map/all_to_all | solution.py:309
  230.7 0.8 copy-start

commit v2 on v0

v2 whole, which is shorter than its diff:
```python
import functools

import jax
import jax.numpy as jnp
from jax import lax
from jax.experimental import pallas as pl
from jax.experimental.pallas import tpu as pltpu
from jax.sharding import PartitionSpec as P

HD = 128
BLK = 256
GROUP = 4
ROW = 16
MIB = 2**20

NN = (((1,), (0,)), ((), ()))
NT = (((1,), (1,)), ((), ()))
TN = (((0,), (0,)), ((), ()))

ANY = pl.BlockSpec(memory_space=pl.ANY)
VMEM = pl.BlockSpec(memory_space=pltpu.VMEM)
SMEM = pl.BlockSpec(memory_space=pltpu.SMEM)
BF16 = jnp.bfloat16
F32 = jnp.float32


def mm(left, right, form):
    return lax.dot_general(left, right, form, preferred_element_type=F32)


def cost(flops, nbytes, exps=0):
    return pl.CostEstimate(flops=int(flops), bytes_accessed=int(nbytes), transcendentals=int(exps))


def span(index, size):
    return slice(index * size, (index + 1) * size)


def call(body, name, ins, outs, scratch, limit, estimate, aliases=None):
    return pl.pallas_call(
        body,
        in_specs=[spec for _, spec in ins],
        out_specs=[spec for _, _, spec in outs],
        out_shape=[jax.ShapeDtypeStruct(shape, dtype) for shape, dtype, _ in outs],
        scratch_shapes=scratch,
        input_output_aliases=aliases or {},
        compiler_params=pltpu.CompilerParams(vmem_limit_bytes=limit * MIB),
        cost_estimate=estimate,
        name=name,
    )(*[array for array, _ in ins])


def copy_of(source, target, sem):
    return pltpu.make_async_copy(source, target, sem)


def lanes_of(index, size):
    return pl.ds(pl.multiple_of(index * size, size), size)


def loop(count, body):
    lax.fori_loop(0, count, lambda i, _: (body(i), 0)[1], 0)


def head_in(h):
    return slice(h * HD, (h + 1) * HD)


def key_body(k_hbm, v_hbm, cum_ref, local_hbm, total_ref, k_ref, v_ref, local_ref, load_sems, store_sems):
    blk_count, groups, group, _ = cum_ref.shape
    wide = group * HD

    def loads(j):
        rows = pl.ds(j * BLK, BLK)
        return (
            copy_of(k_hbm.at[rows], k_ref.at[rows], load_sems.at[0, j]),
            copy_of(v_hbm.at[rows], v_ref.at[rows], load_sems.at[1, j]),
        )

    def store(j):
        return copy_of(local_ref.at[j], local_hbm.at[j], store_sems.at[j])

    for j in range(blk_count):
        for copy in loads(j):
            copy.start()
    local_ref[0] = jnp.zeros_like(local_ref[0])

    def block(j):
        for copy in loads(j):
            copy.wait()
        store(j).start()
        rows = pl.ds(pl.multiple_of(j * BLK, BLK), BLK)

        def some_heads(g):
            cum = cum_ref[j, g].T
            end = cum[BLK - 1 : BLK, :]
            weight = jnp.exp(end - cum)
            end_weight = jnp.exp(end)
            lanes = lanes_of(g, wide)
            these = pl.ds(g * group, group)
            keys, values, entered = k_ref[rows, lanes], v_ref[rows, lanes], local_ref[j, these]
            left = []
            for h in range(group):
                scaled = (keys[:, head_in(h)].astype(F32) * weight[:, h : h + 1]).astype(BF16)
                sums = mm(scaled, values[:, head_in(h)], TN)
                left.append(entered[h] * end_weight[:, h : h + 1] + sums)
            local_ref[j + 1, these] = jnp.stack(left)

        loop(groups, some_heads)

    loop(blk_count, block)
    total_ref[...] = local_ref[blk_count].astype(BF16)
    for j in range(blk_count):
        store(j).wait()


def key_totals(keys, values, cum):
    rows, width = keys.shape
    blk_count, heads = cum.shape[0], width // HD
    return call(
        key_body,
        "key_totals",
        [(keys, ANY), (values, ANY), (cum, VMEM)],
        [((blk_count, heads, HD, HD), F32, ANY), ((heads, HD, HD), BF16, VMEM)],
        [
            pltpu.VMEM((rows, width), BF16),
            pltpu.VMEM((rows, width), BF16),
            pltpu.VMEM((blk_count + 1, heads, HD, HD), F32),
            pltpu.SemaphoreType.DMA((2, blk_count)),
            pltpu.SemaphoreType.DMA((blk_count,)),
        ],
        24,
        cost(2 * rows * width * HD, 4 * rows * width + 4 * blk_count * width * HD),
    )


def near_body(wide, own_hbm, sibling_hbm, w_hbm, out_hbm, grad_ref, w_ref, out_ref, w_sems, grad_sems, out_sems):
    rows, depth = own_hbm.shape
    groups, tiles = w_hbm.shape[0] // wide, rows // BLK
    me = lax.axis_index("tp")
    side = lax.rem(me, 2)
    columns = pl.ds(pl.multiple_of((me - side) * depth, 2 * depth), 2 * depth)

    def w_load(g):
        part = pl.ds(g * wide, wide)
        return copy_of(w_hbm.at[part, columns], w_ref.at[part], w_sems.at[g])

    def grad_loads(r):
        part = pl.ds(r * BLK, BLK)
        return (
            copy_of(own_hbm.at[part], grad_ref.at[part, lanes_of(side, depth)], grad_sems.at[0, r]),
            copy_of(sibling_hbm.at[part], grad_ref.at[part, lanes_of(1 - side, depth)], grad_sems.at[1, r]),
        )

    def store(g):
        return copy_of(out_ref.at[lax.rem(g, 2)], out_hbm.at[:, lanes_of(g, wide)], out_sems.at[lax.rem(g, 2)])

    w_load(0).start()
    for r in range(tiles):
        for copy in grad_loads(r):
            copy.start()
    for g in range(1, groups):
        w_load(g).start()

    def columns_of(g):
        w_load(g).wait()

        @pl.when(g >= 2)
        def _():
            store(g - 2).wait()

        part = w_ref[pl.ds(pl.multiple_of(g * wide, wide), wide)]
        out_ref[lax.rem(g, 2)] = mm(grad_ref[...], part, NT)
        store(g).start()

    for r in range(tiles):
        for copy in grad_loads(r):
            copy.wait()
    loop(groups, columns_of)
    for g in range(max(groups - 2, 0), groups):
        store(g).wait()


def near_product(own, sibling, weight):
    rows, depth = own.shape
    width = weight.shape[0]
    wide = GROUP * HD
    (out,) = call(
        functools.partial(near_body, wide),
        "near_product",
        [(own, ANY), (sibling, ANY), (weight, ANY)],
        [((rows, width), F32, ANY)],
        [
            pltpu.VMEM((rows, 2 * depth), BF16),
            pltpu.VMEM((width, 2 * depth), BF16),
            pltpu.VMEM((2, rows, wide), F32),
            pltpu.SemaphoreType.DMA((width // wide,)),
            pltpu.SemaphoreType.DMA((2, rows // BLK)),
            pltpu.SemaphoreType.DMA((2,)),
        ],
        32,
        cost(4 * rows * width * depth, 4 * depth * (rows + width) + 4 * rows * width),
    )
    return out


def far_body(blk, chips, before_hbm, near_hbm, q_hbm, cum_ref, prior_ref, w_hbm, *refs):
    pieces = refs[: 2 * (chips - 1)]
    grad_hbm, sums_hbm, total_hbm, piece_ref, w_ref, near_ref, q_ref, before_ref = refs[2 * (chips - 1) :][:8]
    grad_ref, sums_ref, total_ref, piece_sems, load_sems, store_sems = refs[2 * (chips - 1) + 8 :]
    rows, depth = pieces[0].shape
    _, groups, group, _ = cum_ref.shape
    wide = group * HD
    me = lax.axis_index("tp")
    side = lax.rem(me, 2)
    chip = lax.div(me, 2)
    block = pl.ds(blk * BLK, BLK)

    def piece_load(n):
        at = 2 * (n // 2) + (side if n % 2 == 0 else 1 - side)
        return copy_of(pieces[n], piece_ref.at[:, lanes_of(at, depth)], piece_sems.at[n])

    def loads(g):
        part, lanes = pl.ds(g * wide, wide), lanes_of(g, wide)
        these = pl.ds(g * group, group)
        found = []
        for d in range(1, chips):
            owner = lax.rem(chip + chips - d, chips)
            held = pl.ds((d - 1) * 2 * depth, 2 * depth)
            found.append(
                copy_of(w_hbm.at[part, lanes_of(owner, 2 * depth)], w_ref.at[part, held], load_sems.at[d + 2, g])
            )
        found.append(copy_of(near_hbm.at[block, lanes], near_ref.at[:, lanes], load_sems.at[0, g]))
        found.append(copy_of(q_hbm.at[block, lanes], q_ref.at[:, lanes], load_sems.at[1, g]))
        if blk:
            found.append(copy_of(before_hbm.at[these], before_ref.at[these], load_sems.at[2, g]))
        return found

    def stores(g):
        these, lanes = pl.ds(g * group, group), lanes_of(g, wide)
        return (
            copy_of(total_ref.at[these], total_hbm.at[these], store_sems.at[0, g]),
            copy_of(grad_ref.at[:, lanes], grad_hbm.at[:, lanes], store_sems.at[1, g]),
            copy_of(sums_ref.at[these], sums_hbm.at[these], store_sems.at[2, g]),
        )

    for n in range(len(pieces)):
        piece_load(n).start()
    for g in range(groups):
        for copy in loads(g):
            copy.start()
    for n in range(len(pieces)):
        piece_load(n).wait()

    def some_heads(g):
        for copy in loads(g):
            copy.wait()
        lanes = lanes_of(g, wide)
        part = pl.ds(pl.multiple_of(g * wide, wide), wide)
        weight = jnp.exp(cum_ref[blk, g].T)
        queries = q_ref[:, lanes]
        grad = (near_ref[:, lanes] + mm(piece_ref[...], w_ref[part], NT)).astype(BF16)
        these = pl.ds(g * group, group)
        before = before_ref[these] if blk else None
        sums, total = [], []
        for h in range(group):
            scaled = (queries[:, head_in(h)].astype(F32) * weight[:, h : h + 1]).astype(BF16)
            sums.append(mm(scaled, grad[:, head_in(h)], TN))
            total.append(before[h] + prior_ref[g * group + h, blk] * sums[h] if blk else sums[h])
        grad_ref[:, lanes] = grad
        sums_ref[these] = jnp.stack(sums)
        total_ref[these] = jnp.stack(total).astype(total_ref.dtype)
        for copy in stores(g):
            copy.start()

    loop(groups, some_heads)
    for g in range(groups):
        for copy in stores(g):
            copy.wait()


def far_product(blk, last, before, pieces, weight, near, queries, cum, prior):
    rows, depth = pieces[0].shape
    _, groups, group, _ = cum.shape
    heads = groups * group
    width = heads * HD
    chips = len(pieces) // 2 + 1
    total_type = BF16 if last else F32
    states = (heads, HD, HD)
    return call(
        functools.partial(far_body, blk, chips),
        "far_product",
        [(before, ANY), (near, ANY), (queries, ANY), (cum, VMEM), (prior, SMEM), (weight, ANY)]
        + [(piece, ANY) for piece in pieces],
        [((rows, width), BF16, ANY), (states, F32, ANY), (states, total_type, ANY)],
        [
            pltpu.VMEM((rows, 2 * (chips - 1) * depth), BF16),
            pltpu.VMEM((width, 2 * (chips - 1) * depth), BF16),
            pltpu.VMEM((rows, width), F32),
            pltpu.VMEM((rows, width), BF16),
            pltpu.VMEM(states, F32),
            pltpu.VMEM((rows, width), BF16),
            pltpu.VMEM(states, F32),
            pltpu.VMEM(states, total_type),
            pltpu.SemaphoreType.DMA((2 * (chips - 1),)),
            pltpu.SemaphoreType.DMA((chips + 2, groups)),
            pltpu.SemaphoreType.DMA((3, groups)),
        ],
        28,
        cost(
            2 * rows * width * (2 * (chips - 1) * depth + HD),
            4 * (chips - 1) * depth * (rows + width) + 8 * rows * width + 12 * width * HD,
        ),
    )


def block_body(blk, q_hbm, k_hbm, v_hbm, grad_hbm, cum_ref, prior_ref, local_hbm, enter_hbm, *refs):
    refs = refs[1:] if blk else refs
    gq_hbm, gk_hbm, gv_hbm, q_ref, k_ref, v_ref, grad_ref, local_ref, enter_ref = refs[:9]
    gq_ref, gk_ref, gv_ref, load_sems, store_sems = refs[9:]
    _, groups, group, _ = cum_ref.shape
    wide = group * HD
    block = pl.ds(blk * BLK, BLK)

    def loads(g):
        lanes, these = lanes_of(g, wide), pl.ds(g * group, group)
        return (
            copy_of(grad_hbm.at[:, lanes], grad_ref.at[:, lanes], load_sems.at[0, g]),
            copy_of(v_hbm.at[block, lanes], v_ref.at[:, lanes], load_sems.at[1, g]),
            copy_of(q_hbm.at[block, lanes], q_ref.at[:, lanes], load_sems.at[2, g]),
            copy_of(k_hbm.at[block, lanes], k_ref.at[:, lanes], load_sems.at[3, g]),
            copy_of(local_hbm.at[blk, these], local_ref.at[these], load_sems.at[4, g]),
            copy_of(enter_hbm.at[these], enter_ref.at[these], load_sems.at[5, g]),
        )

    def stores(g):
        lanes = lanes_of(g, wide)
        return (
            copy_of(gq_ref.at[:, lanes], gq_hbm.at[block, lanes], store_sems.at[0, g]),
            copy_of(gk_ref.at[:, lanes], gk_hbm.at[:, lanes], store_sems.at[1, g]),
            copy_of(gv_ref.at[:, lanes], gv_hbm.at[:, lanes], store_sems.at[2, g]),
        )

    for g in range(groups):
        for copy in loads(g):
            copy.start()
    at_row = lax.broadcasted_iota(jnp.int32, (BLK, BLK), 0)
    at_col = lax.broadcasted_iota(jnp.int32, (BLK, BLK), 1)
    causal, flipped = at_row >= at_col, at_row <= at_col

    def some_heads(g):
        for copy in loads(g):
            copy.wait()
        rows = cum_ref[blk, g]
        cum = rows.T
        head_weight = jnp.exp(cum)
        lanes, these = lanes_of(g, wide), pl.ds(g * group, group)
        queries, keys, values, grads = q_ref[:, lanes], k_ref[:, lanes], v_ref[:, lanes], grad_ref[:, lanes]
        entered, here = enter_ref[these], local_ref[these]
        gq, gk, gv = [], [], []
        for h in range(group):
            head = head_in(h)
            q, k, v, grad = queries[:, head], keys[:, head], values[:, head], grads[:, head]
            by_row, by_col = cum[:, h : h + 1], rows[h : h + 1, :]
            mask = jnp.exp(jnp.where(causal, by_row - by_col, -1e30))
            turned = jnp.exp(jnp.where(flipped, by_col - by_row, -1e30))
            scores = (mm(grad, v, NT) * mask).astype(BF16)
            turned_scores = (mm(v, grad, NT) * turned).astype(BF16)
            turned_attn = (mm(k, q, NT) * turned).astype(BF16)
            enter = entered[h].astype(F32) * prior_ref[g * group + h, blk] + here[h]
            inter = mm(grad, enter.astype(BF16), NT) * head_weight[:, h : h + 1]
            gq.append((mm(scores, k, NN) + inter).astype(BF16))
            gk.append(mm(turned_scores, q, NN).astype(BF16))
            gv.append(mm(turned_attn, grad, NN).astype(BF16))
        gq_ref[:, lanes] = jnp.concatenate(gq, axis=1)
        gk_ref[:, lanes] = jnp.concatenate(gk, axis=1)
        gv_ref[:, lanes] = jnp.concatenate(gv, axis=1)
        for copy in stores(g):
            copy.start()

    loop(groups, some_heads)
    for g in range(groups):
        for copy in stores(g):
            copy.wait()


def block_terms(blk, queries, keys, values, grad, cum, prior, local_enter, enter, gq):
    rows, width = queries.shape
    heads, groups = width // HD, cum.shape[1]
    tile = pltpu.VMEM((BLK, width), BF16)
    part = ((BLK, width), BF16, ANY)
    ins = [queries, keys, values, grad, cum, prior, local_enter, enter]
    specs = [ANY, ANY, ANY, ANY, VMEM, SMEM, ANY, ANY]
    if blk:
        ins, specs = ins + [gq], specs + [ANY]
    return call(
        functools.partial(block_body, blk),
        "block_terms",
        list(zip(ins, specs)),
        [((rows, width), BF16, ANY), part, part],
        [tile] * 4
        + [pltpu.VMEM((heads, HD, HD), F32), pltpu.VMEM((heads, HD, HD), BF16)]
        + [tile] * 3
        + [pltpu.SemaphoreType.DMA((6, groups)), pltpu.SemaphoreType.DMA((3, groups))],
        20,
        cost(BLK * width * (10 * BLK + 2 * HD), 14 * BLK * width + 6 * width * HD, BLK * heads * BLK),
        {8: 0} if blk else None,
    )


def later_body(k_hbm, v_hbm, cum_ref, enter_hbm, *refs):
    blk_count, groups, group, _ = cum_ref.shape
    gk_parts, gv_parts = refs[:blk_count], refs[blk_count : 2 * blk_count]
    sums_hbm = refs[2 * blk_count : 3 * blk_count - 1]
    gk_hbm, gv_hbm, k_ref, v_ref, gk_ref, gv_ref, sums_ref, enter_ref, carry_ref = refs[3 * blk_count - 1 : -2]
    load_sems, store_sems = refs[-2:]
    wide = group * HD

    def rows_of(j):
        return pl.ds(pl.multiple_of(j * BLK, BLK), BLK)

    def sums_load(j, at):
        return copy_of(sums_hbm[at - 1], sums_ref.at[j], load_sems.at[4, j])

    def loads(j, at):
        rows = rows_of(j)
        return [
            copy_of(v_hbm.at[rows], v_ref.at[rows], load_sems.at[0, j]),
            copy_of(k_hbm.at[rows], k_ref.at[rows], load_sems.at[1, j]),
            copy_of(gk_parts[at], gk_ref.at[rows], load_sems.at[2, j]),
            copy_of(gv_parts[at], gv_ref.at[rows], load_sems.at[3, j]),
        ]

    def stores(j):
        rows = rows_of(j)
        return (
            copy_of(gk_ref.at[rows], gk_hbm.at[rows], store_sems.at[0, j]),
            copy_of(gv_ref.at[rows], gv_hbm.at[rows], store_sems.at[1, j]),
        )

    enter_load = copy_of(enter_hbm, enter_ref, load_sems.at[0, blk_count])
    enter_load.start()
    for j in reversed(range(blk_count)):
        for copy in loads(j, j):
            copy.start()
        if j:
            sums_load(j, j).start()
    sums_ref[0] = jnp.zeros_like(sums_ref[0])
    enter_load.wait()
    carry_ref[...] = enter_ref[...].astype(F32)

    def block(back):
        j = blk_count - 1 - back
        rows = rows_of(j)
        for copy in loads(j, 0):
            copy.wait()

        @pl.when(j > 0)
        def _():
            sums_load(j, 1).wait()

        def some_heads(g):
            cum = cum_ref[j, g].T
            end = cum[BLK - 1 : BLK, :]
            weight = jnp.exp(end - cum)
            end_weight = jnp.exp(end)
            lanes, these = lanes_of(g, wide), pl.ds(g * group, group)
            keys, values = k_ref[rows, lanes], v_ref[rows, lanes]
            gk_in, gv_in = gk_ref[rows, lanes], gv_ref[rows, lanes]
            entered, here = carry_ref[these], sums_ref[j, these]
            gk, gv, left = [], [], []
            for h in range(group):
                head, tail = head_in(h), weight[:, h : h + 1]
                enter = entered[h].astype(BF16)
                gk.append((gk_in[:, head].astype(F32) + mm(values[:, head], enter, NT) * tail).astype(BF16))
                gv.append((gv_in[:, head].astype(F32) + mm(keys[:, head], enter, NN) * tail).astype(BF16))
                left.append(entered[h] * end_weight[:, h : h + 1] + here[h])
            gk_ref[rows, lanes] = jnp.concatenate(gk, axis=1)
            gv_ref[rows, lanes] = jnp.concatenate(gv, axis=1)
            carry_ref[these] = jnp.stack(left)

        loop(groups, some_heads)
        for copy in stores(j):
            copy.start()

    loop(blk_count, block)
    for j in range(blk_count):
        for copy in stores(j):
            copy.wait()


def later_terms(keys, values, gk_parts, gv_parts, sums, cum, enter):
    rows, width = keys.shape
    heads, blk_count = width // HD, rows // BLK
    whole = pltpu.VMEM((rows, width), BF16)
    out = ((rows, width), BF16, ANY)
    return call(
        later_body,
        "later_terms",
        [(keys, ANY), (values, ANY), (cum, VMEM), (enter, ANY)]
        + [(x, ANY) for x in gk_parts + gv_parts + sums],
        [out, out],
        [whole] * 4
        + [
            pltpu.VMEM((blk_count, heads, HD, HD), F32),
            pltpu.VMEM((heads, HD, HD), BF16),
            pltpu.VMEM((heads, HD, HD), F32),
            pltpu.SemaphoreType.DMA((5, blk_count + 1)),
            pltpu.SemaphoreType.DMA((2, blk_count)),
        ],
        28,
        cost(rows * width * 4 * HD, 12 * rows * width + 4 * blk_count * width * HD),
    )


def chain_body(reverse, got_ref, weight_ref, out_ref):
    devices, share = got_ref.shape[0], got_ref.shape[1]
    pieces = weight_ref.shape[1]
    part = share // pieces
    for p in range(pieces):
        rows = span(p, part)
        carry = jnp.zeros((part, HD), F32)
        for place in reversed(range(devices)) if reverse else range(devices):
            out_ref[place, rows] = carry.astype(BF16)
            carry = weight_ref[place, p] * carry + got_ref[place, rows].astype(F32)


def chain(got, weights, reverse):
    devices, share, _ = got.shape
    (out,) = call(
        functools.partial(chain_body, reverse),
        "chain_states",
        [(got, VMEM), (weights, SMEM)],
        [((devices, share, HD), BF16, VMEM)],
        [],
        16,
        cost(2 * devices * share * HD, 4 * devices * share * HD),
    )
    return out


def swap(x):
    devices = lax.axis_size("seq")
    flat = x.reshape(-1, HD)
    return lax.all_to_all(flat, "seq", 0, 0, tiled=True).reshape(devices, -1, HD)


def after(x, *earlier):
    return lax.optimization_barrier((x, *earlier))[0]


def local(queries, key_vectors, value_vectors, log_decay, grad_output, out_weight):
    rows, width = queries.shape
    heads, blk_count = width // HD, rows // BLK
    tp, me = lax.axis_size("tp"), lax.axis_index("tp")
    seq, place = lax.axis_size("seq"), lax.axis_index("seq")
    chips = tp // 2
    core = [(i, i ^ 1) for i in range(tp)]

    def from_chip(hops):
        return [(i, (i + 2 * hops) % tp) for i in range(tp)]

    own = grad_output
    sibling = lax.ppermute(own, "tp", core)
    first = []
    for j in range(blk_count):
        piece = own[j * BLK : (j + 1) * BLK]
        first.append([lax.ppermute(piece, "tp", from_chip(d)) for d in range(1, chips)])

    cum = jnp.cumsum(log_decay.reshape(heads, blk_count, BLK), axis=2)
    end = cum[:, :, -1]
    prior = jnp.exp(jnp.cumsum(end, axis=1) - end)
    cum = cum.transpose(1, 0, 2).reshape(blk_count, heads // GROUP, GROUP, BLK)

    own_span = jnp.broadcast_to(jnp.sum(end, axis=1)[None], (seq, heads))
    spans = lax.all_to_all(own_span, "seq", 0, 0, tiled=True)
    share = heads * HD // seq
    pieces = max(share // HD, 1)
    mine = lax.dynamic_slice_in_dim(jnp.exp(spans), place * share // HD, pieces, axis=1)

    local_enter, fwd_total = key_totals(key_vectors, value_vectors, cum)
    fwd_got = swap(fwd_total)

    near = near_product(own, sibling, out_weight)
    fwd_out = chain(after(fwd_got, near), mine, False)
    enter_fwd = swap(fwd_out).reshape(heads, HD, HD)

    total = near
    held = [near, fwd_out, enter_fwd]
    grads, sums = [], []
    for j in range(blk_count):
        wait_for = [total] + ([fwd_out] if j == 1 else []) + ([enter_fwd] if j == 2 else [])
        arrived = []
        for x in first[j]:
            x = after(x, *wait_for)
            arrived += [x, lax.ppermute(x, "tp", core)]
        before = total if j else jnp.zeros((heads, HD, HD), F32)
        grad, part, total = far_product(
            j, j == blk_count - 1, before, arrived, out_weight, near, queries, cum, prior
        )
        grads.append(grad)
        sums.append(part)

    bwd_got = swap(total)
    gq, gk_parts, gv_parts = None, [], []
    half = blk_count // 2
    cum_now = after(cum, total)
    for j in range(blk_count):
        if j == half:
            bwd_out = chain(after(bwd_got, gq), mine, True)
            enter_bwd = swap(bwd_out).reshape(heads, HD, HD)
            cum_now = after(cum, bwd_out)
        gq, gk, gv = block_terms(
            j, queries, key_vectors, value_vectors, grads[j], cum_now, prior, local_enter, enter_fwd, gq
        )
        gk_parts.append(gk)
        gv_parts.append(gv)
    gk, gv = later_terms(key_vectors, value_vectors, gk_parts, gv_parts, sums[1:], cum, enter_bwd)
    return gq, gk, gv


def solution(mesh):
    in_specs = (
        P("seq", "tp"),
        P("seq", "tp"),
        P("seq", "tp"),
        P("tp", "seq"),
        P("seq", "tp"),
        P("tp", None),
    )
    out_specs = (P("seq", "tp"), P("seq", "tp"), P("seq", "tp"))
    return jax.shard_map(local, mesh=mesh, in_specs=in_specs, out_specs=out_specs, check_vma=False)
```

time: 424 us -> 250 us (0.59)
  waiting for transfers between devices: 170 us -> 5.04 us
  Pallas kernels: 0 us -> 114 us
  matrix products: 110 us -> 0 us
  other arithmetic: 46.1 us -> 2.72 us
  starting transfers between devices: 0.29 us -> 35.5 us
  local copies, waits for them, and re-layouts: 54.6 us -> 89.8 us
  blocking collectives: 22.4 us -> 0 us
  between operations: 14.9 us -> 1.13 us
    all_gather x3 -> x0, waiting for transfers between devices: 170 us -> none  [the longest x2 120 us: prefix(): everything = jax.tree.map(lambda part: lax.all_gather(part, axis), x)]
    pallas_call x0 -> x13, Pallas kernels: none -> 114 us  [call(): pl.pallas_call(body, in_specs=[spec for _, spec in ins], out_specs=[spec...]
    dot_general x10 -> x0, matrix products: 110 us -> none  [the longest x9 76.7 us: contract(): return jnp.einsum(form, left, right, preferred_element_type=jnp.float32)]
    unnamed x34 -> x116, local copies, waits for them, and re-layouts: 21.6 us -> 84.4 us
    all_to_all x0 -> x5, starting transfers between devices: none -> 30.8 us  [the longest x4 24 us: swap(): lax.all_to_all(flat, 'seq', 0, 0, tiled=True).reshape(devices, -1, HD)]
    select_n x16 -> x0, other arithmetic: 23.5 us -> none  [hop(): return jax.tree.map(lambda a, b: jnp.where(reached, a, b), new, before)]
    unnamed x1 -> x0, blocking collectives: 22.4 us -> none
    reshape x3, local copies, waits for them, and re-layouts: 14.9 us -> 0.94 us  [the longest x1 7.46 us: split_rows(): return matrix.reshape(blk_count, BLK, head_count, HD)]
  transfers between devices with their start and end apart: 3 -> 14, of which waited for: 3 -> 4; matrix products, arithmetic and copies ran while one was open for 34% -> 3% of each run, Pallas kernels for 0% -> 37%
where the time goes in v2:
time: 250 us; the launch traced here: 249 us
  Pallas kernels  114 us (46%)
  local copies, waits for them, and re-layouts  89.8 us (36%)
  starting transfers between devices  35.5 us (14%)
  waiting for transfers between devices  5.04 us (2%)
  other arithmetic  2.72 us (1%)
    pallas_call x13, Pallas kernels, call(): pl.pallas_call(body, in_specs=[spec for _, spec in ins], out_specs=[spec...  114 us
    unnamed x116, local copies, waits for them, and re-layouts  84.4 us
    all_to_all x4, starting transfers between devices, swap(): lax.all_to_all(flat, 'seq', 0, 0, tiled=True).reshape(devices, -1, HD)  24 us
    all_to_all x1, starting transfers between devices, local(): spans = lax.all_to_all(own_span, 'seq', 0, 0, tiled=True)  6.82 us
  transfers between devices with their start and end apart: 14, of which 4 were waited for; matrix products, arithmetic and copies ran while one was open for 3% of the time, Pallas kernels for 37%

profile of v2, /device:TPU:0, one launch (start us, length us, event | category | flops | bytes accessed | tf_op | source)
XLA Modules:
  0.0 248.5 jit_solution(445674308370959878)
XLA Ops:
  2.1 2.3 reduce-window.6
  5.4 6.8 %all-to-all-start.1 = ((f32[8,1,16]{2,1,0:T(1,128)}), f32[8,1,16]{2,1,0:T(1,128)S(1)}, u32[]{:S(2)}, u32[]{:S(2)}) async-start(f32[8,1,16]{2,1,0:T(1,128)} %broadcast_in_dim.10), calls=%async_computation.1 | async-start | bytes 8192 | tf_op jit(solution)/shard_map/all_to_all | solution.py:576
  12.3 3.3 %fusion.1 = (bf16[256,1536]{1,0:T(8,128)(2,1)}, bf16[256,1536]{1,0:T(8,128)(2,1)}, bf16[256,1536]{1,0:T(8,128)(2,1)S(1)}, bf16[256,1536]{1,0:T(8,128)(2,1)}) fusion(bf16[1024,1536]{1,0:T(8,128)(2,1)} %own_hbm.1), kind=kLoop, calls=%fused_computation.7 | loop fusion | bytes 6291456 | tf_op jit(solution)/shard_map/slice | solution.py:567
  21.5 13.2 %key_totals.1 = (f32[4,16,128,128]{3,2,1,0:T(8,128)S(1)}, bf16[16,128,128]{2,1,0:T(8,128)(2,1)}) custom-call(bf16[1024,2048]{1,0:T(8,128)(2,1)S(1)} %copy-done.5, bf16[1024,2048]{1,0:T(8,128)(2,1)S(1)} %copy-done.9, f32[4,4,4,256]{3,2,1,0:T(4,128)S(1)} %reshape.53.cum_ref), custom_call_target="tpu_custom_call" | custom-call | flops 536870912 | bytes 12582912 | tf_op jit(solution)/shard_map/key_totals/pallas_call | solution.py:40
  36.8 6.0 %all-to-all-start = ((bf16[8,256,128]{2,1,0:T(8,128)(2,1)}), bf16[8,256,128]{2,1,0:T(8,128)(2,1)S(1)}, u32[]{:S(2)}, u32[]{:S(2)}) async-start(bf16[8,256,128]{2,1,0:T(8,128)(2,1)} %bitcast.2), calls=%async_computation | async-start | bytes 1048576 | tf_op jit(solution)/shard_map/all_to_all | solution.py:545
  44.7 20.1 %near_product.1.near_hbm = f32[1024,2048]{1,0:T(8,128)S(1)} custom-call(bf16[1024,1536]{1,0:T(8,128)(2,1)S(1)} %copy-done.20, bf16[1024,1536]{1,0:T(8,128)(2,1)} %collective-permute-done.sibling_hbm, bf16[2048,6144]{1,0:T(8,128)(2,1)} %w_hbm.9), custom_call_target="tpu_custom_call" | custom-call | flops 12884901888 | bytes 27262976 | tf_op jit(solution)/shard_map/near_product/pallas_call | solution.py:40
  64.8 3.3 %copy-done.13 = f32[1024,2048]{1,0:T(8,128)} copy-done((f32[1024,2048]{1,0:T(8,128)}, f32[1024,2048]{1,0:T(8,128)S(1)}, u32[]{:S(2)}) %copy-start.13) | copy-done | bytes 8388632
  73.8 3.4 %copy-done.14 = f32[1024,2048]{1,0:T(8,128)S(1)} copy-done((f32[1024,2048]{1,0:T(8,128)S(1)}, f32[1024,2048]{1,0:T(8,128)}, u32[]{:S(2)}) %copy-start.14) | copy-done | bytes 8388632
  78.3 8.7 %far_product.4 = (bf16[256,2048]{1,0:T(8,128)(2,1)S(1)}, f32[16,128,128]{2,1,0:T(8,128)}, f32[16,128,128]{2,1,0:T(8,128)S(1)}) custom-call(f32[16,128,128]{2,1,0:T(8,128)S(1)} %broadcast_in_dim.4.before_hbm, f32[1024,2048]{1,0:T(8,128)S(1)} %copy-done.14, bf16[1024,2048]{1,0:T(8,128)(2,1)S(1)} %copy-done, f32[4,4,4,256]{3,2,1,0:T(4,128)S(1)} %reshape.53.cum_ref, ...), custom_call_target="tpu_custom_call" | custom-call | flops 3355443200 | bytes 21495808 | tf_op jit(solution)/shard_map/far_product/pallas_call | solution.py:40
  88.2 6.0 %all-to-all-start.2 = ((bf16[8,256,128]{2,1,0:T(8,128)(2,1)}), bf16[8,256,128]{2,1,0:T(8,128)(2,1)S(1)}, u32[]{:S(2)}, u32[]{:S(2)}) async-start(bf16[8,256,128]{2,1,0:T(8,128)(2,1)} %chain_states.2), calls=%async_computation.2 | async-start | bytes 1048576 | tf_op jit(solution)/shard_map/all_to_all | solution.py:545
  98.8 3.4 %copy-done.15 = f32[1024,2048]{1,0:T(8,128)S(1)} copy-done((f32[1024,2048]{1,0:T(8,128)S(1)}, f32[1024,2048]{1,0:T(8,128)}, u32[]{:S(2)}) %copy-start.15) | copy-done | bytes 8388632
  105.7 8.1 %far_product.5 = (bf16[256,2048]{1,0:T(8,128)(2,1)S(1)}, f32[16,128,128]{2,1,0:T(8,128)S(1)}, f32[16,128,128]{2,1,0:T(8,128)S(1)}) custom-call(f32[16,128,128]{2,1,0:T(8,128)S(1)} %copy-done.50, f32[1024,2048]{1,0:T(8,128)S(1)} %copy-done.15, bf16[1024,2048]{1,0:T(8,128)(2,1)S(1)} %copy-done.1, f32[4,4,4,256]{3,2,1,0:T(4,128)S(1)} %reshape.53.cum_ref, ...), custom_call_target="tpu_custom_call" | custom-call | flops 3355443200 | bytes 21495808 | tf_op jit(solution)/shard_map/far_product/pallas_call | solution.py:40
  118.3 2.2 copy-done.2
  120.5 3.4 %copy-done.16 = f32[1024,2048]{1,0:T(8,128)S(1)} copy-done((f32[1024,2048]{1,0:T(8,128)S(1)}, f32[1024,2048]{1,0:T(8,128)}, u32[]{:S(2)}) %copy-start.16) | copy-done | bytes 8388632
  125.1 8.3 %far_product.6 = (bf16[256,2048]{1,0:T(8,128)(2,1)S(1)}, f32[16,128,128]{2,1,0:T(8,128)S(1)}, f32[16,128,128]{2,1,0:T(8,128)S(1)}) custom-call(f32[16,128,128]{2,1,0:T(8,128)S(1)} %copy-done.48, f32[1024,2048]{1,0:T(8,128)S(1)} %copy-done.16, bf16[1024,2048]{1,0:T(8,128)(2,1)S(1)} %copy-done.2, f32[4,4,4,256]{3,2,1,0:T(4,128)S(1)} %reshape.53.cum_ref, ...), custom_call_target="tpu_custom_call" | custom-call | flops 3355443200 | bytes 21495808 | tf_op jit(solution)/shard_map/far_product/pallas_call | solution.py:40
  136.0 2.3 collective-permute-done.8.refs_1_
  138.2 8.7 %far_product.7 = (bf16[256,2048]{1,0:T(8,128)(2,1)S(1)}, f32[16,128,128]{2,1,0:T(8,128)S(1)}, bf16[16,128,128]{2,1,0:T(8,128)(2,1)S(1)}) custom-call(f32[16,128,128]{2,1,0:T(8,128)S(1)} %get-tuple-element.45.before_hbm, f32[1024,2048]{1,0:T(8,128)S(1)} %copy-done.16, bf16[1024,2048]{1,0:T(8,128)(2,1)S(1)} %copy-done.2, ...), custom_call_target="tpu_custom_call" | custom-call | flops 3355443200 | bytes 21495808 | tf_op jit(solution)/shard_map/far_product/pallas_call | solution.py:40
  149.7 6.0 %all-to-all-start.3 = ((bf16[8,256,128]{2,1,0:T(8,128)(2,1)}), bf16[8,256,128]{2,1,0:T(8,128)(2,1)S(1)}, u32[]{:S(2)}, u32[]{:S(2)}) async-start(bf16[8,256,128]{2,1,0:T(8,128)(2,1)} %bitcast.22), calls=%async_computation.3 | async-start | bytes 1048576 | tf_op jit(solution)/shard_map/all_to_all | solution.py:545
  157.9 2.2 copy-done.6
  160.1 2.2 copy-done.10
  162.3 2.2 copy-done.18
  164.5 8.3 %block_terms.4 = (bf16[1024,2048]{1,0:T(8,128)(2,1)}, bf16[256,2048]{1,0:T(8,128)(2,1)S(1)}, bf16[256,2048]{1,0:T(8,128)(2,1)S(1)}) custom-call(bf16[1024,2048]{1,0:T(8,128)(2,1)S(1)} %copy-done.3, bf16[1024,2048]{1,0:T(8,128)(2,1)S(1)} %copy-done.6, bf16[1024,2048]{1,0:T(8,128)(2,1)S(1)} %copy-done.10, bf16[256,2048]{1,0:T(8,128)(2,1)S(1)} %get-tuple-element.52.grad_hbm, ...), custom_call_target="tpu_custom_call" | custom-call | flops 1476395008 | bytes 8912896 | tf_op jit(solution)/shard_map/block_terms/pallas_call | solution.py:40
  174.7 8.3 %block_terms.5 = (bf16[1024,2048]{1,0:T(8,128)(2,1)}, bf16[256,2048]{1,0:T(8,128)(2,1)S(1)}, bf16[256,2048]{1,0:T(8,128)(2,1)S(1)}) custom-call(bf16[1024,2048]{1,0:T(8,128)(2,1)S(1)} %copy-done.3, bf16[1024,2048]{1,0:T(8,128)(2,1)S(1)} %copy-done.6, bf16[1024,2048]{1,0:T(8,128)(2,1)S(1)} %copy-done.10, ...), custom_call_target="tpu_custom_call", output_to_operand_aliasing={{0}: (8, {})} | custom-call | flops 1476395008 | bytes 8912896 | tf_op jit(solution)/shard_map/block_terms/pallas_call | solution.py:40
  186.5 6.0 %all-to-all-start.4 = ((bf16[8,256,128]{2,1,0:T(8,128)(2,1)}), bf16[8,256,128]{2,1,0:T(8,128)(2,1)S(1)}, u32[]{:S(2)}, u32[]{:S(2)}) async-start(bf16[8,256,128]{2,1,0:T(8,128)(2,1)} %chain_states.3), calls=%async_computation.4 | async-start | bytes 1048576 | tf_op jit(solution)/shard_map/all_to_all | solution.py:545
  194.7 2.2 copy-done.7
  196.9 2.2 copy-done.11
  199.1 2.2 copy-done.19
  201.3 8.3 %block_terms.6 = (bf16[1024,2048]{1,0:T(8,128)(2,1)}, bf16[256,2048]{1,0:T(8,128)(2,1)S(1)}, bf16[256,2048]{1,0:T(8,128)(2,1)S(1)}) custom-call(bf16[1024,2048]{1,0:T(8,128)(2,1)S(1)} %copy-done.4, bf16[1024,2048]{1,0:T(8,128)(2,1)S(1)} %copy-done.7, bf16[1024,2048]{1,0:T(8,128)(2,1)S(1)} %copy-done.11, ...), custom_call_target="tpu_custom_call", output_to_operand_aliasing={{0}: (8, {})} | custom-call | flops 1476395008 | bytes 8912896 | tf_op jit(solution)/shard_map/block_terms/pallas_call | solution.py:40
  211.6 8.3 %block_terms.7 = (bf16[1024,2048]{1,0:T(8,128)(2,1)}, bf16[256,2048]{1,0:T(8,128)(2,1)S(1)}, bf16[256,2048]{1,0:T(8,128)(2,1)S(1)}) custom-call(bf16[1024,2048]{1,0:T(8,128)(2,1)S(1)} %copy-done.4, bf16[1024,2048]{1,0:T(8,128)(2,1)S(1)} %copy-done.7, bf16[1024,2048]{1,0:T(8,128)(2,1)S(1)} %copy-done.11, ...), custom_call_target="tpu_custom_call", output_to_operand_aliasing={{0}: (8, {})} | custom-call | flops 1476395008 | bytes 8912896 | tf_op jit(solution)/shard_map/block_terms/pallas_call | solution.py:40
  221.9 2.2 copy-done.8
  224.1 2.2 copy-done.12
  237.3 11.0 %later_terms.1 = (bf16[1024,2048]{1,0:T(8,128)(2,1)}, bf16[1024,2048]{1,0:T(8,128)(2,1)}) custom-call(bf16[1024,2048]{1,0:T(8,128)(2,1)S(1)} %copy-done.8, bf16[1024,2048]{1,0:T(8,128)(2,1)S(1)} %copy-done.12, f32[4,4,4,256]{3,2,1,0:T(4,128)S(1)} %reshape.53.cum_ref, bf16[16,128,128]{2,1,0:T(8,128)(2,1)S(1)} %bitcast.21, bf16[256,2048]{1,0:T(8,128)(2,1)S(1)} %copy-done.30, ...), custom_call_target="tpu_custom_call" | custom-call | flops 1073741824 | bytes 29360128 | tf_op jit(solution)/shard_map/later_terms/pallas_call | solution.py:40
  (141 shorter events, 64.3 us)
Async XLA Ops:
  0.6 42.1 %collective-permute-start = (bf16[1024,1536]{1,0:T(8,128)(2,1)}, bf16[1024,1536]{1,0:T(8,128)(2,1)}, u32[]{:S(2)}, u32[]{:S(2)}) collective-permute-start(bf16[1024,1536]{1,0:T(8,128)(2,1)} %own_hbm.1), channel_id=1, source_target_pairs={{0,1},{1,0},{2,3},{3,2},{4,5},{5,4},{6,7},{7,6},{8,9},{9,8},{10,11... | collective-permute-start | bytes 9437192 | tf_op jit(solution)/shard_map/ppermute | solution.py:564
  5.4 31.3 %all-to-all-start.1 = ((f32[8,1,16]{2,1,0:T(1,128)}), f32[8,1,16]{2,1,0:T(1,128)S(1)}, u32[]{:S(2)}, u32[]{:S(2)}) async-start(f32[8,1,16]{2,1,0:T(1,128)} %broadcast_in_dim.10), calls=%async_computation.1 | async-start | bytes 8192 | tf_op jit(solution)/shard_map/all_to_all | solution.py:576
  15.6 52.5 %collective-permute-start.1 = (bf16[256,1536]{1,0:T(8,128)(2,1)S(1)}, bf16[256,1536]{1,0:T(8,128)(2,1)S(1)}, u32[]{:S(2)}, u32[]{:S(2)}) collective-permute-start(bf16[256,1536]{1,0:T(8,128)(2,1)S(1)} %get-tuple-element.75), channel_id=1, source_target_pairs={{0,2},{1,3},{2,0},{3,1},{4,6},{5,7},{6,4},{7,5},{8,10},{9,11},{10,... | collective-permute-start | bytes 2359304 | tf_op jit(solution)/shard_map/ppermute | solution.py:568
  17.1 2.2 copy-start.5
  19.3 2.2 copy-start.9
  36.8 32.3 %all-to-all-start = ((bf16[8,256,128]{2,1,0:T(8,128)(2,1)}), bf16[8,256,128]{2,1,0:T(8,128)(2,1)S(1)}, u32[]{:S(2)}, u32[]{:S(2)}) async-start(bf16[8,256,128]{2,1,0:T(8,128)(2,1)} %bitcast.2), calls=%async_computation | async-start | bytes 1048576 | tf_op jit(solution)/shard_map/all_to_all | solution.py:545
  64.7 3.3 %copy-start.13 = (f32[1024,2048]{1,0:T(8,128)}, f32[1024,2048]{1,0:T(8,128)S(1)}, u32[]{:S(2)}) copy-start(f32[1024,2048]{1,0:T(8,128)S(1)} %near_product.1.near_hbm) | copy-start | bytes 25165828
  68.1 2.5 %collective-permute-start.2 = (bf16[256,1536]{1,0:T(8,128)(2,1)S(1)}, bf16[256,1536]{1,0:T(8,128)(2,1)S(1)}, u32[]{:S(2)}, u32[]{:S(2)}) collective-permute-start(bf16[256,1536]{1,0:T(8,128)(2,1)S(1)} %collective-permute-done.1.refs_0_), channel_id=1, source_target_pairs={{0,1},{1,0},{2,3},{3,2},{4,5},{5,4},{6,7},{7,6},{8,9},{9,8},{10,11... | collective-permute-start | bytes 2359304 | tf_op jit(solution)/shard_map/ppermute | solution.py:596
  68.1 20.2 %collective-permute-start.3 = (bf16[256,1536]{1,0:T(8,128)(2,1)}, bf16[256,1536]{1,0:T(8,128)(2,1)S(1)}, u32[]{:S(2)}, u32[]{:S(2)}) collective-permute-start(bf16[256,1536]{1,0:T(8,128)(2,1)} %get-tuple-element.74), channel_id=1, source_target_pairs={{0,2},{1,3},{2,0},{3,1},{4,6},{5,7},{6,4},{7,5},{8,10},{9,11},{10,... | collective-permute-start | bytes 2359304 | tf_op jit(solution)/shard_map/ppermute | solution.py:568
  71.6 2.2 copy-start
  73.8 3.4 %copy-start.14 = (f32[1024,2048]{1,0:T(8,128)S(1)}, f32[1024,2048]{1,0:T(8,128)}, u32[]{:S(2)}) copy-start(f32[1024,2048]{1,0:T(8,128)} %copy-done.13) | copy-start | bytes 25165828
  88.2 7.5 %copy-start.51 = (bf16[256,1536]{1,0:T(8,128)(2,1)}, bf16[256,1536]{1,0:T(8,128)(2,1)S(1)}, u32[]{:S(2)}) copy-start(bf16[256,1536]{1,0:T(8,128)(2,1)S(1)} %collective-permute-done.3.refs_0_) | copy-start | bytes 2359300
  88.2 7.5 %collective-permute-start.4 = (bf16[256,1536]{1,0:T(8,128)(2,1)S(1)}, bf16[256,1536]{1,0:T(8,128)(2,1)S(1)}, u32[]{:S(2)}, u32[]{:S(2)}) collective-permute-start(bf16[256,1536]{1,0:T(8,128)(2,1)S(1)} %collective-permute-done.3.refs_0_), channel_id=1, source_target_pairs={{0,1},{1,0},{2,3},{3,2},{4,5},{5,4},{6,7},{7,6},{8,9},{9,8},{10,11... | collective-permute-start | bytes 2359304 | tf_op jit(solution)/shard_map/ppermute | solution.py:596
  88.2 27.5 %all-to-all-start.2 = ((bf16[8,256,128]{2,1,0:T(8,128)(2,1)}), bf16[8,256,128]{2,1,0:T(8,128)(2,1)S(1)}, u32[]{:S(2)}, u32[]{:S(2)}) async-start(bf16[8,256,128]{2,1,0:T(8,128)(2,1)} %chain_states.2), calls=%async_computation.2 | async-start | bytes 1048576 | tf_op jit(solution)/shard_map/all_to_all | solution.py:545
  94.2 21.5 %collective-permute-start.5 = (bf16[256,1536]{1,0:T(8,128)(2,1)}, bf16[256,1536]{1,0:T(8,128)(2,1)}, u32[]{:S(2)}, u32[]{:S(2)}) collective-permute-start(bf16[256,1536]{1,0:T(8,128)(2,1)} %get-tuple-element.76), channel_id=1, source_target_pairs={{0,2},{1,3},{2,0},{3,1},{4,6},{5,7},{6,4},{7,5},{8,10},{9,11},{10,... | collective-permute-start | bytes 2359304 | tf_op jit(solution)/shard_map/ppermute | solution.py:568
  96.7 2.2 copy-start.1
  98.8 3.4 %copy-start.15 = (f32[1024,2048]{1,0:T(8,128)S(1)}, f32[1024,2048]{1,0:T(8,128)}, u32[]{:S(2)}) copy-start(f32[1024,2048]{1,0:T(8,128)} %copy-done.13) | copy-start | bytes 25165828
  115.8 2.5 %collective-permute-start.6 = (bf16[256,1536]{1,0:T(8,128)(2,1)}, bf16[256,1536]{1,0:T(8,128)(2,1)S(1)}, u32[]{:S(2)}, u32[]{:S(2)}) collective-permute-start(bf16[256,1536]{1,0:T(8,128)(2,1)} %collective-permute-done.5.refs_0_), channel_id=1, source_target_pairs={{0,1},{1,0},{2,3},{3,2},{4,5},{5,4},{6,7},{7,6},{8,9},{9,8},{10,11... | collective-permute-start | bytes 2359304 | tf_op jit(solution)/shard_map/ppermute | solution.py:596
  115.8 20.2 %collective-permute-start.7 = (bf16[256,1536]{1,0:T(8,128)(2,1)}, bf16[256,1536]{1,0:T(8,128)(2,1)S(1)}, u32[]{:S(2)}, u32[]{:S(2)}) collective-permute-start(bf16[256,1536]{1,0:T(8,128)(2,1)} %get-tuple-element.73), channel_id=1, source_target_pairs={{0,2},{1,3},{2,0},{3,1},{4,6},{5,7},{6,4},{7,5},{8,10},{9,11},{10,... | collective-permute-start | bytes 2359304 | tf_op jit(solution)/shard_map/ppermute | solution.py:568
  118.3 2.2 copy-start.2
  120.5 3.4 %copy-start.16 = (f32[1024,2048]{1,0:T(8,128)S(1)}, f32[1024,2048]{1,0:T(8,128)}, u32[]{:S(2)}) copy-start(f32[1024,2048]{1,0:T(8,128)} %copy-done.13) | copy-start | bytes 25165828
  135.9 2.3 collective-permute-start.8
  149.7 35.3 %all-to-all-start.3 = ((bf16[8,256,128]{2,1,0:T(8,128)(2,1)}), bf16[8,256,128]{2,1,0:T(8,128)(2,1)S(1)}, u32[]{:S(2)}, u32[]{:S(2)}) async-start(bf16[8,256,128]{2,1,0:T(8,128)(2,1)} %bitcast.22), calls=%async_computation.3 | async-start | bytes 1048576 | tf_op jit(solution)/shard_map/all_to_all | solution.py:545
  155.7 2.2 copy-start.3
  157.9 2.2 copy-start.6
  164.5 10.3 %copy-start.24 = (bf16[256,2048]{1,0:T(8,128)(2,1)S(1)}, bf16[256,2048]{1,0:T(8,128)(2,1)}, u32[]{:S(2)}) copy-start(bf16[256,2048]{1,0:T(8,128)(2,1)} %copy-done.23) | copy-start | bytes 3145732
  174.7 17.8 %copy-start.28 = (bf16[256,2048]{1,0:T(8,128)(2,1)S(1)}, bf16[256,2048]{1,0:T(8,128)(2,1)}, u32[]{:S(2)}) copy-start(bf16[256,2048]{1,0:T(8,128)(2,1)} %copy-done.27) | copy-start | bytes 3145732
  186.5 35.4 %all-to-all-start.4 = ((bf16[8,256,128]{2,1,0:T(8,128)(2,1)}), bf16[8,256,128]{2,1,0:T(8,128)(2,1)S(1)}, u32[]{:S(2)}, u32[]{:S(2)}) async-start(bf16[8,256,128]{2,1,0:T(8,128)(2,1)} %chain_states.3), calls=%async_computation.4 | async-start | bytes 1048576 | tf_op jit(solution)/shard_map/all_to_all | solution.py:545
  192.5 2.2 copy-start.4
  201.3 10.3 %copy-start.38 = (bf16[256,2048]{1,0:T(8,128)(2,1)S(1)}, bf16[256,2048]{1,0:T(8,128)(2,1)}, u32[]{:S(2)}) copy-start(bf16[256,2048]{1,0:T(8,128)(2,1)} %copy-done.37) | copy-start | bytes 3145732
  211.6 10.3 %copy-start.22 = (f32[16,128,128]{2,1,0:T(8,128)S(1)}, f32[16,128,128]{2,1,0:T(8,128)}, u32[]{:S(2)}) copy-start(f32[16,128,128]{2,1,0:T(8,128)} %copy-done.21) | copy-start | bytes 3145732
  221.9 2.2 copy-start.8
  (40 other events, 51.4 us)

commit v3 on v2

--- a/solution.py
+++ b/solution.py
@@ -18,6 +18,7 @@
 TN = (((0,), (0,)), ((), ()))
 
 ANY = pl.BlockSpec(memory_space=pl.ANY)
+HBM = pl.BlockSpec(memory_space=pltpu.HBM)
 VMEM = pl.BlockSpec(memory_space=pltpu.VMEM)
 SMEM = pl.BlockSpec(memory_space=pltpu.SMEM)
 BF16 = jnp.bfloat16
@@ -41,13 +42,16 @@
         body,
         in_specs=[spec for _, spec in ins],
         out_specs=[spec for _, _, spec in outs],
-        out_shape=[jax.ShapeDtypeStruct(shape, dtype) for shape, dtype, _ in outs],
+        out_shape=[
+            pltpu.HBM(shape, dtype) if spec is HBM else jax.ShapeDtypeStruct(shape, dtype)
+            for shape, dtype, spec in outs
+        ],
         scratch_shapes=scratch,
         input_output_aliases=aliases or {},
         compiler_params=pltpu.CompilerParams(vmem_limit_bytes=limit * MIB),
         cost_estimate=estimate,
         name=name,
-    )(*[array for array, _ in ins])
+    )(*[pltpu.with_memory_space_constraint(x, pltpu.HBM) if spec is HBM else x for x, spec in ins])
 
 
 def copy_of(source, target, sem):
@@ -66,7 +70,7 @@
     return slice(h * HD, (h + 1) * HD)
 
 
-def key_body(k_hbm, v_hbm, cum_ref, local_hbm, total_ref, k_ref, v_ref, local_ref, load_sems, store_sems):
+def key_body(k_hbm, v_hbm, cum_ref, span_ref, local_hbm, total_ref, k_ref, v_ref, local_ref, load_sems, store_sems):
     blk_count, groups, group, _ = cum_ref.shape
     wide = group * HD
 
@@ -92,8 +96,8 @@
         rows = pl.ds(pl.multiple_of(j * BLK, BLK), BLK)
 
         def some_heads(g):
-            cum = cum_ref[j, g].T
-            end = cum[BLK - 1 : BLK, :]
+            cum = cum_ref[j, g]
+            end = cum[:, BLK - 1 : BLK]
             weight = jnp.exp(end - cum)
             end_weight = jnp.exp(end)
             lanes = lanes_of(g, wide)
@@ -101,27 +105,40 @@
             keys, values, entered = k_ref[rows, lanes], v_ref[rows, lanes], local_ref[j, these]
             left = []
             for h in range(group):
-                scaled = (keys[:, head_in(h)].astype(F32) * weight[:, h : h + 1]).astype(BF16)
-                sums = mm(scaled, values[:, head_in(h)], TN)
-                left.append(entered[h] * end_weight[:, h : h + 1] + sums)
+                turned = keys[:, head_in(h)].T.astype(F32)
+                scaled = (turned * weight[h : h + 1]).astype(BF16)
+                sums = mm(scaled, values[:, head_in(h)], NN)
+                left.append(entered[h] * end_weight[h : h + 1] + sums)
             local_ref[j + 1, these] = jnp.stack(left)
 
         loop(groups, some_heads)
 
     loop(blk_count, block)
-    total_ref[...] = local_ref[blk_count].astype(BF16)
+    devices, share = total_ref.shape[0], total_ref.shape[1] - ROW
+    total_ref[:, :share] = local_ref[blk_count].astype(BF16).reshape(devices, share, HD)
+    left, parts = jnp.broadcast_to(span_ref[...], (ROW, HD)), jnp.zeros((ROW, HD), F32)
+    at_row = lax.broadcasted_iota(jnp.int32, (ROW, HD), 0)
+    for n in range(3):
+        rounded = left.astype(BF16).astype(F32)
+        parts = jnp.where(at_row == n, rounded, parts)
+        left = left - rounded
+    for d in range(devices):
+        total_ref[d, share:] = parts.astype(BF16)
     for j in range(blk_count):
         store(j).wait()
 
 
-def key_totals(keys, values, cum):
+def key_totals(keys, values, cum, own_span, devices):
     rows, width = keys.shape
     blk_count, heads = cum.shape[0], width // HD
     return call(
         key_body,
         "key_totals",
-        [(keys, ANY), (values, ANY), (cum, VMEM)],
-        [((blk_count, heads, HD, HD), F32, ANY), ((heads, HD, HD), BF16, VMEM)],
+        [(keys, HBM), (values, HBM), (cum, VMEM), (own_span, VMEM)],
+        [
+            ((blk_count, heads, HD, HD), F32, HBM),
+            ((devices, heads * HD // devices + ROW, HD), BF16, VMEM),
+        ],
         [
             pltpu.VMEM((rows, width), BF16),
             pltpu.VMEM((rows, width), BF16),
@@ -188,8 +205,8 @@
     (out,) = call(
         functools.partial(near_body, wide),
         "near_product",
-        [(own, ANY), (sibling, ANY), (weight, ANY)],
-        [((rows, width), F32, ANY)],
+        [(own, HBM), (sibling, HBM), (weight, HBM)],
+        [((rows, width), F32, HBM)],
         [
             pltpu.VMEM((rows, 2 * depth), BF16),
             pltpu.VMEM((width, 2 * depth), BF16),
@@ -204,17 +221,42 @@
     return out
 
 
-def far_body(blk, chips, before_hbm, near_hbm, q_hbm, cum_ref, prior_ref, w_hbm, *refs):
-    pieces = refs[: 2 * (chips - 1)]
-    grad_hbm, sums_hbm, total_hbm, piece_ref, w_ref, near_ref, q_ref, before_ref = refs[2 * (chips - 1) :][:8]
-    grad_ref, sums_ref, total_ref, piece_sems, load_sems, store_sems = refs[2 * (chips - 1) + 8 :]
+def far_sums(blks, g, group, q_ref, cum_ref, prior_ref, grad, before_ref, sums_refs, total_ref):
+    wide = group * HD
+    lanes, these = lanes_of(g, wide), pl.ds(g * group, group)
+    chained = before_ref[these] if before_ref is not None else None
+    chained = [chained[h] for h in range(group)] if chained is not None else None
+    for n, blk in enumerate(blks):
+        weight = jnp.exp(cum_ref[blk, g])
+        queries = q_ref[span(n, BLK), lanes]
+        sums = []
+        for h in range(group):
+            turned = queries[:, head_in(h)].T.astype(F32)
+            scaled = (turned * weight[h : h + 1]).astype(BF16)
+            sums.append(mm(scaled, grad[span(n, BLK), head_in(h)], NN))
+        sums_refs[n][these] = jnp.stack(sums)
+        if chained is None:
+            chained = sums
+        else:
+            chained = [chained[h] + prior_ref[g * group + h, blk] * sums[h] for h in range(group)]
+    total_ref[these] = jnp.stack(chained).astype(total_ref.dtype)
+
+
+def far_body(chips, blks, keep, before_ref, near_hbm, q_hbm, cum_ref, prior_ref, w_hbm, *refs):
+    pieces, refs = refs[: 2 * (chips - 1)], refs[2 * (chips - 1) :]
+    count = len(blks)
+    (grad_hbm, total_ref, *sums_hbm), refs = refs[: 2 + count], refs[2 + count :]
+    w_ref, refs = refs[0], refs[1:]
+    if keep:
+        (last_near_ref, last_q_ref), refs = refs[:2], refs[2:]
+    piece_ref, near_ref, q_ref, grad_ref, sums_ref, piece_sems, load_sems, store_sems = refs
+    here = blks[0] * BLK
     rows, depth = pieces[0].shape
     _, groups, group, _ = cum_ref.shape
     wide = group * HD
     me = lax.axis_index("tp")
     side = lax.rem(me, 2)
     chip = lax.div(me, 2)
-    block = pl.ds(blk * BLK, BLK)
 
     def piece_load(n):
         at = 2 * (n // 2) + (side if n % 2 == 0 else 1 - side)
@@ -222,33 +264,39 @@
 
     def loads(g):
         part, lanes = pl.ds(g * wide, wide), lanes_of(g, wide)
-        these = pl.ds(g * group, group)
         found = []
         for d in range(1, chips):
             owner = lax.rem(chip + chips - d, chips)
             held = pl.ds((d - 1) * 2 * depth, 2 * depth)
             found.append(
-                copy_of(w_hbm.at[part, lanes_of(owner, 2 * depth)], w_ref.at[part, held], load_sems.at[d + 2, g])
+                copy_of(w_hbm.at[part, lanes_of(owner, 2 * depth)], w_ref.at[part, held], load_sems.at[d + 1, g])
             )
-        found.append(copy_of(near_hbm.at[block, lanes], near_ref.at[:, lanes], load_sems.at[0, g]))
-        found.append(copy_of(q_hbm.at[block, lanes], q_ref.at[:, lanes], load_sems.at[1, g]))
-        if blk:
-            found.append(copy_of(before_hbm.at[these], before_ref.at[these], load_sems.at[2, g]))
+        found.append(copy_of(near_hbm.at[pl.ds(here, rows), lanes], near_ref.at[:, lanes], load_sems.at[0, g]))
+        found.append(copy_of(q_hbm.at[pl.ds(here, rows), lanes], q_ref.at[:, lanes], load_sems.at[1, g]))
         return found
+
+    def last_loads():
+        if not keep:
+            return ()
+        block = pl.ds(here + rows, BLK)
+        return (
+            copy_of(near_hbm.at[block], last_near_ref, piece_sems.at[len(pieces)]),
+            copy_of(q_hbm.at[block], last_q_ref, piece_sems.at[len(pieces) + 1]),
+        )
 
     def stores(g):
         these, lanes = pl.ds(g * group, group), lanes_of(g, wide)
-        return (
-            copy_of(total_ref.at[these], total_hbm.at[these], store_sems.at[0, g]),
-            copy_of(grad_ref.at[:, lanes], grad_hbm.at[:, lanes], store_sems.at[1, g]),
-            copy_of(sums_ref.at[these], sums_hbm.at[these], store_sems.at[2, g]),
-        )
+        return [copy_of(grad_ref.at[:, lanes], grad_hbm.at[:, lanes], store_sems.at[count, g])] + [
+            copy_of(sums_ref.at[n, these], sums_hbm[n].at[these], store_sems.at[n, g]) for n in range(count)
+        ]
 
     for n in range(len(pieces)):
         piece_load(n).start()
     for g in range(groups):
         for copy in loads(g):
             copy.start()
+    for copy in last_loads():
+        copy.start()
     for n in range(len(pieces)):
         piece_load(n).wait()
 
@@ -257,64 +305,114 @@
             copy.wait()
         lanes = lanes_of(g, wide)
         part = pl.ds(pl.multiple_of(g * wide, wide), wide)
-        weight = jnp.exp(cum_ref[blk, g].T)
-        queries = q_ref[:, lanes]
         grad = (near_ref[:, lanes] + mm(piece_ref[...], w_ref[part], NT)).astype(BF16)
-        these = pl.ds(g * group, group)
-        before = before_ref[these] if blk else None
-        sums, total = [], []
-        for h in range(group):
-            scaled = (queries[:, head_in(h)].astype(F32) * weight[:, h : h + 1]).astype(BF16)
-            sums.append(mm(scaled, grad[:, head_in(h)], TN))
-            total.append(before[h] + prior_ref[g * group + h, blk] * sums[h] if blk else sums[h])
         grad_ref[:, lanes] = grad
-        sums_ref[these] = jnp.stack(sums)
-        total_ref[these] = jnp.stack(total).astype(total_ref.dtype)
+        sums_refs = [sums_ref.at[n] for n in range(count)]
+        before = before_ref if blks[0] else None
+        far_sums(blks, g, group, q_ref, cum_ref, prior_ref, grad, before, sums_refs, total_ref)
         for copy in stores(g):
             copy.start()
 
     loop(groups, some_heads)
+    for copy in last_loads():
+        copy.wait()
     for g in range(groups):
         for copy in stores(g):
             copy.wait()
 
 
-def far_product(blk, last, before, pieces, weight, near, queries, cum, prior):
+def far_product(start, keep, before, pieces, weight, near, queries, cum, prior):
     rows, depth = pieces[0].shape
     _, groups, group, _ = cum.shape
     heads = groups * group
     width = heads * HD
     chips = len(pieces) // 2 + 1
-    total_type = BF16 if last else F32
+    blks = list(range(start, start + rows // BLK))
+    states = (heads, HD, HD)
+    far_depth = 2 * (chips - 1) * depth
+    kept = [((width, far_depth), BF16, VMEM), ((BLK, width), F32, VMEM), ((BLK, width), BF16, VMEM)]
+    return call(
+        functools.partial(far_body, chips, blks, keep),
+        "far_product",
+        [(before, VMEM), (near, HBM), (queries, HBM), (cum, VMEM), (prior, SMEM), (weight, HBM)]
+        + [(piece, ANY) for piece in pieces],
+        [((rows, width), BF16, HBM), (states, F32, VMEM)]
+        + [(states, F32, HBM)] * len(blks)
+        + (kept if keep else []),
+        ([] if keep else [pltpu.VMEM((width, far_depth), BF16)])
+        + [
+            pltpu.VMEM((rows, far_depth), BF16),
+            pltpu.VMEM((rows, width), F32),
+            pltpu.VMEM((rows, width), BF16),
+            pltpu.VMEM((rows, width), BF16),
+            pltpu.VMEM((len(blks), *states), F32),
+            pltpu.SemaphoreType.DMA((len(pieces) + 2,)),
+            pltpu.SemaphoreType.DMA((chips + 1, groups)),
+            pltpu.SemaphoreType.DMA((len(blks) + 1, groups)),
+        ],
+        32,
+        cost(
+            2 * rows * width * (far_depth + HD),
+            2 * far_depth * (rows + width) + 8 * rows * width + 12 * width * HD,
+        ),
+    )
+
+
+def last_body(blk, before_ref, near_ref, q_ref, cum_ref, prior_ref, w_ref, *refs):
+    pieces, (grad_hbm, sums_hbm, total_ref, grad_ref, sums_ref, sems) = refs[:-6], refs[-6:]
+    depth = pieces[0].shape[1]
+    _, groups, group, _ = cum_ref.shape
+    wide = group * HD
+    side = lax.rem(lax.axis_index("tp"), 2)
+
+    def stores(g):
+        these, lanes = pl.ds(g * group, group), lanes_of(g, wide)
+        return (
+            copy_of(grad_ref.at[:, lanes], grad_hbm.at[:, lanes], sems.at[0, g]),
+            copy_of(sums_ref.at[these], sums_hbm.at[these], sems.at[1, g]),
+        )
+
+    def some_heads(g):
+        lanes = lanes_of(g, wide)
+        part = pl.ds(pl.multiple_of(g * wide, wide), wide)
+        total = near_ref[:, lanes]
+        for n, piece in enumerate(pieces):
+            at = 2 * (n // 2) + (side if n % 2 == 0 else 1 - side)
+            total += mm(piece[...], w_ref[part, lanes_of(at, depth)], NT)
+        grad = total.astype(BF16)
+        grad_ref[:, lanes] = grad
+        far_sums([blk], g, group, q_ref, cum_ref, prior_ref, grad, before_ref, [sums_ref], total_ref)
+        for copy in stores(g):
+            copy.start()
+
+    loop(groups, some_heads)
+    for g in range(groups):
+        for copy in stores(g):
+            copy.wait()
+
+
+def last_product(before, pieces, weight, near, queries, cum, prior):
+    rows, depth = pieces[0].shape
+    blk_count, groups, group, _ = cum.shape
+    heads = groups * group
+    width = heads * HD
     states = (heads, HD, HD)
     return call(
-        functools.partial(far_body, blk, chips),
-        "far_product",
-        [(before, ANY), (near, ANY), (queries, ANY), (cum, VMEM), (prior, SMEM), (weight, ANY)]
-        + [(piece, ANY) for piece in pieces],
-        [((rows, width), BF16, ANY), (states, F32, ANY), (states, total_type, ANY)],
-        [
-            pltpu.VMEM((rows, 2 * (chips - 1) * depth), BF16),
-            pltpu.VMEM((width, 2 * (chips - 1) * depth), BF16),
-            pltpu.VMEM((rows, width), F32),
-            pltpu.VMEM((rows, width), BF16),
-            pltpu.VMEM(states, F32),
-            pltpu.VMEM((rows, width), BF16),
-            pltpu.VMEM(states, F32),
-            pltpu.VMEM(states, total_type),
-            pltpu.SemaphoreType.DMA((2 * (chips - 1),)),
-            pltpu.SemaphoreType.DMA((chips + 2, groups)),
-            pltpu.SemaphoreType.DMA((3, groups)),
-        ],
-        28,
+        functools.partial(last_body, blk_count - 1),
+        "last_product",
+        [(before, VMEM), (near, VMEM), (queries, VMEM), (cum, VMEM), (prior, SMEM), (weight, VMEM)]
+        + [(piece, VMEM) for piece in pieces],
+        [((rows, width), BF16, HBM), (states, F32, HBM), (states, BF16, VMEM)],
+        [pltpu.VMEM((rows, width), BF16), pltpu.VMEM(states, F32), pltpu.SemaphoreType.DMA((2, groups))],
+        8,
         cost(
-            2 * rows * width * (2 * (chips - 1) * depth + HD),
-            4 * (chips - 1) * depth * (rows + width) + 8 * rows * width + 12 * width * HD,
+            2 * rows * width * (len(pieces) * depth + HD),
+            2 * len(pieces) * depth * (rows + width) + 8 * rows * width + 12 * width * HD,
         ),
     )
 
 
-def block_body(blk, q_hbm, k_hbm, v_hbm, grad_hbm, cum_ref, prior_ref, local_hbm, enter_hbm, *refs):
+def block_body(blk, grad_blk, q_hbm, k_hbm, v_hbm, grad_hbm, cum_ref, prior_ref, local_hbm, enter_hbm, *refs):
     refs = refs[1:] if blk else refs
     gq_hbm, gk_hbm, gv_hbm, q_ref, k_ref, v_ref, grad_ref, local_ref, enter_ref = refs[:9]
     gq_ref, gk_ref, gv_ref, load_sems, store_sems = refs[9:]
@@ -325,7 +423,7 @@
     def loads(g):
         lanes, these = lanes_of(g, wide), pl.ds(g * group, group)
         return (
-            copy_of(grad_hbm.at[:, lanes], grad_ref.at[:, lanes], load_sems.at[0, g]),
+            copy_of(grad_hbm.at[pl.ds(grad_blk * BLK, BLK), lanes], grad_ref.at[:, lanes], load_sems.at[0, g]),
             copy_of(v_hbm.at[block, lanes], v_ref.at[:, lanes], load_sems.at[1, g]),
             copy_of(q_hbm.at[block, lanes], q_ref.at[:, lanes], load_sems.at[2, g]),
             copy_of(k_hbm.at[block, lanes], k_ref.at[:, lanes], load_sems.at[3, g]),
@@ -384,20 +482,20 @@
             copy.wait()
 
 
-def block_terms(blk, queries, keys, values, grad, cum, prior, local_enter, enter, gq):
+def block_terms(blk, grad_blk, queries, keys, values, grad, cum, prior, local_enter, enter, gq):
     rows, width = queries.shape
     heads, groups = width // HD, cum.shape[1]
     tile = pltpu.VMEM((BLK, width), BF16)
-    part = ((BLK, width), BF16, ANY)
+    part = ((BLK, width), BF16, HBM)
     ins = [queries, keys, values, grad, cum, prior, local_enter, enter]
-    specs = [ANY, ANY, ANY, ANY, VMEM, SMEM, ANY, ANY]
+    specs = [HBM, HBM, HBM, HBM, VMEM, SMEM, HBM, HBM]
     if blk:
-        ins, specs = ins + [gq], specs + [ANY]
+        ins, specs = ins + [gq], specs + [HBM]
     return call(
-        functools.partial(block_body, blk),
+        functools.partial(block_body, blk, grad_blk),
         "block_terms",
         list(zip(ins, specs)),
-        [((rows, width), BF16, ANY), part, part],
+        [((rows, width), BF16, HBM), part, part],
         [tile] * 4
         + [pltpu.VMEM((heads, HD, HD), F32), pltpu.VMEM((heads, HD, HD), BF16)]
         + [tile] * 3
@@ -493,12 +591,12 @@
     rows, width = keys.shape
     heads, blk_count = width // HD, rows // BLK
     whole = pltpu.VMEM((rows, width), BF16)
-    out = ((rows, width), BF16, ANY)
+    out = ((rows, width), BF16, HBM)
     return call(
         later_body,
         "later_terms",
-        [(keys, ANY), (values, ANY), (cum, VMEM), (enter, ANY)]
-        + [(x, ANY) for x in gk_parts + gv_parts + sums],
+        [(keys, HBM), (values, HBM), (cum, VMEM), (enter, HBM)]
+        + [(x, HBM) for x in gk_parts + gv_parts + sums],
         [out, out],
         [whole] * 4
         + [
@@ -514,7 +612,7 @@
 
 
 def chain_body(reverse, got_ref, weight_ref, out_ref):
-    devices, share = got_ref.shape[0], got_ref.shape[1]
+    devices, share = out_ref.shape[0], out_ref.shape[1]
     pieces = weight_ref.shape[1]
     part = share // pieces
     for p in range(pieces):
@@ -525,8 +623,8 @@
             carry = weight_ref[place, p] * carry + got_ref[place, rows].astype(F32)
 
 
-def chain(got, weights, reverse):
-    devices, share, _ = got.shape
+def chain(got, weights, share, reverse):
+    devices = got.shape[0]
     (out,) = call(
         functools.partial(chain_body, reverse),
         "chain_states",
@@ -562,59 +660,78 @@
 
     own = grad_output
     sibling = lax.ppermute(own, "tp", core)
-    first = []
-    for j in range(blk_count):
-        piece = own[j * BLK : (j + 1) * BLK]
-        first.append([lax.ppermute(piece, "tp", from_chip(d)) for d in range(1, chips)])
-
-    cum = jnp.cumsum(log_decay.reshape(heads, blk_count, BLK), axis=2)
+    starts = [0, blk_count - 2, blk_count - 1, blk_count]
+    cuts, rest = [], own
+    for a, b in zip(starts, starts[1:]):
+        cuts.append(rest[a * BLK : b * BLK])
+        rest = after(own, cuts[0])
+    first = [[lax.ppermute(x, "tp", from_chip(d)) for d in range(1, chips)] for x in cuts]
+
+    def hand_on(j, *earlier):
+        arrived = []
+        for x in first[j]:
+            x = after(x, *earlier)
+            arrived += [x, lax.ppermute(x, "tp", core)]
+        return arrived
+
+    cum = jnp.cumsum(after(log_decay, *cuts).reshape(heads, blk_count, BLK), axis=2)
     end = cum[:, :, -1]
     prior = jnp.exp(jnp.cumsum(end, axis=1) - end)
     cum = cum.transpose(1, 0, 2).reshape(blk_count, heads // GROUP, GROUP, BLK)
-
-    own_span = jnp.broadcast_to(jnp.sum(end, axis=1)[None], (seq, heads))
-    spans = lax.all_to_all(own_span, "seq", 0, 0, tiled=True)
+    own_span = jnp.pad(jnp.sum(end, axis=1), (0, HD - heads))[None]
+
+    local_enter, fwd_total = key_totals(key_vectors, value_vectors, cum, own_span, seq)
+    fwd_got = swap(fwd_total)
+
+    near = near_product(own, sibling, out_weight)
+    fwd_got = after(fwd_got, near)
+
     share = heads * HD // seq
     pieces = max(share // HD, 1)
+    spans = jnp.sum(fwd_got[:, share : share + 3, :heads].astype(F32), axis=1)
     mine = lax.dynamic_slice_in_dim(jnp.exp(spans), place * share // HD, pieces, axis=1)
-
-    local_enter, fwd_total = key_totals(key_vectors, value_vectors, cum)
-    fwd_got = swap(fwd_total)
-
-    near = near_product(own, sibling, out_weight)
-    fwd_out = chain(after(fwd_got, near), mine, False)
+    fwd_out = chain(fwd_got, mine, share, False)
     enter_fwd = swap(fwd_out).reshape(heads, HD, HD)
 
-    total = near
-    held = [near, fwd_out, enter_fwd]
-    grads, sums = [], []
-    for j in range(blk_count):
-        wait_for = [total] + ([fwd_out] if j == 1 else []) + ([enter_fwd] if j == 2 else [])
-        arrived = []
-        for x in first[j]:
-            x = after(x, *wait_for)
-            arrived += [x, lax.ppermute(x, "tp", core)]
-        before = total if j else jnp.zeros((heads, HD, HD), F32)
-        grad, part, total = far_product(
-            j, j == blk_count - 1, before, arrived, out_weight, near, queries, cum, prior
-        )
-        grads.append(grad)
-        sums.append(part)
+    arrived = hand_on(0, near, fwd_out)
+    total = jnp.zeros((heads, HD, HD), F32)
+    early_grad, total, *sums = far_product(
+        0, False, total, arrived, out_weight, near, queries, cum, prior
+    )
+    arrived = hand_on(1, early_grad)
+    next_grad, total, next_sums, far_weight, last_near, last_queries = far_product(
+        starts[1], True, total, arrived, out_weight, near, queries, after(cum, enter_fwd), prior
+    )
+    arrived = hand_on(2, next_grad)
+    last_grad, last_sums, total = last_product(
+        total, arrived, far_weight, last_near, last_queries, cum, prior
+    )
+    sums += [next_sums, last_sums]
+    grads = [(j, early_grad) for j in range(starts[1])] + [(0, next_grad), (0, last_grad)]
+    gq, parts = None, []
 
     bwd_got = swap(total)
-    gq, gk_parts, gv_parts = None, [], []
-    half = blk_count // 2
     cum_now = after(cum, total)
     for j in range(blk_count):
-        if j == half:
-            bwd_out = chain(after(bwd_got, gq), mine, True)
+        if j == blk_count // 2:
+            bwd_out = chain(after(bwd_got, gq), mine, share, True)
             enter_bwd = swap(bwd_out).reshape(heads, HD, HD)
             cum_now = after(cum, bwd_out)
-        gq, gk, gv = block_terms(
-            j, queries, key_vectors, value_vectors, grads[j], cum_now, prior, local_enter, enter_fwd, gq
+        gq, *part = block_terms(
+            j,
+            grads[j][0],
+            queries,
+            key_vectors,
+            value_vectors,
+            grads[j][1],
+            cum_now,
+            prior,
+            local_enter,
+            enter_fwd,
+            gq,
         )
-        gk_parts.append(gk)
-        gv_parts.append(gv)
+        parts.append(part)
+    gk_parts, gv_parts = [list(x) for x in zip(*parts)]
     gk, gv = later_terms(key_vectors, value_vectors, gk_parts, gv_parts, sums[1:], cum, enter_bwd)
     return gq, gk, gv
 

time: 250 us -> 160 us (0.64)
  local copies, waits for them, and re-layouts: 89.8 us -> 5.73 us
  starting transfers between devices: 35.5 us -> 28.8 us
  waiting for transfers between devices: 5.04 us -> 11.5 us
  Pallas kernels: 114 us -> 110 us
    unnamed x116 -> x6, local copies, waits for them, and re-layouts: 84.4 us -> 0.81 us
    all_to_all x1 -> x0, starting transfers between devices: 6.82 us -> none  [local(): spans = lax.all_to_all(own_span, 'seq', 0, 0, tiled=True)]
    ppermute x8 -> x6, waiting for transfers between devices: 5.02 us -> 11.5 us  [the longest x3 8.2 us: local(): lax.ppermute(x, 'tp', from_chip(d))]
    pallas_call x13 -> x12, Pallas kernels: 114 us -> 110 us  [call(): pl.pallas_call(body, in_specs=[spec for _, spec in ins], out_specs=[spec...]
  transfers between devices with their start and end apart: 14 -> 11, of which waited for: 4 -> 3; matrix products, arithmetic and copies ran while one was open for 3% -> 5% of each run, Pallas kernels for 37% -> 56%
where the time goes in v3:
time: 160 us
  Pallas kernels  110 us (69%)
  starting transfers between devices  28.8 us (18%)
  waiting for transfers between devices  11.5 us (7%)
  local copies, waits for them, and re-layouts  5.73 us (4%)
  other arithmetic  2.74 us (2%)
    pallas_call x12, Pallas kernels, call(): pl.pallas_call(body, in_specs=[spec for _, spec in ins], out_specs=[spec...  110 us
    all_to_all x4, starting transfers between devices, swap(): lax.all_to_all(flat, 'seq', 0, 0, tiled=True).reshape(devices, -1, HD)  23.8 us
    ppermute x3, waiting for transfers between devices, local(): lax.ppermute(x, 'tp', from_chip(d))  8.2 us
    ppermute x3, starting transfers between devices, local(): lax.ppermute(x, 'tp', from_chip(d))  4.41 us
    slice x2, local copies, waits for them, and re-layouts, local(): cuts.append(rest[a * BLK:b * BLK])  4.26 us
    ppermute x3, waiting for transfers between devices, hand_on(): arrived += [x, lax.ppermute(x, 'tp', core)]  3.27 us
  transfers between devices with their start and end apart: 11, of which 3 were waited for; matrix products, arithmetic and copies ran while one was open for 5% of the time, Pallas kernels for 56%

profile of v3, /device:TPU:0, one launch (start us, length us, event | category | flops | bytes accessed | tf_op | source)
XLA Modules:
  0.0 160.0 jit_solution(8300761711818143545)
XLA Ops:
  0.7 0.5 collective-permute-start
  1.2 2.9 %slice.21 = bf16[512,1536]{1,0:T(8,128)(2,1)} slice(bf16[1024,1536]{1,0:T(8,128)(2,1)} %own_hbm.1), slice={[0:512], [0:1536]} | slice | bytes 3145728 | tf_op jit(solution)/shard_map/slice | solution.py:666
  4.1 2.4 %collective-permute-start.1 = (bf16[512,1536]{1,0:T(8,128)(2,1)}, bf16[512,1536]{1,0:T(8,128)(2,1)S(1)}, u32[]{:S(2)}, u32[]{:S(2)}) collective-permute-start(bf16[512,1536]{1,0:T(8,128)(2,1)} %slice.21), channel_id=1, source_target_pairs={{0,2},{1,3},{2,0},{3,1},{4,6},{5,7},{6,4},{7,5},{8,10},{9,11},{10,... | collective-permute-start | bytes 4718600 | tf_op jit(solution)/shard_map/ppermute | solution.py:668
  6.5 1.3 fusion.1
  7.9 2.3 %reduce-window.6 = f32[16,4,2,128]{3,0,1,2:T(8,128)S(1)} reduce-window(f32[16,4,2,128]{3,0,1,2:T(8,128)S(1)} %copy.20, f32[]{:T(128)} %constant.27.clone.1), window={size=1x1x1x128 pad=0_0x0_0x0_0x127_0}, to_apply=%region_0.0 | reduce-window | flops 2080768 | bytes 131076 | tf_op jit(solution)/shard_map/reduce-window
  10.2 0.2 slice_reduce_fusion
  10.6 0.2 slice_reduce_fusion.1
  10.7 7.3 %key_totals.1 = (f32[4,16,128,128]{3,2,1,0:T(8,128)}, bf16[8,272,128]{2,1,0:T(8,128)(2,1)}) custom-call(bf16[1024,2048]{1,0:T(8,128)(2,1)} %k_hbm.11, bf16[1024,2048]{1,0:T(8,128)(2,1)} %v_hbm.11, f32[4,4,4,256]{3,2,1,0:T(4,128)S(1)} %reshape.45.cum_ref, f32[1,128]{1,0:T(1,128)S(1)} %pad_bitcast_fusion.span_ref), custom_call_target="tpu_custom_call" | custom-call | flops 536870912 | bytes 12582912 | tf_op jit(solution)/shard_map/key_totals/pallas_call | solution.py:41
  18.0 5.8 %all-to-all-start = ((bf16[8,272,128]{2,1,0:T(8,128)(2,1)}), bf16[8,272,128]{2,1,0:T(8,128)(2,1)S(1)}, u32[]{:S(2)}, u32[]{:S(2)}) async-start(bf16[8,272,128]{2,1,0:T(8,128)(2,1)} %get-tuple-element.43), calls=%async_computation | async-start | bytes 1114112 | tf_op jit(solution)/shard_map/all_to_all | solution.py:643
  23.8 20.8 %near_product.1.near_hbm = f32[1024,2048]{1,0:T(8,128)} custom-call(bf16[1024,1536]{1,0:T(8,128)(2,1)} %own_hbm.1, bf16[1024,1536]{1,0:T(8,128)(2,1)} %collective-permute-done.sibling_hbm, bf16[2048,6144]{1,0:T(8,128)(2,1)} %w_hbm.5), custom_call_target="tpu_custom_call" | custom-call | flops 12884901888 | bytes 27262976 | tf_op jit(solution)/shard_map/near_product/pallas_call | solution.py:41
  44.8 1.5 chain_states.2
  46.3 0.5 collective-permute-start.3
  46.8 0.2 copy.24
  47.0 0.2 reduce_window_sum.28
  47.1 6.0 %all-to-all-start.1 = ((bf16[8,256,128]{2,1,0:T(8,128)(2,1)}), bf16[8,256,128]{2,1,0:T(8,128)(2,1)}, u32[]{:S(2)}, u32[]{:S(2)}) async-start(bf16[8,256,128]{2,1,0:T(8,128)(2,1)} %chain_states.2), calls=%async_computation.1 | async-start | bytes 1048576 | tf_op jit(solution)/shard_map/all_to_all | solution.py:643
  53.1 0.1 broadcast_in_dim.6.before_ref
  53.2 17.0 %far_product.2 = (bf16[512,2048]{1,0:T(8,128)(2,1)}, f32[16,128,128]{2,1,0:T(8,128)S(1)}, f32[16,128,128]{2,1,0:T(8,128)}, f32[16,128,128]{2,1,0:T(8,128)}) custom-call(f32[16,128,128]{2,1,0:T(8,128)S(1)} %broadcast_in_dim.6.before_ref, f32[1024,2048]{1,0:T(8,128)} %near_product.1.near_hbm, bf16[1024,2048]{1,0:T(8,128)(2,1)} %q_hbm.11, ...), custom_call_target="tpu_custom_call" | custom-call | flops 6710886400 | bytes 27262976 | tf_op jit(solution)/shard_map/far_product/pallas_call | solution.py:41
  70.4 1.5 collective-permute-start.5
  71.9 1.0 collective-permute-done.4.refs_1_
  72.8 9.5 %far_product.3 = (bf16[256,2048]{1,0:T(8,128)(2,1)}, f32[16,128,128]{2,1,0:T(8,128)S(1)}, f32[16,128,128]{2,1,0:T(8,128)}, bf16[2048,3072]{1,0:T(8,128)(2,1)S(1)...) custom-call(f32[16,128,128]{2,1,0:T(8,128)S(1)} %get-tuple-element.46.before_ref, ...), custom_call_target="tpu_custom_call" | custom-call | flops 3355443200 | bytes 21495808 | tf_op jit(solution)/shard_map/far_product/pallas_call | solution.py:41
  82.3 8.2 %collective-permute-done.5.refs_0_ = bf16[256,1536]{1,0:T(8,128)(2,1)S(1)} collective-permute-done((bf16[256,1536]{1,0:T(8,128)(2,1)}, bf16[256,1536]{1,0:T(8,128)(2,1)S(1)}, u32[]{:S(2)}, u32[]{:S(2)}) %collective-permute-start.5) | collective-permute-done | bytes 786464 | tf_op jit(solution)/shard_map/ppermute | solution.py:668
  90.5 2.3 %collective-permute-done.6.refs_1_ = bf16[256,1536]{1,0:T(8,128)(2,1)S(1)} collective-permute-done((bf16[256,1536]{1,0:T(8,128)(2,1)S(1)}, bf16[256,1536]{1,0:T(8,128)(2,1)S(1)}, u32[]{:S(2)}, u32[]{:S(2)}) %collective-permute-start.6) | collective-permute-done | bytes 786464 | tf_op jit(solution)/shard_map/ppermute | solution.py:674
  92.8 7.2 %last_product.1 = (bf16[256,2048]{1,0:T(8,128)(2,1)}, f32[16,128,128]{2,1,0:T(8,128)}, bf16[16,128,128]{2,1,0:T(8,128)(2,1)}) custom-call(f32[16,128,128]{2,1,0:T(8,128)S(1)} %get-tuple-element.50.before_ref, f32[256,2048]{1,0:T(8,128)S(1)} %get-tuple-element.51.near_ref, bf16[256,2048]{1,0:T(8,128)(2,1)S(1)} %get-tuple-element.52.q_ref, ...), custom_call_target="tpu_custom_call" | custom-call | flops 3355443200 | bytes 21495808 | tf_op jit(solution)/shard_map/last_product/pallas_call | solution.py:41
  100.0 6.0 %all-to-all-start.2 = ((bf16[8,256,128]{2,1,0:T(8,128)(2,1)}), bf16[8,256,128]{2,1,0:T(8,128)(2,1)S(1)}, u32[]{:S(2)}, u32[]{:S(2)}) async-start(bf16[8,256,128]{2,1,0:T(8,128)(2,1)} %bitcast.4), calls=%async_computation.2 | async-start | bytes 1048576 | tf_op jit(solution)/shard_map/all_to_all | solution.py:643
  106.0 8.3 %block_terms.4 = (bf16[1024,2048]{1,0:T(8,128)(2,1)}, bf16[256,2048]{1,0:T(8,128)(2,1)}, bf16[256,2048]{1,0:T(8,128)(2,1)}) custom-call(bf16[1024,2048]{1,0:T(8,128)(2,1)} %q_hbm.11, bf16[1024,2048]{1,0:T(8,128)(2,1)} %k_hbm.11, bf16[1024,2048]{1,0:T(8,128)(2,1)} %v_hbm.11, bf16[512,2048]{1,0:T(8,128)(2,1)} %get-tuple-element.48.grad_hbm, ...), custom_call_target="tpu_custom_call" | custom-call | flops 1476395008 | bytes 8912896 | tf_op jit(solution)/shard_map/block_terms/pallas_call | solution.py:41
  114.3 8.3 %block_terms.5 = (bf16[1024,2048]{1,0:T(8,128)(2,1)}, bf16[256,2048]{1,0:T(8,128)(2,1)}, bf16[256,2048]{1,0:T(8,128)(2,1)}) custom-call(bf16[1024,2048]{1,0:T(8,128)(2,1)} %q_hbm.11, bf16[1024,2048]{1,0:T(8,128)(2,1)} %k_hbm.11, bf16[1024,2048]{1,0:T(8,128)(2,1)} %v_hbm.11, ...), custom_call_target="tpu_custom_call", output_to_operand_aliasing={{0}: (8, {})} | custom-call | flops 1476395008 | bytes 8912896 | tf_op jit(solution)/shard_map/block_terms/pallas_call | solution.py:41
  122.6 1.5 chain_states.3
  124.1 6.0 %all-to-all-start.3 = ((bf16[8,256,128]{2,1,0:T(8,128)(2,1)}), bf16[8,256,128]{2,1,0:T(8,128)(2,1)S(1)}, u32[]{:S(2)}, u32[]{:S(2)}) async-start(bf16[8,256,128]{2,1,0:T(8,128)(2,1)} %chain_states.3), calls=%async_computation.3 | async-start | bytes 1048576 | tf_op jit(solution)/shard_map/all_to_all | solution.py:643
  130.1 8.3 %block_terms.6 = (bf16[1024,2048]{1,0:T(8,128)(2,1)}, bf16[256,2048]{1,0:T(8,128)(2,1)}, bf16[256,2048]{1,0:T(8,128)(2,1)}) custom-call(bf16[1024,2048]{1,0:T(8,128)(2,1)} %q_hbm.11, bf16[1024,2048]{1,0:T(8,128)(2,1)} %k_hbm.11, bf16[1024,2048]{1,0:T(8,128)(2,1)} %v_hbm.11, ...), custom_call_target="tpu_custom_call", output_to_operand_aliasing={{0}: (8, {})} | custom-call | flops 1476395008 | bytes 8912896 | tf_op jit(solution)/shard_map/block_terms/pallas_call | solution.py:41
  138.4 8.3 %block_terms.7 = (bf16[1024,2048]{1,0:T(8,128)(2,1)}, bf16[256,2048]{1,0:T(8,128)(2,1)}, bf16[256,2048]{1,0:T(8,128)(2,1)}) custom-call(bf16[1024,2048]{1,0:T(8,128)(2,1)} %q_hbm.11, bf16[1024,2048]{1,0:T(8,128)(2,1)} %k_hbm.11, bf16[1024,2048]{1,0:T(8,128)(2,1)} %v_hbm.11, ...), custom_call_target="tpu_custom_call", output_to_operand_aliasing={{0}: (8, {})} | custom-call | flops 1476395008 | bytes 8912896 | tf_op jit(solution)/shard_map/block_terms/pallas_call | solution.py:41
  146.7 0.8 copy-done.1
  147.5 12.3 %later_terms.1 = (bf16[1024,2048]{1,0:T(8,128)(2,1)}, bf16[1024,2048]{1,0:T(8,128)(2,1)}) custom-call(bf16[1024,2048]{1,0:T(8,128)(2,1)} %k_hbm.11, bf16[1024,2048]{1,0:T(8,128)(2,1)} %v_hbm.11, f32[4,4,4,256]{3,2,1,0:T(4,128)S(1)} %reshape.45.cum_ref, bf16[16,128,128]{2,1,0:T(8,128)(2,1)} %bitcast.17, bf16[256,2048]{1,0:T(8,128)(2,1)} %get-tuple-element.66.refs_0_, ...), custom_call_target="tpu_custom_call" | custom-call | flops 1073741824 | bytes 29360128 | tf_op jit(solution)/shard_map/later_terms/pallas_call | solution.py:41
  (27 shorter events, 0.4 us)
Async XLA Ops:
  0.6 5.9 %copy-start = (bf16[1024,1536]{1,0:T(8,128)(2,1)S(1)}, bf16[1024,1536]{1,0:T(8,128)(2,1)}, u32[]{:S(2)}) copy-start(bf16[1024,1536]{1,0:T(8,128)(2,1)} %own_hbm.1) | copy-start | bytes 9437188
  0.6 7.2 %copy-start.2 = (f32[16,1024]{1,0:T(8,128)S(1)}, f32[16,1024]{1,0:T(8,128)}, u32[]{:S(2)}) copy-start(f32[16,1024]{1,0:T(8,128)} %param.9) | copy-start | bytes 196612
  0.7 23.2 %collective-permute-start = (bf16[1024,1536]{1,0:T(8,128)(2,1)}, bf16[1024,1536]{1,0:T(8,128)(2,1)}, u32[]{:S(2)}, u32[]{:S(2)}) collective-permute-start(bf16[1024,1536]{1,0:T(8,128)(2,1)} %own_hbm.1), channel_id=1, source_target_pairs={{0,1},{1,0},{2,3},{3,2},{4,5},{5,4},{6,7},{7,6},{8,9},{9,8},{10,11... | collective-permute-start | bytes 9437192 | tf_op jit(solution)/shard_map/ppermute | solution.py:662
  4.1 42.2 %collective-permute-start.1 = (bf16[512,1536]{1,0:T(8,128)(2,1)}, bf16[512,1536]{1,0:T(8,128)(2,1)S(1)}, u32[]{:S(2)}, u32[]{:S(2)}) collective-permute-start(bf16[512,1536]{1,0:T(8,128)(2,1)} %slice.21), channel_id=1, source_target_pairs={{0,2},{1,3},{2,0},{3,1},{4,6},{5,7},{6,4},{7,5},{8,10},{9,11},{10,... | collective-permute-start | bytes 4718600 | tf_op jit(solution)/shard_map/ppermute | solution.py:668
  18.0 26.6 %all-to-all-start = ((bf16[8,272,128]{2,1,0:T(8,128)(2,1)}), bf16[8,272,128]{2,1,0:T(8,128)(2,1)S(1)}, u32[]{:S(2)}, u32[]{:S(2)}) async-start(bf16[8,272,128]{2,1,0:T(8,128)(2,1)} %get-tuple-element.43), calls=%async_computation | async-start | bytes 1114112 | tf_op jit(solution)/shard_map/all_to_all | solution.py:643
  46.3 6.9 %collective-permute-start.2 = (bf16[512,1536]{1,0:T(8,128)(2,1)S(1)}, bf16[512,1536]{1,0:T(8,128)(2,1)}, u32[]{:S(2)}, u32[]{:S(2)}) collective-permute-start(bf16[512,1536]{1,0:T(8,128)(2,1)S(1)} %collective-permute-done.1.refs_0_), channel_id=1, source_target_pairs={{0,1},{1,0},{2,3},{3,2},{4,5},{5,4},{6,7},{7,6},{8,9},{9,8},{10,11... | collective-permute-start | bytes 4718600 | tf_op jit(solution)/shard_map/ppermute | solution.py:674
  46.3 24.0 %collective-permute-start.3 = (bf16[256,1536]{1,0:T(8,128)(2,1)}, bf16[256,1536]{1,0:T(8,128)(2,1)}, u32[]{:S(2)}, u32[]{:S(2)}) collective-permute-start(bf16[256,1536]{1,0:T(8,128)(2,1)} %get-tuple-element.80), channel_id=1, source_target_pairs={{0,2},{1,3},{2,0},{3,1},{4,6},{5,7},{6,4},{7,5},{8,10},{9,11},{10,... | collective-permute-start | bytes 2359304 | tf_op jit(solution)/shard_map/ppermute | solution.py:668
  47.1 24.7 %all-to-all-start.1 = ((bf16[8,256,128]{2,1,0:T(8,128)(2,1)}), bf16[8,256,128]{2,1,0:T(8,128)(2,1)}, u32[]{:S(2)}, u32[]{:S(2)}) async-start(bf16[8,256,128]{2,1,0:T(8,128)(2,1)} %chain_states.2), calls=%async_computation.1 | async-start | bytes 1048576 | tf_op jit(solution)/shard_map/all_to_all | solution.py:643
  70.3 2.6 %collective-permute-start.4 = (bf16[256,1536]{1,0:T(8,128)(2,1)}, bf16[256,1536]{1,0:T(8,128)(2,1)S(1)}, u32[]{:S(2)}, u32[]{:S(2)}) collective-permute-start(bf16[256,1536]{1,0:T(8,128)(2,1)} %collective-permute-done.3.refs_0_), channel_id=1, source_target_pairs={{0,1},{1,0},{2,3},{3,2},{4,5},{5,4},{6,7},{7,6},{8,9},{9,8},{10,11... | collective-permute-start | bytes 2359304 | tf_op jit(solution)/shard_map/ppermute | solution.py:674
  70.4 20.2 %collective-permute-start.5 = (bf16[256,1536]{1,0:T(8,128)(2,1)}, bf16[256,1536]{1,0:T(8,128)(2,1)S(1)}, u32[]{:S(2)}, u32[]{:S(2)}) collective-permute-start(bf16[256,1536]{1,0:T(8,128)(2,1)} %get-tuple-element.79), channel_id=1, source_target_pairs={{0,2},{1,3},{2,0},{3,1},{4,6},{5,7},{6,4},{7,5},{8,10},{9,11},{10,... | collective-permute-start | bytes 2359304 | tf_op jit(solution)/shard_map/ppermute | solution.py:668
  90.5 2.3 %collective-permute-start.6 = (bf16[256,1536]{1,0:T(8,128)(2,1)S(1)}, bf16[256,1536]{1,0:T(8,128)(2,1)S(1)}, u32[]{:S(2)}, u32[]{:S(2)}) collective-permute-start(bf16[256,1536]{1,0:T(8,128)(2,1)S(1)} %collective-permute-done.5.refs_0_), channel_id=1, source_target_pairs={{0,1},{1,0},{2,3},{3,2},{4,5},{5,4},{6,7},{7,6},{8,9},{9,8},{10,11... | collective-permute-start | bytes 2359304 | tf_op jit(solution)/shard_map/ppermute | solution.py:674
  100.0 22.7 %all-to-all-start.2 = ((bf16[8,256,128]{2,1,0:T(8,128)(2,1)}), bf16[8,256,128]{2,1,0:T(8,128)(2,1)S(1)}, u32[]{:S(2)}, u32[]{:S(2)}) async-start(bf16[8,256,128]{2,1,0:T(8,128)(2,1)} %bitcast.4), calls=%async_computation.2 | async-start | bytes 1048576 | tf_op jit(solution)/shard_map/all_to_all | solution.py:643
  124.1 22.6 %all-to-all-start.3 = ((bf16[8,256,128]{2,1,0:T(8,128)(2,1)}), bf16[8,256,128]{2,1,0:T(8,128)(2,1)S(1)}, u32[]{:S(2)}, u32[]{:S(2)}) async-start(bf16[8,256,128]{2,1,0:T(8,128)(2,1)} %chain_states.3), calls=%async_computation.3 | async-start | bytes 1048576 | tf_op jit(solution)/shard_map/all_to_all | solution.py:643
  146.7 0.8 copy-start.1

commit v4 on v3

v4 whole, which is shorter than its diff:
```python
import functools

import jax
import jax.numpy as jnp
from jax import lax
from jax.experimental import pallas as pl
from jax.experimental.pallas import tpu as pltpu
from jax.sharding import PartitionSpec as P

HD = 128
BLK = 256
GROUP = 4
ROW = 16
MIB = 2**20

NN = (((1,), (0,)), ((), ()))
NT = (((1,), (1,)), ((), ()))
TN = (((0,), (0,)), ((), ()))

ANY = pl.BlockSpec(memory_space=pl.ANY)
HBM = pl.BlockSpec(memory_space=pltpu.HBM)
VMEM = pl.BlockSpec(memory_space=pltpu.VMEM)
SMEM = pl.BlockSpec(memory_space=pltpu.SMEM)
BF16 = jnp.bfloat16
F32 = jnp.float32


def mm(left, right, form):
    return lax.dot_general(left, right, form, preferred_element_type=F32)


def cost(flops, nbytes, exps=0):
    return pl.CostEstimate(flops=int(flops), bytes_accessed=int(nbytes), transcendentals=int(exps))


def span(index, size):
    return slice(index * size, (index + 1) * size)


def call(body, name, ins, outs, scratch, limit, estimate, aliases=None):
    return pl.pallas_call(
        body,
        in_specs=[spec for _, spec in ins],
        out_specs=[spec for _, _, spec in outs],
        out_shape=[
            pltpu.HBM(shape, dtype) if spec is HBM else jax.ShapeDtypeStruct(shape, dtype)
            for shape, dtype, spec in outs
        ],
        scratch_shapes=scratch,
        input_output_aliases=aliases or {},
        compiler_params=pltpu.CompilerParams(vmem_limit_bytes=limit * MIB),
        cost_estimate=estimate,
        name=name,
    )(*[pltpu.with_memory_space_constraint(x, pltpu.HBM) if spec is HBM else x for x, spec in ins])


def copy_of(source, target, sem):
    return pltpu.make_async_copy(source, target, sem)


def lanes_of(index, size):
    return pl.ds(pl.multiple_of(index * size, size), size)


def loop(count, body):
    lax.fori_loop(0, count, lambda i, _: (body(i), 0)[1], 0)


def head_in(h):
    return slice(h * HD, (h + 1) * HD)


def key_body(k_hbm, v_hbm, cum_ref, span_ref, local_hbm, total_ref, k_ref, v_ref, local_ref, load_sems, store_sems):
    blk_count, groups, group, _ = cum_ref.shape
    wide = group * HD

    def loads(j):
        rows = pl.ds(j * BLK, BLK)
        return (
            copy_of(k_hbm.at[rows], k_ref.at[rows], load_sems.at[0, j]),
            copy_of(v_hbm.at[rows], v_ref.at[rows], load_sems.at[1, j]),
        )

    def store(j):
        return copy_of(local_ref.at[j], local_hbm.at[j], store_sems.at[j])

    for j in range(min(2, blk_count)):
        for copy in loads(j):
            copy.start()
    local_ref[0] = jnp.zeros_like(local_ref[0])

    def block(j):
        for copy in loads(j):
            copy.wait()

        @pl.when(j + 2 < blk_count)
        def _():
            for copy in loads(j + 2):
                copy.start()

        store(j).start()
        rows = pl.ds(pl.multiple_of(j * BLK, BLK), BLK)

        def some_heads(g):
            cum = cum_ref[j, g]
            end = cum[:, BLK - 1 : BLK]
            weight = jnp.exp(end - cum)
            end_weight = jnp.exp(end)
            lanes = lanes_of(g, wide)
            these = pl.ds(g * group, group)
            keys, values, entered = k_ref[rows, lanes], v_ref[rows, lanes], local_ref[j, these]
            left = []
            for h in range(group):
                turned = keys[:, head_in(h)].T.astype(F32)
                scaled = (turned * weight[h : h + 1]).astype(BF16)
                sums = mm(scaled, values[:, head_in(h)], NN)
                left.append(entered[h] * end_weight[h : h + 1] + sums)
            local_ref[j + 1, these] = jnp.stack(left)

        loop(groups, some_heads)

    loop(blk_count, block)
    devices, share = total_ref.shape[0], total_ref.shape[1] - ROW
    total_ref[:, :share] = local_ref[blk_count].astype(BF16).reshape(devices, share, HD)
    left, parts = jnp.broadcast_to(span_ref[...], (ROW, HD)), jnp.zeros((ROW, HD), F32)
    at_row = lax.broadcasted_iota(jnp.int32, (ROW, HD), 0)
    for n in range(3):
        rounded = left.astype(BF16).astype(F32)
        parts = jnp.where(at_row == n, rounded, parts)
        left = left - rounded
    for d in range(devices):
        total_ref[d, share:] = parts.astype(BF16)
    for j in range(blk_count):
        store(j).wait()


def key_totals(keys, values, cum, own_span, devices):
    rows, width = keys.shape
    blk_count, heads = cum.shape[0], width // HD
    return call(
        key_body,
        "key_totals",
        [(keys, HBM), (values, HBM), (cum, VMEM), (own_span, VMEM)],
        [
            ((blk_count, heads, HD, HD), F32, HBM),
            ((devices, heads * HD // devices + ROW, HD), BF16, VMEM),
        ],
        [
            pltpu.VMEM((rows, width), BF16),
            pltpu.VMEM((rows, width), BF16),
            pltpu.VMEM((blk_count + 1, heads, HD, HD), F32),
            pltpu.SemaphoreType.DMA((2, blk_count)),
            pltpu.SemaphoreType.DMA((blk_count,)),
        ],
        24,
        cost(2 * rows * width * HD, 4 * rows * width + 4 * blk_count * width * HD),
    )


def near_body(wide, own_hbm, sibling_hbm, w_hbm, out_hbm, grad_ref, w_ref, out_ref, w_sems, grad_sems, out_sems):
    rows, depth = own_hbm.shape
    groups, tiles = w_hbm.shape[0] // wide, rows // BLK
    me = lax.axis_index("tp")
    side = lax.rem(me, 2)
    columns = pl.ds(pl.multiple_of((me - side) * depth, 2 * depth), 2 * depth)

    def w_load(g):
        part = pl.ds(g * wide, wide)
        return copy_of(w_hbm.at[part, columns], w_ref.at[part], w_sems.at[g])

    def grad_loads(r):
        part = pl.ds(r * BLK, BLK)
        return (
            copy_of(own_hbm.at[part], grad_ref.at[part, lanes_of(side, depth)], grad_sems.at[0, r]),
            copy_of(sibling_hbm.at[part], grad_ref.at[part, lanes_of(1 - side, depth)], grad_sems.at[1, r]),
        )

    def store(g):
        return copy_of(out_ref.at[lax.rem(g, 2)], out_hbm.at[:, lanes_of(g, wide)], out_sems.at[lax.rem(g, 2)])

    w_load(0).start()
    for r in range(tiles):
        for copy in grad_loads(r):
            copy.start()

    def first_tile(r):
        for copy in grad_loads(r):
            copy.wait()
        these = pl.ds(pl.multiple_of(r * BLK, BLK), BLK)
        out_ref[0, these] = mm(grad_ref[these], w_ref[:wide], NT)

    def columns_of(before):
        g = before + 1
        w_load(g).wait()

        @pl.when(g + 1 < groups)
        def _():
            w_load(g + 1).start()

        @pl.when(g >= 2)
        def _():
            store(g - 2).wait()

        part = w_ref[pl.ds(pl.multiple_of(g * wide, wide), wide)]
        out_ref[lax.rem(g, 2)] = mm(grad_ref[...], part, NT)
        store(g).start()

    w_load(0).wait()
    if groups > 1:
        w_load(1).start()
    loop(tiles, first_tile)
    store(0).start()
    loop(groups - 1, columns_of)
    for g in range(max(groups - 2, 0), groups):
        store(g).wait()


def near_product(own, sibling, weight):
    rows, depth = own.shape
    width = weight.shape[0]
    wide = GROUP * HD
    (out,) = call(
        functools.partial(near_body, wide),
        "near_product",
        [(own, HBM), (sibling, HBM), (weight, HBM)],
        [((rows, width), F32, HBM)],
        [
            pltpu.VMEM((rows, 2 * depth), BF16),
            pltpu.VMEM((width, 2 * depth), BF16),
            pltpu.VMEM((2, rows, wide), F32),
            pltpu.SemaphoreType.DMA((width // wide,)),
            pltpu.SemaphoreType.DMA((2, rows // BLK)),
            pltpu.SemaphoreType.DMA((2,)),
        ],
        32,
        cost(4 * rows * width * depth, 4 * depth * (rows + width) + 4 * rows * width),
    )
    return out


def far_sums(blks, g, group, q_ref, cum_ref, prior_ref, grad, before_ref, sums_refs, total_ref):
    wide = group * HD
    lanes, these = lanes_of(g, wide), pl.ds(g * group, group)
    chained = None
    if before_ref is not None:
        before = before_ref[these]
        chained = [before[h] for h in range(group)]
    for n, blk in enumerate(blks):
        weight = jnp.exp(cum_ref[blk, g])
        queries = q_ref[span(n, BLK), lanes]
        sums = []
        for h in range(group):
            turned = queries[:, head_in(h)].T.astype(F32)
            scaled = (turned * weight[h : h + 1]).astype(BF16)
            sums.append(mm(scaled, grad[span(n, BLK), head_in(h)], NN))
        sums_refs[n][these] = jnp.stack(sums)
        if chained is None:
            chained = sums
        else:
            chained = [chained[h] + prior_ref[g * group + h, blk] * sums[h] for h in range(group)]
    total_ref[these] = jnp.stack(chained).astype(total_ref.dtype)


def far_grad(near, pieces, w_ref, g, wide, side):
    part = pl.ds(pl.multiple_of(g * wide, wide), wide)
    for n, piece in enumerate(pieces):
        at = 2 * (n // 2) + (side if n % 2 == 0 else 1 - side)
        near += mm(piece[...], w_ref[part, lanes_of(at, piece.shape[1])], NT)
    return near.astype(BF16)


def far_body(chips, blks, direct, *refs):
    count = len(blks)
    if blks[0]:
        before_hbm, refs = refs[0], refs[1:]
    near_hbm, q_hbm, cum_ref, prior_ref, w_hbm, *refs = refs
    pieces, refs = refs[: 2 * (chips - 1)], refs[2 * (chips - 1) :]
    total_ref, grad_hbm, *sums_hbm = refs[: 2 + count]
    refs = refs[2 + count :]
    if direct:
        held = pieces
    else:
        held, refs = refs[: len(pieces)], refs[len(pieces) :]
    w_ref, near_ref, q_ref, grad_ref, before_ref, sums_ref, piece_sems, load_sems, store_sems = refs
    rows, depth = pieces[0].shape
    _, groups, group, _ = cum_ref.shape
    wide = group * HD
    me = lax.axis_index("tp")
    side = lax.rem(me, 2)
    chip = lax.div(me, 2)
    here = pl.ds(blks[0] * BLK, rows)

    def loads(g):
        part, lanes, these = pl.ds(g * wide, wide), lanes_of(g, wide), pl.ds(g * group, group)
        found = []
        for d in range(1, chips):
            owner = lax.rem(chip + chips - d, chips)
            columns = pl.ds((d - 1) * 2 * depth, 2 * depth)
            found.append(
                copy_of(w_hbm.at[part, lanes_of(owner, 2 * depth)], w_ref.at[part, columns], load_sems.at[d + 2, g])
            )
        found.append(copy_of(near_hbm.at[here, lanes], near_ref.at[:, lanes], load_sems.at[0, g]))
        found.append(copy_of(q_hbm.at[here, lanes], q_ref.at[:, lanes], load_sems.at[1, g]))
        if blks[0]:
            found.append(copy_of(before_hbm.at[these], before_ref.at[these], load_sems.at[2, g]))
        return found

    def piece_loads():
        if direct:
            return ()
        return [copy_of(piece, held[n], piece_sems.at[n]) for n, piece in enumerate(pieces)]

    def store(g):
        lanes = lanes_of(g, wide)
        return copy_of(grad_ref.at[:, lanes], grad_hbm.at[:, lanes], store_sems.at[count, g])

    def sums_stores(g):
        these = pl.ds(g * group, group)
        return [copy_of(sums_ref.at[n, these], sums_hbm[n].at[these], store_sems.at[n, g]) for n in range(count)]

    def product(g):
        for copy in loads(g):
            copy.wait()
        return far_grad(near_ref[:, lanes_of(g, wide)], held, w_ref, g, wide, side)

    def sums_of(g, grad):
        far_sums(
            blks, g, group, q_ref, cum_ref, prior_ref, grad, before_ref if blks[0] else None,
            [sums_ref.at[n] for n in range(count)], total_ref,
        )

    for copy in loads(0):
        copy.start()
    for copy in piece_loads():
        copy.start()
    for copy in loads(1):
        copy.start()
    for copy in piece_loads():
        copy.wait()
    grad_ref[:, :wide] = product(0)
    store(0).start()

    def step(g):
        @pl.when(g + 2 < groups)
        def _():
            for copy in loads(g + 2):
                copy.start()

        mine = grad_ref[:, lanes_of(g, wide)]
        grad = product(g + 1)
        sums_of(g, mine)
        grad_ref[:, lanes_of(g + 1, wide)] = grad
        store(g + 1).start()
        for copy in sums_stores(g):
            copy.start()

    loop(groups - 1, step)
    sums_of(groups - 1, grad_ref[:, lanes_of(groups - 1, wide)])
    for copy in sums_stores(groups - 1):
        copy.start()
    for g in range(groups):
        store(g).wait()
        for copy in sums_stores(g):
            copy.wait()


def far_product(start, before, pieces, weight, near, queries, cum, prior):
    rows, depth = pieces[0].shape
    blk_count, groups, group, _ = cum.shape
    heads = groups * group
    width = heads * HD
    chips = len(pieces) // 2 + 1
    count = rows // BLK
    blks = list(range(start, start + count))
    last = start + count == blk_count
    states = (heads, HD, HD)
    far_depth = 2 * (chips - 1) * depth
    total, grad, *sums = call(
        functools.partial(far_body, chips, blks, last),
        "far_product",
        ([(before, HBM)] if start else [])
        + [(near, HBM), (queries, HBM), (cum, VMEM), (prior, SMEM), (weight, HBM)]
        + [(piece, VMEM if last else HBM) for piece in pieces],
        [(states, BF16 if last else F32, VMEM), ((rows, width), BF16, HBM)] + [(states, F32, HBM)] * count,
        ([] if last else [pltpu.VMEM(piece.shape, BF16) for piece in pieces])
        + [
            pltpu.VMEM((width, far_depth), BF16),
            pltpu.VMEM((rows, width), F32),
            pltpu.VMEM((rows, width), BF16),
            pltpu.VMEM((rows, width), BF16),
            pltpu.VMEM(states, F32),
            pltpu.VMEM((count, *states), F32),
            pltpu.SemaphoreType.DMA((len(pieces),)),
            pltpu.SemaphoreType.DMA((chips + 2, groups)),
            pltpu.SemaphoreType.DMA((count + 1, groups)),
        ],
        36,
        cost(
            2 * rows * width * (far_depth + HD),
            2 * far_depth * (rows + width) + 8 * rows * width + 12 * width * HD,
        ),
    )
    return grad, sums, total


def block_body(blks, grad_blks, q_hbm, k_hbm, v_hbm, grads_hbm, cum_ref, prior_ref, local_hbm, enter_ref, *refs):
    count = len(blks)
    gq_hbm, gk_hbm, gv_hbm, q_ref, k_ref, v_ref, grad_ref, local_ref, gq_ref, gk_ref, gv_ref = refs[-13:-2]
    load_sems, store_sems = refs[-2:]
    _, groups, group, _ = cum_ref.shape
    wide = group * HD

    def loads(n, g):
        lanes, these = lanes_of(g, wide), pl.ds(g * group, group)
        block = pl.ds((blks[0] + n) * BLK, BLK)
        return (
            copy_of(v_hbm.at[block, lanes], v_ref.at[n, :, lanes], load_sems.at[0, n, g]),
            copy_of(q_hbm.at[block, lanes], q_ref.at[n, :, lanes], load_sems.at[1, n, g]),
            copy_of(k_hbm.at[block, lanes], k_ref.at[n, :, lanes], load_sems.at[2, n, g]),
            copy_of(local_hbm.at[blks[0] + n, these], local_ref.at[n, these], load_sems.at[3, n, g]),
        )

    def grad_load(n, g, source=0):
        lanes = lanes_of(g, wide)
        block = pl.ds(grad_blks[source] * BLK, BLK)
        return copy_of(grads_hbm[source].at[block, lanes], grad_ref.at[n, :, lanes], load_sems.at[4, n, g])

    def stores(n, g):
        lanes = lanes_of(g, wide)
        block, part = pl.ds((blks[0] + n) * BLK, BLK), pl.ds(n * BLK, BLK)
        return (
            copy_of(gq_ref.at[n, :, lanes], gq_hbm.at[block, lanes], store_sems.at[0, n, g]),
            copy_of(gk_ref.at[n, :, lanes], gk_hbm.at[part, lanes], store_sems.at[1, n, g]),
            copy_of(gv_ref.at[n, :, lanes], gv_hbm.at[part, lanes], store_sems.at[2, n, g]),
        )

    def start(n, g):
        grad_load(n, g, n).start()
        for copy in loads(n, g):
            copy.start()

    for g in range(groups):
        start(0, g)
    at_row = lax.broadcasted_iota(jnp.int32, (BLK, BLK), 0)
    at_col = lax.broadcasted_iota(jnp.int32, (BLK, BLK), 1)
    causal, flipped = at_row >= at_col, at_row <= at_col

    def some_heads(at):
        n, g = lax.div(at, groups), lax.rem(at, groups)
        blk = blks[0] + n
        for m in range(1, count):

            @pl.when(n == m - 1)
            def _(m=m):
                start(m, g)

        grad_load(n, g).wait()
        for copy in loads(n, g):
            copy.wait()
        rows = cum_ref[blk, g]
        cum = rows.T
        head_weight = jnp.exp(cum)
        lanes, these = lanes_of(g, wide), pl.ds(g * group, group)
        queries, keys, values, grads = (ref[n, :, lanes] for ref in (q_ref, k_ref, v_ref, grad_ref))
        entered, here = enter_ref[these], local_ref[n, these]
        gq, gk, gv = [], [], []
        for h in range(group):
            head = head_in(h)
            q, k, v, grad = queries[:, head], keys[:, head], values[:, head], grads[:, head]
            by_row, by_col = cum[:, h : h + 1], rows[h : h + 1, :]
            mask = jnp.exp(jnp.where(causal, by_row - by_col, -1e30))
            turned = jnp.exp(jnp.where(flipped, by_col - by_row, -1e30))
            scores = (mm(grad, v, NT) * mask).astype(BF16)
            turned_scores = (mm(v, grad, NT) * turned).astype(BF16)
            turned_attn = (mm(k, q, NT) * turned).astype(BF16)
            enter = entered[h].astype(F32) * prior_ref[g * group + h, blk] + here[h]
            inter = mm(grad, enter.astype(BF16), NT) * head_weight[:, h : h + 1]
            gq.append((mm(scores, k, NN) + inter).astype(BF16))
            gk.append(mm(turned_scores, q, NN).astype(BF16))
            gv.append(mm(turned_attn, grad, NN).astype(BF16))
        gq_ref[n, :, lanes] = jnp.concatenate(gq, axis=1)
        gk_ref[n, :, lanes] = jnp.concatenate(gk, axis=1)
        gv_ref[n, :, lanes] = jnp.concatenate(gv, axis=1)
        for copy in stores(n, g):
            copy.start()

    loop(count * groups, some_heads)
    for n in range(count):
        for g in range(groups):
            for copy in stores(n, g):
                copy.wait()


def block_terms(blks, queries, keys, values, grads, cum, prior, local_enter, enter, gq):
    rows, width = queries.shape
    heads, groups, count = width // HD, cum.shape[1], len(blks)
    tile = pltpu.VMEM((count, BLK, width), BF16)
    part = ((count * BLK, width), BF16, HBM)
    ins = [(queries, HBM), (keys, HBM), (values, HBM)] + [(grad, HBM) for _, grad in grads]
    ins += [(cum, VMEM), (prior, SMEM), (local_enter, HBM), (enter, VMEM)]
    if gq is not None:
        ins.append((gq, HBM))

    def body(q_hbm, k_hbm, v_hbm, *refs):
        block_body(blks, [at for at, _ in grads], q_hbm, k_hbm, v_hbm, refs[:count], *refs[count:])

    return call(
        body,
        "block_terms",
        ins,
        [((rows, width), BF16, HBM), part, part],
        [tile] * 4
        + [pltpu.VMEM((count, heads, HD, HD), F32)]
        + [tile] * 3
        + [pltpu.SemaphoreType.DMA((5, count, groups)), pltpu.SemaphoreType.DMA((3, count, groups))],
        28,
        cost(
            count * BLK * width * (10 * BLK + 2 * HD),
            count * (14 * BLK * width + 6 * width * HD),
            count * BLK * heads * BLK,
        ),
        {len(ins) - 1: 0} if gq is not None else None,
    )


def later_body(k_hbm, v_hbm, cum_ref, enter_hbm, *refs):
    blk_count, groups, group, _ = cum_ref.shape
    halves = len(refs) - 11 - (blk_count - 1)
    gk_parts, gv_parts = refs[: halves // 2], refs[halves // 2 : halves]
    each = blk_count // len(gk_parts)
    sums_hbm = refs[halves : halves + blk_count - 1]
    gk_hbm, gv_hbm, k_ref, v_ref, gk_ref, gv_ref, sums_ref, enter_ref, carry_ref = refs[halves + blk_count - 1 : -2]
    load_sems, store_sems = refs[-2:]
    wide = group * HD

    def loads(j, g):
        rows, lanes, these = pl.ds(j * BLK, BLK), lanes_of(g, wide), pl.ds(g * group, group)
        part = pl.ds(j % each * BLK, BLK)
        found = [
            copy_of(v_hbm.at[rows, lanes], v_ref.at[rows, lanes], load_sems.at[0, j, g]),
            copy_of(k_hbm.at[rows, lanes], k_ref.at[rows, lanes], load_sems.at[1, j, g]),
            copy_of(gk_parts[j // each].at[part, lanes], gk_ref.at[rows, lanes], load_sems.at[2, j, g]),
            copy_of(gv_parts[j // each].at[part, lanes], gv_ref.at[rows, lanes], load_sems.at[3, j, g]),
        ]
        if j:
            found.append(copy_of(sums_hbm[j - 1].at[these], sums_ref.at[j, these], load_sems.at[4, j, g]))
        return found

    def stores(j, g):
        rows, lanes = pl.ds(j * BLK, BLK), lanes_of(g, wide)
        return (
            copy_of(gk_ref.at[rows, lanes], gk_hbm.at[rows, lanes], store_sems.at[0, j, g]),
            copy_of(gv_ref.at[rows, lanes], gv_hbm.at[rows, lanes], store_sems.at[1, j, g]),
        )

    enter_load = copy_of(enter_hbm, enter_ref, load_sems.at[4, 0, 0])
    enter_load.start()
    for g in range(groups):
        for copy in loads(blk_count - 1, g):
            copy.start()
    enter_load.wait()
    for j in reversed(range(blk_count)):

        def some_heads(g, j=j):
            if j:
                for copy in loads(j - 1, g):
                    copy.start()
            for copy in loads(j, g):
                copy.wait()
            rows = span(j, BLK)
            cum = cum_ref[j, g].T
            end = cum[BLK - 1 : BLK, :]
            weight = jnp.exp(end - cum)
            end_weight = jnp.exp(end)
            lanes, these = lanes_of(g, wide), pl.ds(g * group, group)
            keys, values = k_ref[rows, lanes], v_ref[rows, lanes]
            gk_in, gv_in = gk_ref[rows, lanes], gv_ref[rows, lanes]
            entered = enter_ref[these].astype(F32) if j + 1 == blk_count else carry_ref[these]
            here = sums_ref[j, these] if j else None
            gk, gv, left = [], [], []
            for h in range(group):
                head, tail = head_in(h), weight[:, h : h + 1]
                enter = entered[h].astype(BF16)
                gk.append((gk_in[:, head].astype(F32) + mm(values[:, head], enter, NT) * tail).astype(BF16))
                gv.append((gv_in[:, head].astype(F32) + mm(keys[:, head], enter, NN) * tail).astype(BF16))
                if j:
                    left.append(entered[h] * end_weight[:, h : h + 1] + here[h])
            gk_ref[rows, lanes] = jnp.concatenate(gk, axis=1)
            gv_ref[rows, lanes] = jnp.concatenate(gv, axis=1)
            if j:
                carry_ref[these] = jnp.stack(left)
            for copy in stores(j, g):
                copy.start()

        loop(groups, some_heads)
    for j in range(blk_count):
        for g in range(groups):
            for copy in stores(j, g):
                copy.wait()


def later_terms(keys, values, gk_parts, gv_parts, sums, cum, enter):
    rows, width = keys.shape
    heads, blk_count = width // HD, rows // BLK
    whole = pltpu.VMEM((rows, width), BF16)
    out = ((rows, width), BF16, HBM)
    return call(
        later_body,
        "later_terms",
        [(keys, HBM), (values, HBM), (cum, VMEM), (enter, HBM)]
        + [(x, HBM) for x in gk_parts + gv_parts + sums],
        [out, out],
        [whole] * 4
        + [
            pltpu.VMEM((blk_count, heads, HD, HD), F32),
            pltpu.VMEM((heads, HD, HD), BF16),
            pltpu.VMEM((heads, HD, HD), F32),
            pltpu.SemaphoreType.DMA((5, blk_count, cum.shape[1])),
            pltpu.SemaphoreType.DMA((2, blk_count, cum.shape[1])),
        ],
        28,
        cost(rows * width * 4 * HD, 12 * rows * width + 4 * blk_count * width * HD),
    )


def chain_body(reverse, got_ref, weight_ref, out_ref):
    devices, share = out_ref.shape[0], out_ref.shape[1]
    pieces = weight_ref.shape[1]
    part = share // pieces
    for p in range(pieces):
        rows = span(p, part)
        carry = jnp.zeros((part, HD), F32)
        for place in reversed(range(devices)) if reverse else range(devices):
            out_ref[place, rows] = carry.astype(BF16)
            carry = weight_ref[place, p] * carry + got_ref[place, rows].astype(F32)


def chain(got, weights, share, reverse):
    devices = got.shape[0]
    (out,) = call(
        functools.partial(chain_body, reverse),
        "chain_states",
        [(got, VMEM), (weights, SMEM)],
        [((devices, share, HD), BF16, VMEM)],
        [],
        16,
        cost(2 * devices * share * HD, 4 * devices * share * HD),
    )
    return out


def swap(x):
    devices = lax.axis_size("seq")
    flat = x.reshape(-1, HD)
    return lax.all_to_all(flat, "seq", 0, 0, tiled=True).reshape(devices, -1, HD)


def after(x, *earlier):
    return lax.optimization_barrier((x, *earlier))[0]


def local(queries, key_vectors, value_vectors, log_decay, grad_output, out_weight):
    rows, width = queries.shape
    heads, blk_count = width // HD, rows // BLK
    tp, me = lax.axis_size("tp"), lax.axis_index("tp")
    seq, place = lax.axis_size("seq"), lax.axis_index("seq")
    chips = tp // 2
    core = [(i, i ^ 1) for i in range(tp)]

    def from_chip(hops):
        return [(i, (i + 2 * hops) % tp) for i in range(tp)]

    own = grad_output
    sibling = lax.ppermute(own, "tp", core)
    starts = [0, 1, blk_count - 1, blk_count]
    cuts, rest = [], own
    for a, b in zip(starts, starts[1:]):
        cuts.append(rest[a * BLK : b * BLK])
        rest = after(own, cuts[0])
    first = [[lax.ppermute(x, "tp", from_chip(d)) for d in range(1, chips)] for x in cuts]

    def hand_on(j, *earlier):
        arrived = []
        for x in first[j]:
            x = after(x, *earlier)
            arrived += [x, lax.ppermute(x, "tp", core)]
        return arrived

    cum = jnp.cumsum(after(log_decay, *cuts).reshape(heads, blk_count, BLK), axis=2)
    end = cum[:, :, -1]
    prior = jnp.exp(jnp.cumsum(end, axis=1) - end)
    cum = cum.transpose(1, 0, 2).reshape(blk_count, heads // GROUP, GROUP, BLK)
    own_span = jnp.pad(jnp.sum(end, axis=1), (0, HD - heads))[None]

    local_enter, fwd_total = key_totals(key_vectors, value_vectors, cum, own_span, seq)
    fwd_got = swap(fwd_total)

    arrived = hand_on(0, fwd_total)
    near = near_product(own, after(sibling, arrived[0]), out_weight)
    fwd_got = after(fwd_got, near)

    share = heads * HD // seq
    pieces = max(share // HD, 1)
    spans = jnp.sum(fwd_got[:, share : share + 3, :heads].astype(F32), axis=1)
    mine = lax.dynamic_slice_in_dim(jnp.exp(spans), place * share // HD, pieces, axis=1)
    fwd_out = chain(fwd_got, mine, share, False)
    enter_fwd = swap(fwd_out).reshape(heads, HD, HD)

    grads, sums, total, cum_now = [], [], None, after(cum, fwd_out)
    for part, start in enumerate(starts[:-1]):
        if part:
            arrived = hand_on(part, total)
            cum_now = after(cum, enter_fwd) if part == 2 else cum
        grad, some, total = far_product(start, total, arrived, out_weight, near, queries, cum_now, prior)
        grads += [(j, grad) for j in range(grad.shape[0] // BLK)]
        sums += some
    gq, parts = None, []

    bwd_got = swap(total)
    cum_now = after(cum, total)
    half = blk_count // 2
    for blks in (list(range(half)), list(range(half, blk_count))):
        if blks[0]:
            bwd_out = chain(after(bwd_got, gq), mine, share, True)
            enter_bwd = swap(bwd_out).reshape(heads, HD, HD)
            cum_now = after(cum, bwd_out)
        gq, *part = block_terms(
            blks,
            queries,
            key_vectors,
            value_vectors,
            [grads[j] for j in blks],
            cum_now,
            prior,
            local_enter,
            enter_fwd,
            gq,
        )
        parts.append(part)
    gk_parts, gv_parts = [list(x) for x in zip(*parts)]
    gk, gv = later_terms(key_vectors, value_vectors, gk_parts, gv_parts, sums[1:], cum, enter_bwd)
    return gq, gk, gv


def solution(mesh):
    in_specs = (
        P("seq", "tp"),
        P("seq", "tp"),
        P("seq", "tp"),
        P("tp", "seq"),
        P("seq", "tp"),
        P("tp", None),
    )
    out_specs = (P("seq", "tp"), P("seq", "tp"), P("seq", "tp"))
    return jax.shard_map(local, mesh=mesh, in_specs=in_specs, out_specs=out_specs, check_vma=False)
```

time: 160 us -> 152 us (0.950)
  waiting for transfers between devices: 11.5 us -> 4 us
  Pallas kernels: 110 us -> 106 us
  local copies, waits for them, and re-layouts: 5.73 us -> 9.28 us
    ppermute x3, waiting for transfers between devices: 8.2 us -> 0.01 us  [local(): lax.ppermute(x, 'tp', from_chip(d))]
    pallas_call x12 -> x10, Pallas kernels: 110 us -> 106 us  [call(): pl.pallas_call(body, in_specs=[spec for _, spec in ins], out_specs=[spec...]
    unnamed x6 -> x10, local copies, waits for them, and re-layouts: 0.81 us -> 3.69 us
    all_to_all x4, waiting for transfers between devices: 0.01 us -> 1.71 us  [swap(): lax.all_to_all(flat, 'seq', 0, 0, tiled=True).reshape(devices, -1, HD)]
    slice x2 -> x3, local copies, waits for them, and re-layouts: 4.26 us -> 5.02 us  [local(): cuts.append(rest[a * BLK:b * BLK])]
  transfers between devices with their start and end apart: 11 -> 11, of which waited for: 3 -> 3; matrix products, arithmetic and copies ran while one was open for 5% -> 5% of each run, Pallas kernels for 56% -> 54%
where the time goes in v4:
time: 152 us
  Pallas kernels  106 us (70%)
  starting transfers between devices  28.5 us (19%)
  local copies, waits for them, and re-layouts  9.28 us (6%)
  waiting for transfers between devices  4 us (3%)
  other arithmetic  2.74 us (2%)
    pallas_call x10, Pallas kernels, call(): pl.pallas_call(body, in_specs=[spec for _, spec in ins], out_specs=[spec...  106 us
    all_to_all x4, starting transfers between devices, swap(): lax.all_to_all(flat, 'seq', 0, 0, tiled=True).reshape(devices, -1, HD)  23.2 us
    slice x3, local copies, waits for them, and re-layouts, local(): cuts.append(rest[a * BLK:b * BLK])  5.02 us
    ppermute x3, starting transfers between devices, local(): lax.ppermute(x, 'tp', from_chip(d))  4.24 us
    unnamed x10, local copies, waits for them, and re-layouts  3.69 us
  transfers between devices with their start and end apart: 11, of which 3 were waited for; matrix products, arithmetic and copies ran while one was open for 5% of the time, Pallas kernels for 54%

profile of v4, /device:TPU:0, one launch (start us, length us, event | category | flops | bytes accessed | tf_op | source)
XLA Modules:
  0.0 151.8 jit_solution(16967904146956934946)
XLA Ops:
  0.6 0.5 collective-permute-start
  1.2 1.2 slice.21
  2.3 2.6 %collective-permute-start.1 = (bf16[256,1536]{1,0:T(8,128)(2,1)S(1)}, bf16[256,1536]{1,0:T(8,128)(2,1)}, u32[]{:S(2)}, u32[]{:S(2)}) collective-permute-start(bf16[256,1536]{1,0:T(8,128)(2,1)S(1)} %slice.21), channel_id=1, source_target_pairs={{0,2},{1,3},{2,0},{3,1},{4,6},{5,7},{6,4},{7,5},{8,10},{9,11},{10,... | collective-permute-start | bytes 2359304 | tf_op jit(solution)/shard_map/ppermute | solution.py:680
  4.9 2.7 %slice.22 = bf16[512,1536]{1,0:T(8,128)(2,1)} slice(bf16[1024,1536]{1,0:T(8,128)(2,1)} %own_hbm.1), slice={[256:768], [0:1536]} | slice | bytes 3145728 | tf_op jit(solution)/shard_map/slice | solution.py:678
  7.6 1.2 slice.23
  8.9 2.3 %reduce-window.6 = f32[16,4,2,128]{3,0,1,2:T(8,128)S(1)} reduce-window(f32[16,4,2,128]{3,0,1,2:T(8,128)S(1)} %copy.18, f32[]{:T(128)} %constant.26.clone.1), window={size=1x1x1x128 pad=0_0x0_0x0_0x127_0}, to_apply=%region_0.0 | reduce-window | flops 2080768 | bytes 131076 | tf_op jit(solution)/shard_map/reduce-window
  11.2 0.2 slice_reduce_fusion
  11.5 0.2 fusion.1
  11.7 7.3 %key_totals.1 = (f32[4,16,128,128]{3,2,1,0:T(8,128)}, bf16[8,272,128]{2,1,0:T(8,128)(2,1)}) custom-call(bf16[1024,2048]{1,0:T(8,128)(2,1)} %k_hbm.7, bf16[1024,2048]{1,0:T(8,128)(2,1)} %v_hbm.7, f32[4,4,4,256]{3,2,1,0:T(4,128)S(1)} %reshape.45.cum_ref.refs_2_.refs_3_, f32[1,128]{1,0:T(1,128)S(1)} %pad_bitcast_fusion.span_ref), custom_call_target="tpu_custom_call" | custom-call | flops 536870912 | bytes 12582912 | tf_op jit(solution)/shard_map/key_totals/pallas_call | solution.py:41
  19.0 6.3 %all-to-all-start = ((bf16[8,272,128]{2,1,0:T(8,128)(2,1)}), bf16[8,272,128]{2,1,0:T(8,128)(2,1)S(1)}, u32[]{:S(2)}, u32[]{:S(2)}) async-start(bf16[8,272,128]{2,1,0:T(8,128)(2,1)} %get-tuple-element.36), calls=%async_computation | async-start | bytes 1114112 | tf_op jit(solution)/shard_map/all_to_all | solution.py:655
  25.3 0.2 copy.22
  25.7 19.5 %near_product.1.refs_0_.refs_1_ = f32[1024,2048]{1,0:T(8,128)} custom-call(bf16[1024,1536]{1,0:T(8,128)(2,1)} %own_hbm.1, bf16[1024,1536]{1,0:T(8,128)(2,1)} %collective-permute-done.sibling_hbm, bf16[2048,6144]{1,0:T(8,128)(2,1)} %refs_5_.3), custom_call_target="tpu_custom_call" | custom-call | flops 12884901888 | bytes 27262976 | tf_op jit(solution)/shard_map/near_product/pallas_call | solution.py:41
  45.4 1.5 chain_states.2
  46.8 1.0 copy-done.3
  47.8 11.2 %far_product.3 = (f32[16,128,128]{2,1,0:T(8,128)S(1)}, bf16[256,2048]{1,0:T(8,128)(2,1)}, f32[16,128,128]{2,1,0:T(8,128)}) custom-call(f32[1024,2048]{1,0:T(8,128)} %near_product.1.refs_0_.refs_1_, bf16[1024,2048]{1,0:T(8,128)(2,1)} %q_hbm.3, f32[4,4,4,256]{3,2,1,0:T(4,128)S(1)} %reshape.45.cum_ref.refs_2_.refs_3_, ...), custom_call_target="tpu_custom_call" | custom-call | flops 3355443200 | bytes 21495808 | tf_op jit(solution)/shard_map/far_product/pallas_call | solution.py:41
  59.1 1.0 copy-done
  60.0 0.5 collective-permute-start.4
  60.5 1.6 %collective-permute-start.5 = (bf16[256,1536]{1,0:T(8,128)(2,1)S(1)}, bf16[256,1536]{1,0:T(8,128)(2,1)S(1)}, u32[]{:S(2)}, u32[]{:S(2)}) collective-permute-start(bf16[256,1536]{1,0:T(8,128)(2,1)S(1)} %slice.23), channel_id=1, source_target_pairs={{0,2},{1,3},{2,0},{3,1},{4,6},{5,7},{6,4},{7,5},{8,10},{9,11},{10,... | collective-permute-start | bytes 2359304 | tf_op jit(solution)/shard_map/ppermute | solution.py:680
  62.1 6.0 %all-to-all-start.1 = ((bf16[8,256,128]{2,1,0:T(8,128)(2,1)}), bf16[8,256,128]{2,1,0:T(8,128)(2,1)S(1)}, u32[]{:S(2)}, u32[]{:S(2)}) async-start(bf16[8,256,128]{2,1,0:T(8,128)(2,1)} %chain_states.2), calls=%async_computation.1 | async-start | bytes 1048576 | tf_op jit(solution)/shard_map/all_to_all | solution.py:655
  68.1 15.3 %far_product.4 = (f32[16,128,128]{2,1,0:T(8,128)S(1)}, bf16[512,2048]{1,0:T(8,128)(2,1)}, f32[16,128,128]{2,1,0:T(8,128)}, f32[16,128,128]{2,1,0:T(8,128)}) custom-call(f32[16,128,128]{2,1,0:T(8,128)} %copy-done, f32[1024,2048]{1,0:T(8,128)} %near_product.1.refs_0_.refs_1_, bf16[1024,2048]{1,0:T(8,128)(2,1)} %q_hbm.3, ...), custom_call_target="tpu_custom_call" | custom-call | flops 6710886400 | bytes 27262976 | tf_op jit(solution)/shard_map/far_product/pallas_call | solution.py:41
  83.5 1.0 copy-done.1
  84.4 2.3 %collective-permute-done.6.refs_7_ = bf16[256,1536]{1,0:T(8,128)(2,1)S(1)} collective-permute-done((bf16[256,1536]{1,0:T(8,128)(2,1)S(1)}, bf16[256,1536]{1,0:T(8,128)(2,1)S(1)}, u32[]{:S(2)}, u32[]{:S(2)}) %collective-permute-start.6) | collective-permute-done | bytes 786464 | tf_op jit(solution)/shard_map/ppermute | solution.py:686
  86.7 10.8 %far_product.5 = (bf16[16,128,128]{2,1,0:T(8,128)(2,1)}, bf16[256,2048]{1,0:T(8,128)(2,1)}, f32[16,128,128]{2,1,0:T(8,128)}) custom-call(f32[16,128,128]{2,1,0:T(8,128)} %copy-done.1, f32[1024,2048]{1,0:T(8,128)} %near_product.1.refs_0_.refs_1_, bf16[1024,2048]{1,0:T(8,128)(2,1)} %q_hbm.3, f32[4,4,4,256]{3,2,1,0:T(4,128)S(1)} %reshape.45.cum_ref.refs_2_.refs_3_, ...), custom_call_target="tpu_custom_call" | custom-call | flops 3355443200 | bytes 21495808 | tf_op jit(solution)/shard_map/far_product/pallas_call | solution.py:41
  97.5 6.0 %all-to-all-start.2 = ((bf16[8,256,128]{2,1,0:T(8,128)(2,1)}), bf16[8,256,128]{2,1,0:T(8,128)(2,1)S(1)}, u32[]{:S(2)}, u32[]{:S(2)}) async-start(bf16[8,256,128]{2,1,0:T(8,128)(2,1)} %bitcast.4), calls=%async_computation.2 | async-start | bytes 1048576 | tf_op jit(solution)/shard_map/all_to_all | solution.py:655
  103.5 13.7 %block_terms.2 = (bf16[1024,2048]{1,0:T(8,128)(2,1)}, bf16[512,2048]{1,0:T(8,128)(2,1)}, bf16[512,2048]{1,0:T(8,128)(2,1)}) custom-call(bf16[1024,2048]{1,0:T(8,128)(2,1)} %q_hbm.3, bf16[1024,2048]{1,0:T(8,128)(2,1)} %k_hbm.7, bf16[1024,2048]{1,0:T(8,128)(2,1)} %v_hbm.7, bf16[256,2048]{1,0:T(8,128)(2,1)} %get-tuple-element.49.refs_0_, ...), custom_call_target="tpu_custom_call" | custom-call | flops 2952790016 | bytes 17825792 | tf_op jit(solution)/shard_map/block_terms/pallas_call | solution.py:41
  117.2 1.1 all-to-all-done.2.got_ref
  118.3 1.5 chain_states.3
  119.8 4.9 %all-to-all-start.3 = ((bf16[8,256,128]{2,1,0:T(8,128)(2,1)}), bf16[8,256,128]{2,1,0:T(8,128)(2,1)S(1)}, u32[]{:S(2)}, u32[]{:S(2)}) async-start(bf16[8,256,128]{2,1,0:T(8,128)(2,1)} %chain_states.3), calls=%async_computation.3 | async-start | bytes 1048576 | tf_op jit(solution)/shard_map/all_to_all | solution.py:655
  124.7 13.7 %block_terms.3 = (bf16[1024,2048]{1,0:T(8,128)(2,1)}, bf16[512,2048]{1,0:T(8,128)(2,1)}, bf16[512,2048]{1,0:T(8,128)(2,1)}) custom-call(bf16[1024,2048]{1,0:T(8,128)(2,1)} %q_hbm.3, bf16[1024,2048]{1,0:T(8,128)(2,1)} %k_hbm.7, bf16[1024,2048]{1,0:T(8,128)(2,1)} %v_hbm.7, ...), custom_call_target="tpu_custom_call", output_to_operand_aliasing={{0}: (9, {})} | custom-call | flops 2952790016 | bytes 17825792 | tf_op jit(solution)/shard_map/block_terms/pallas_call | solution.py:41
  138.4 0.6 all-to-all-done.3
  139.0 0.8 copy-done.2
  139.8 11.8 %later_terms.1 = (bf16[1024,2048]{1,0:T(8,128)(2,1)}, bf16[1024,2048]{1,0:T(8,128)(2,1)}) custom-call(bf16[1024,2048]{1,0:T(8,128)(2,1)} %k_hbm.7, bf16[1024,2048]{1,0:T(8,128)(2,1)} %v_hbm.7, f32[4,4,4,256]{3,2,1,0:T(4,128)S(1)} %reshape.45.cum_ref.refs_2_.refs_3_, bf16[16,128,128]{2,1,0:T(8,128)(2,1)} %bitcast.19, ...), custom_call_target="tpu_custom_call" | custom-call | flops 1073741824 | bytes 29360128 | tf_op jit(solution)/shard_map/later_terms/pallas_call | solution.py:41
  (29 shorter events, 0.6 us)
Async XLA Ops:
  0.6 8.2 %copy-start.4 = (f32[16,1024]{1,0:T(8,128)S(1)}, f32[16,1024]{1,0:T(8,128)}, u32[]{:S(2)}) copy-start(f32[16,1024]{1,0:T(8,128)} %param.9) | copy-start | bytes 196612
  0.6 25.1 %collective-permute-start = (bf16[1024,1536]{1,0:T(8,128)(2,1)}, bf16[1024,1536]{1,0:T(8,128)(2,1)}, u32[]{:S(2)}, u32[]{:S(2)}) collective-permute-start(bf16[1024,1536]{1,0:T(8,128)(2,1)} %own_hbm.1), channel_id=1, source_target_pairs={{0,1},{1,0},{2,3},{3,2},{4,5},{5,4},{6,7},{7,6},{8,9},{9,8},{10,11... | collective-permute-start | bytes 9437192 | tf_op jit(solution)/shard_map/ppermute | solution.py:674
  2.3 23.3 %collective-permute-start.1 = (bf16[256,1536]{1,0:T(8,128)(2,1)S(1)}, bf16[256,1536]{1,0:T(8,128)(2,1)}, u32[]{:S(2)}, u32[]{:S(2)}) collective-permute-start(bf16[256,1536]{1,0:T(8,128)(2,1)S(1)} %slice.21), channel_id=1, source_target_pairs={{0,2},{1,3},{2,0},{3,1},{4,6},{5,7},{6,4},{7,5},{8,10},{9,11},{10,... | collective-permute-start | bytes 2359304 | tf_op jit(solution)/shard_map/ppermute | solution.py:680
  7.6 52.4 %collective-permute-start.3 = (bf16[512,1536]{1,0:T(8,128)(2,1)}, bf16[512,1536]{1,0:T(8,128)(2,1)}, u32[]{:S(2)}, u32[]{:S(2)}) collective-permute-start(bf16[512,1536]{1,0:T(8,128)(2,1)} %slice.22), channel_id=1, source_target_pairs={{0,2},{1,3},{2,0},{3,1},{4,6},{5,7},{6,4},{7,5},{8,10},{9,11},{10,... | collective-permute-start | bytes 4718600 | tf_op jit(solution)/shard_map/ppermute | solution.py:680
  19.0 26.3 %all-to-all-start = ((bf16[8,272,128]{2,1,0:T(8,128)(2,1)}), bf16[8,272,128]{2,1,0:T(8,128)(2,1)S(1)}, u32[]{:S(2)}, u32[]{:S(2)}) async-start(bf16[8,272,128]{2,1,0:T(8,128)(2,1)} %get-tuple-element.36), calls=%async_computation | async-start | bytes 1114112 | tf_op jit(solution)/shard_map/all_to_all | solution.py:655
  25.7 21.2 %collective-permute-start.2 = (bf16[256,1536]{1,0:T(8,128)(2,1)}, bf16[256,1536]{1,0:T(8,128)(2,1)S(1)}, u32[]{:S(2)}, u32[]{:S(2)}) collective-permute-start(bf16[256,1536]{1,0:T(8,128)(2,1)} %collective-permute-done.1.refs_5_), channel_id=1, source_target_pairs={{0,1},{1,0},{2,3},{3,2},{4,5},{5,4},{6,7},{7,6},{8,9},{9,8},{10,11... | collective-permute-start | bytes 2359304 | tf_op jit(solution)/shard_map/ppermute | solution.py:686
  46.8 1.0 copy-start.3
  59.1 1.0 copy-start
  60.0 8.1 %collective-permute-start.4 = (bf16[512,1536]{1,0:T(8,128)(2,1)}, bf16[512,1536]{1,0:T(8,128)(2,1)}, u32[]{:S(2)}, u32[]{:S(2)}) collective-permute-start(bf16[512,1536]{1,0:T(8,128)(2,1)} %collective-permute-done.3.refs_6_), channel_id=1, source_target_pairs={{0,1},{1,0},{2,3},{3,2},{4,5},{5,4},{6,7},{7,6},{8,9},{9,8},{10,11... | collective-permute-start | bytes 4718600 | tf_op jit(solution)/shard_map/ppermute | solution.py:686
  60.5 23.9 %collective-permute-start.5 = (bf16[256,1536]{1,0:T(8,128)(2,1)S(1)}, bf16[256,1536]{1,0:T(8,128)(2,1)S(1)}, u32[]{:S(2)}, u32[]{:S(2)}) collective-permute-start(bf16[256,1536]{1,0:T(8,128)(2,1)S(1)} %slice.23), channel_id=1, source_target_pairs={{0,2},{1,3},{2,0},{3,1},{4,6},{5,7},{6,4},{7,5},{8,10},{9,11},{10,... | collective-permute-start | bytes 2359304 | tf_op jit(solution)/shard_map/ppermute | solution.py:680
  62.1 22.3 %all-to-all-start.1 = ((bf16[8,256,128]{2,1,0:T(8,128)(2,1)}), bf16[8,256,128]{2,1,0:T(8,128)(2,1)S(1)}, u32[]{:S(2)}, u32[]{:S(2)}) async-start(bf16[8,256,128]{2,1,0:T(8,128)(2,1)} %chain_states.2), calls=%async_computation.1 | async-start | bytes 1048576 | tf_op jit(solution)/shard_map/all_to_all | solution.py:655
  83.5 1.0 copy-start.1
  84.4 2.3 %collective-permute-start.6 = (bf16[256,1536]{1,0:T(8,128)(2,1)S(1)}, bf16[256,1536]{1,0:T(8,128)(2,1)S(1)}, u32[]{:S(2)}, u32[]{:S(2)}) collective-permute-start(bf16[256,1536]{1,0:T(8,128)(2,1)S(1)} %collective-permute-done.5.refs_6_), channel_id=1, source_target_pairs={{0,1},{1,0},{2,3},{3,2},{4,5},{5,4},{6,7},{7,6},{8,9},{9,8},{10,11... | collective-permute-start | bytes 2359304 | tf_op jit(solution)/shard_map/ppermute | solution.py:686
  97.5 20.8 %all-to-all-start.2 = ((bf16[8,256,128]{2,1,0:T(8,128)(2,1)}), bf16[8,256,128]{2,1,0:T(8,128)(2,1)S(1)}, u32[]{:S(2)}, u32[]{:S(2)}) async-start(bf16[8,256,128]{2,1,0:T(8,128)(2,1)} %bitcast.4), calls=%async_computation.2 | async-start | bytes 1048576 | tf_op jit(solution)/shard_map/all_to_all | solution.py:655
  119.8 19.2 %all-to-all-start.3 = ((bf16[8,256,128]{2,1,0:T(8,128)(2,1)}), bf16[8,256,128]{2,1,0:T(8,128)(2,1)S(1)}, u32[]{:S(2)}, u32[]{:S(2)}) async-start(bf16[8,256,128]{2,1,0:T(8,128)(2,1)} %chain_states.3), calls=%async_computation.3 | async-start | bytes 1048576 | tf_op jit(solution)/shard_map/all_to_all | solution.py:655
  139.0 0.8 copy-start.2

commit v5 on v4

--- a/solution.py
+++ b/solution.py
@@ -10,6 +10,7 @@
 HD = 128
 BLK = 256
 GROUP = 4
+PAIR = 2
 ROW = 16
 MIB = 2**20
 
@@ -70,9 +71,20 @@
     return slice(h * HD, (h + 1) * HD)
 
 
-def key_body(k_hbm, v_hbm, cum_ref, span_ref, local_hbm, total_ref, k_ref, v_ref, local_ref, load_sems, store_sems):
+def prefix_sums(x):
+    at = lax.broadcasted_iota(jnp.int32, x.shape, 1)
+    step = 1
+    while step < x.shape[1]:
+        x = x + jnp.where(at >= step, pltpu.roll(x, step, 1), 0.0)
+        step *= 2
+    return x
+
+
+def key_body(cuts, k_hbm, v_hbm, decay_hbm, grad_hbm, local_hbm, total_ref, cum_ref, pair_ref, *refs):
+    cut_hbm, refs = refs[: len(cuts)], refs[len(cuts) :]
+    decay_ref, cut_ref, k_ref, v_ref, local_ref, load_sems, store_sems, cut_sems = refs
     blk_count, groups, group, _ = cum_ref.shape
-    wide = group * HD
+    heads, wide = groups * group, group * HD
 
     def loads(j):
         rows = pl.ds(j * BLK, BLK)
@@ -84,10 +96,32 @@
     def store(j):
         return copy_of(local_ref.at[j], local_hbm.at[j], store_sems.at[j])
 
+    origin = cuts[0][0]
+    cut_load = copy_of(grad_hbm.at[pl.ds(origin, cuts[-1][1] - origin)], cut_ref, cut_sems.at[len(cuts)])
+
+    def cut_store(n):
+        first, last = cuts[n]
+        return copy_of(cut_ref.at[pl.ds(first - origin, last - first)], cut_hbm[n], cut_sems.at[n])
+
+    decay_load = copy_of(decay_hbm, decay_ref, cut_sems.at[len(cuts) + 1])
+    decay_load.start()
     for j in range(min(2, blk_count)):
         for copy in loads(j):
             copy.start()
+    cut_load.start()
+    decay_load.wait()
+    span_of = jnp.zeros((heads, 1), F32)
+    for j in range(blk_count):
+        cum = prefix_sums(decay_ref[:, span(j, BLK)])
+        for g in range(groups):
+            cum_ref[j, g] = cum[span(g, group)]
+        for g in range(heads // PAIR):
+            pair_ref[j, g] = cum[span(g, PAIR)]
+        span_of = span_of + cum[:, BLK - 1 : BLK]
     local_ref[0] = jnp.zeros_like(local_ref[0])
+    cut_load.wait()
+    for n in range(len(cuts)):
+        cut_store(n).start()
 
     def block(j):
         for copy in loads(j):
@@ -122,7 +156,10 @@
     loop(blk_count, block)
     devices, share = total_ref.shape[0], total_ref.shape[1] - ROW
     total_ref[:, :share] = local_ref[blk_count].astype(BF16).reshape(devices, share, HD)
-    left, parts = jnp.broadcast_to(span_ref[...], (ROW, HD)), jnp.zeros((ROW, HD), F32)
+
+    diagonal = lax.broadcasted_iota(jnp.int32, (heads, HD), 0) == lax.broadcasted_iota(jnp.int32, (heads, HD), 1)
+    spans = jnp.sum(jnp.where(diagonal, span_of, 0.0), axis=0, keepdims=True)
+    left, parts = jnp.broadcast_to(spans, (ROW, HD)), jnp.zeros((ROW, HD), F32)
     at_row = lax.broadcasted_iota(jnp.int32, (ROW, HD), 0)
     for n in range(3):
         rounded = left.astype(BF16).astype(F32)
@@ -132,29 +169,38 @@
         total_ref[d, share:] = parts.astype(BF16)
     for j in range(blk_count):
         store(j).wait()
-
-
-def key_totals(keys, values, cum, own_span, devices):
+    for n in range(len(cuts)):
+        cut_store(n).wait()
+
+
+def key_totals(keys, values, log_decay, grad, cuts, devices):
     rows, width = keys.shape
-    blk_count, heads = cum.shape[0], width // HD
-    return call(
-        key_body,
+    blk_count, heads = rows // BLK, width // HD
+    local_enter, total, cum, pair_cum, *parts = call(
+        functools.partial(key_body, cuts),
         "key_totals",
-        [(keys, HBM), (values, HBM), (cum, VMEM), (own_span, VMEM)],
+        [(keys, HBM), (values, HBM), (log_decay, HBM), (grad, HBM)],
         [
             ((blk_count, heads, HD, HD), F32, HBM),
             ((devices, heads * HD // devices + ROW, HD), BF16, VMEM),
-        ],
+            ((blk_count, heads // GROUP, GROUP, BLK), F32, VMEM),
+            ((blk_count, heads // PAIR, PAIR, BLK), F32, VMEM),
+        ]
+        + [((last - first, grad.shape[1]), BF16, HBM) for first, last in cuts],
         [
+            pltpu.VMEM(log_decay.shape, F32),
+            pltpu.VMEM((cuts[-1][1] - cuts[0][0], grad.shape[1]), BF16),
             pltpu.VMEM((rows, width), BF16),
             pltpu.VMEM((rows, width), BF16),
             pltpu.VMEM((blk_count + 1, heads, HD, HD), F32),
             pltpu.SemaphoreType.DMA((2, blk_count)),
             pltpu.SemaphoreType.DMA((blk_count,)),
+            pltpu.SemaphoreType.DMA((len(cuts) + 2,)),
         ],
         24,
         cost(2 * rows * width * HD, 4 * rows * width + 4 * blk_count * width * HD),
     )
+    return local_enter, total, cum, pair_cum, parts
 
 
 def near_body(wide, own_hbm, sibling_hbm, w_hbm, out_hbm, grad_ref, w_ref, out_ref, w_sems, grad_sems, out_sems):
@@ -278,9 +324,9 @@
     total_ref, grad_hbm, *sums_hbm = refs[: 2 + count]
     refs = refs[2 + count :]
     if direct:
-        held = pieces
+        held, total_hbm = pieces, None
     else:
-        held, refs = refs[: len(pieces)], refs[len(pieces) :]
+        held, total_hbm, total_ref, refs = refs[: len(pieces)], total_ref, refs[len(pieces)], refs[len(pieces) + 1 :]
     w_ref, near_ref, q_ref, grad_ref, before_ref, sums_ref, piece_sems, load_sems, store_sems = refs
     rows, depth = pieces[0].shape
     _, groups, group, _ = cum_ref.shape
@@ -316,7 +362,10 @@
 
     def sums_stores(g):
         these = pl.ds(g * group, group)
-        return [copy_of(sums_ref.at[n, these], sums_hbm[n].at[these], store_sems.at[n, g]) for n in range(count)]
+        found = [copy_of(sums_ref.at[n, these], sums_hbm[n].at[these], store_sems.at[n, g]) for n in range(count)]
+        if total_hbm is not None:
+            found.append(copy_of(total_ref.at[these], total_hbm.at[these], store_sems.at[count + 1, g]))
+        return found
 
     def product(g):
         for copy in loads(g):
@@ -337,13 +386,15 @@
         copy.start()
     for copy in piece_loads():
         copy.wait()
+    for copy in loads(2) if groups > 2 else ():
+        copy.start()
     grad_ref[:, :wide] = product(0)
     store(0).start()
 
     def step(g):
-        @pl.when(g + 2 < groups)
+        @pl.when(g + 3 < groups)
         def _():
-            for copy in loads(g + 2):
+            for copy in loads(g + 3):
                 copy.start()
 
         mine = grad_ref[:, lanes_of(g, wide)]
@@ -380,9 +431,9 @@
         "far_product",
         ([(before, HBM)] if start else [])
         + [(near, HBM), (queries, HBM), (cum, VMEM), (prior, SMEM), (weight, HBM)]
-        + [(piece, VMEM if last else HBM) for piece in pieces],
-        [(states, BF16 if last else F32, VMEM), ((rows, width), BF16, HBM)] + [(states, F32, HBM)] * count,
-        ([] if last else [pltpu.VMEM(piece.shape, BF16) for piece in pieces])
+        + [(piece, VMEM if last else ANY) for piece in pieces],
+        [(states, BF16 if last else F32, VMEM if last else HBM), ((rows, width), BF16, HBM)] + [(states, F32, HBM)] * count,
+        ([] if last else [pltpu.VMEM(piece.shape, BF16) for piece in pieces] + [pltpu.VMEM(states, F32)])
         + [
             pltpu.VMEM((width, far_depth), BF16),
             pltpu.VMEM((rows, width), F32),
@@ -392,7 +443,7 @@
             pltpu.VMEM((count, *states), F32),
             pltpu.SemaphoreType.DMA((len(pieces),)),
             pltpu.SemaphoreType.DMA((chips + 2, groups)),
-            pltpu.SemaphoreType.DMA((count + 1, groups)),
+            pltpu.SemaphoreType.DMA((count + 2, groups)),
         ],
         36,
         cost(
@@ -523,13 +574,13 @@
     )
 
 
-def later_body(k_hbm, v_hbm, cum_ref, enter_hbm, *refs):
+def later_body(k_hbm, v_hbm, cum_ref, enter_ref, *refs):
     blk_count, groups, group, _ = cum_ref.shape
-    halves = len(refs) - 11 - (blk_count - 1)
+    halves = len(refs) - 10 - (blk_count - 1)
     gk_parts, gv_parts = refs[: halves // 2], refs[halves // 2 : halves]
     each = blk_count // len(gk_parts)
     sums_hbm = refs[halves : halves + blk_count - 1]
-    gk_hbm, gv_hbm, k_ref, v_ref, gk_ref, gv_ref, sums_ref, enter_ref, carry_ref = refs[halves + blk_count - 1 : -2]
+    gk_hbm, gv_hbm, k_ref, v_ref, gk_ref, gv_ref, sums_ref, carry_ref = refs[halves + blk_count - 1 : -2]
     load_sems, store_sems = refs[-2:]
     wide = group * HD
 
@@ -553,12 +604,9 @@
             copy_of(gv_ref.at[rows, lanes], gv_hbm.at[rows, lanes], store_sems.at[1, j, g]),
         )
 
-    enter_load = copy_of(enter_hbm, enter_ref, load_sems.at[4, 0, 0])
-    enter_load.start()
     for g in range(groups):
         for copy in loads(blk_count - 1, g):
             copy.start()
-    enter_load.wait()
     for j in reversed(range(blk_count)):
 
         def some_heads(g, j=j):
@@ -607,13 +655,12 @@
     return call(
         later_body,
         "later_terms",
-        [(keys, HBM), (values, HBM), (cum, VMEM), (enter, HBM)]
+        [(keys, HBM), (values, HBM), (cum, VMEM), (enter, VMEM)]
         + [(x, HBM) for x in gk_parts + gv_parts + sums],
         [out, out],
         [whole] * 4
         + [
             pltpu.VMEM((blk_count, heads, HD, HD), F32),
-            pltpu.VMEM((heads, HD, HD), BF16),
             pltpu.VMEM((heads, HD, HD), F32),
             pltpu.SemaphoreType.DMA((5, blk_count, cum.shape[1])),
             pltpu.SemaphoreType.DMA((2, blk_count, cum.shape[1])),
@@ -673,11 +720,13 @@
     own = grad_output
     sibling = lax.ppermute(own, "tp", core)
     starts = [0, 1, blk_count - 1, blk_count]
-    cuts, rest = [], own
-    for a, b in zip(starts, starts[1:]):
-        cuts.append(rest[a * BLK : b * BLK])
-        rest = after(own, cuts[0])
-    first = [[lax.ppermute(x, "tp", from_chip(d)) for d in range(1, chips)] for x in cuts]
+    cuts = [(a * BLK, b * BLK) for a, b in zip(starts, starts[1:])]
+    head_rows = own[: cuts[0][1]]
+    local_enter, fwd_total, cum, pair_cum, rest = key_totals(
+        key_vectors, value_vectors, after(log_decay, head_rows), own, cuts[1:], seq
+    )
+    fwd_got = swap(fwd_total)
+    first = [[lax.ppermute(x, "tp", from_chip(d)) for d in range(1, chips)] for x in [head_rows, *rest]]
 
     def hand_on(j, *earlier):
         arrived = []
@@ -686,14 +735,8 @@
             arrived += [x, lax.ppermute(x, "tp", core)]
         return arrived
 
-    cum = jnp.cumsum(after(log_decay, *cuts).reshape(heads, blk_count, BLK), axis=2)
-    end = cum[:, :, -1]
-    prior = jnp.exp(jnp.cumsum(end, axis=1) - end)
-    cum = cum.transpose(1, 0, 2).reshape(blk_count, heads // GROUP, GROUP, BLK)
-    own_span = jnp.pad(jnp.sum(end, axis=1), (0, HD - heads))[None]
-
-    local_enter, fwd_total = key_totals(key_vectors, value_vectors, cum, own_span, seq)
-    fwd_got = swap(fwd_total)
+    end = cum[:, :, :, BLK - 1].reshape(blk_count, heads)
+    prior = jnp.exp(jnp.cumsum(end, axis=0) - end).T
 
     arrived = hand_on(0, fwd_total)
     near = near_product(own, after(sibling, arrived[0]), out_weight)
@@ -706,11 +749,11 @@
     fwd_out = chain(fwd_got, mine, share, False)
     enter_fwd = swap(fwd_out).reshape(heads, HD, HD)
 
-    grads, sums, total, cum_now = [], [], None, after(cum, fwd_out)
+    grads, sums, total, cum_now = [], [], None, after(pair_cum, fwd_out)
     for part, start in enumerate(starts[:-1]):
         if part:
             arrived = hand_on(part, total)
-            cum_now = after(cum, enter_fwd) if part == 2 else cum
+            cum_now = after(pair_cum, enter_fwd) if part == 2 else pair_cum
         grad, some, total = far_product(start, total, arrived, out_weight, near, queries, cum_now, prior)
         grads += [(j, grad) for j in range(grad.shape[0] // BLK)]
         sums += some

time: 152 us -> 146 us (0.961)
  local copies, waits for them, and re-layouts: 9.28 us -> 2.42 us
  waiting for transfers between devices: 4 us -> 7.94 us
  other arithmetic: 2.74 us -> 0.18 us
    ppermute x3, waiting for transfers between devices: 0.01 us -> 4.18 us  [local(): lax.ppermute(x, 'tp', from_chip(d))]
    unnamed x10 -> x0, local copies, waits for them, and re-layouts: 3.69 us -> none
    slice x4 -> x2, local copies, waits for them, and re-layouts: 5.2 us -> 2.14 us  [the longest x1 2.06 us: local(): head_rows = own[:cuts[0][1]]]
    another operation x4 -> x1, other arithmetic: 2.53 us -> 0.16 us  [local(): prior = jnp.exp(jnp.cumsum(end, axis=0) - end).T]
  transfers between devices with their start and end apart: 11 -> 11, of which waited for: 3 -> 6; matrix products, arithmetic and copies ran while one was open for 5% -> 2% of each run, Pallas kernels for 54% -> 57%
where the time goes in v5:
time: 146 us
  Pallas kernels  106 us (73%)
  starting transfers between devices  28 us (19%)
  waiting for transfers between devices  7.94 us (5%)
  local copies, waits for them, and re-layouts  2.42 us (2%)
    pallas_call x10, Pallas kernels, call(): pl.pallas_call(body, in_specs=[spec for _, spec in ins], out_specs=[spec...  106 us
    all_to_all x4, starting transfers between devices, swap(): lax.all_to_all(flat, 'seq', 0, 0, tiled=True).reshape(devices, -1, HD)  22.6 us
    ppermute x3, starting transfers between devices, local(): lax.ppermute(x, 'tp', from_chip(d))  4.78 us
    ppermute x3, waiting for transfers between devices, local(): lax.ppermute(x, 'tp', from_chip(d))  4.18 us
  transfers between devices with their start and end apart: 11, of which 6 were waited for; matrix products, arithmetic and copies ran while one was open for 2% of the time, Pallas kernels for 57%

profile of v5, /device:TPU:0, one launch (start us, length us, event | category | flops | bytes accessed | tf_op | source)
XLA Modules:
  0.0 145.9 jit_solution(15021779753554932495)
XLA Ops:
  0.6 0.5 collective-permute-start
  1.1 2.1 %slice.9 = bf16[256,1536]{1,0:T(8,128)(2,1)} slice(bf16[1024,1536]{1,0:T(8,128)(2,1)} %own_hbm.1), slice={[0:256], [0:1536]} | slice | bytes 1572864 | tf_op jit(solution)/shard_map/slice | solution.py:724
  3.2 2.5 %collective-permute-start.1 = (bf16[256,1536]{1,0:T(8,128)(2,1)}, bf16[256,1536]{1,0:T(8,128)(2,1)S(1)}, u32[]{:S(2)}, u32[]{:S(2)}) collective-permute-start(bf16[256,1536]{1,0:T(8,128)(2,1)} %slice.9), channel_id=1, source_target_pairs={{0,2},{1,3},{2,0},{3,1},{4,6},{5,7},{6,4},{7,5},{8,10},{9,11},{10,... | collective-permute-start | bytes 2359304 | tf_op jit(solution)/shard_map/ppermute | solution.py:729
  5.7 9.5 %key_totals.1 = (f32[4,16,128,128]{3,2,1,0:T(8,128)}, bf16[8,272,128]{2,1,0:T(8,128)(2,1)}, f32[4,4,4,256]{3,2,1,0:T(4,128)S(1)}, f32[4,8,2,256]{3,2,1,0:T(2,128...) custom-call(bf16[1024,2048]{1,0:T(8,128)(2,1)} %k_hbm.7, bf16[1024,2048]{1,0:T(8,128)(2,1)} %v_hbm.7, ...), custom_call_target="tpu_custom_call" | custom-call | flops 536870912 | bytes 12582912 | tf_op jit(solution)/shard_map/key_totals/pallas_call | solution.py:42
  15.2 5.8 %all-to-all-start = ((bf16[8,272,128]{2,1,0:T(8,128)(2,1)}), bf16[8,272,128]{2,1,0:T(8,128)(2,1)S(1)}, u32[]{:S(2)}, u32[]{:S(2)}) async-start(bf16[8,272,128]{2,1,0:T(8,128)(2,1)} %get-tuple-element.38), calls=%async_computation | async-start | bytes 1114112 | tf_op jit(solution)/shard_map/all_to_all | solution.py:702
  21.0 0.5 collective-permute-start.3
  21.5 0.1 slice.11
  21.6 0.2 copy.14
  21.8 0.2 reduce_window_sum.11
  22.0 2.4 %collective-permute-done.1.refs_5_ = bf16[256,1536]{1,0:T(8,128)(2,1)S(1)} collective-permute-done((bf16[256,1536]{1,0:T(8,128)(2,1)}, bf16[256,1536]{1,0:T(8,128)(2,1)S(1)}, u32[]{:S(2)}, u32[]{:S(2)}) %collective-permute-start.1) | collective-permute-done | bytes 786464 | tf_op jit(solution)/shard_map/ppermute | solution.py:729
  24.3 0.0 collective-permute-start.2
  24.4 19.5 %near_product.1.refs_0_.refs_1_ = f32[1024,2048]{1,0:T(8,128)} custom-call(bf16[1024,1536]{1,0:T(8,128)(2,1)} %own_hbm.1, bf16[1024,1536]{1,0:T(8,128)(2,1)} %collective-permute-done.sibling_hbm, bf16[2048,6144]{1,0:T(8,128)(2,1)} %refs_5_.3), custom_call_target="tpu_custom_call" | custom-call | flops 12884901888 | bytes 27262976 | tf_op jit(solution)/shard_map/near_product/pallas_call | solution.py:42
  43.9 0.0 all-to-all-done.got_ref
  43.9 0.1 constant_dynamic-slice_fusion.weight_ref
  44.0 1.5 %chain_states.2 = bf16[8,256,128]{2,1,0:T(8,128)(2,1)} custom-call(bf16[8,272,128]{2,1,0:T(8,128)(2,1)S(1)} %all-to-all-done.got_ref, f32[8,2]{1,0:T(8,128)S(1)} %constant_dynamic-slice_fusion.weight_ref), custom_call_target="tpu_custom_call" | custom-call | flops 524288 | bytes 1048576 | tf_op jit(solution)/shard_map/chain_states/pallas_call | solution.py:42
  45.5 10.5 %far_product.3 = (f32[16,128,128]{2,1,0:T(8,128)}, bf16[256,2048]{1,0:T(8,128)(2,1)}, f32[16,128,128]{2,1,0:T(8,128)}) custom-call(f32[1024,2048]{1,0:T(8,128)} %near_product.1.refs_0_.refs_1_, bf16[1024,2048]{1,0:T(8,128)(2,1)} %q_hbm.3, f32[4,8,2,256]{3,2,1,0:T(2,128)S(1)} %get-tuple-element.50.refs_2_.refs_3_, ...), custom_call_target="tpu_custom_call" | custom-call | flops 3355443200 | bytes 21495808 | tf_op jit(solution)/shard_map/far_product/pallas_call | solution.py:42
  56.0 1.8 %collective-permute-done.3.refs_6_ = bf16[512,1536]{1,0:T(8,128)(2,1)S(1)} collective-permute-done((bf16[512,1536]{1,0:T(8,128)(2,1)}, bf16[512,1536]{1,0:T(8,128)(2,1)S(1)}, u32[]{:S(2)}, u32[]{:S(2)}) %collective-permute-start.3) | collective-permute-done | bytes 1572896 | tf_op jit(solution)/shard_map/ppermute | solution.py:729
  57.9 1.7 %collective-permute-start.5 = (bf16[256,1536]{1,0:T(8,128)(2,1)}, bf16[256,1536]{1,0:T(8,128)(2,1)S(1)}, u32[]{:S(2)}, u32[]{:S(2)}) collective-permute-start(bf16[256,1536]{1,0:T(8,128)(2,1)} %get-tuple-element.51), channel_id=1, source_target_pairs={{0,2},{1,3},{2,0},{3,1},{4,6},{5,7},{6,4},{7,5},{8,10},{9,11},{10,... | collective-permute-start | bytes 2359304 | tf_op jit(solution)/shard_map/ppermute | solution.py:729
  59.6 5.8 %all-to-all-start.1 = ((bf16[8,256,128]{2,1,0:T(8,128)(2,1)}), bf16[8,256,128]{2,1,0:T(8,128)(2,1)S(1)}, u32[]{:S(2)}, u32[]{:S(2)}) async-start(bf16[8,256,128]{2,1,0:T(8,128)(2,1)} %chain_states.2), calls=%async_computation.1 | async-start | bytes 1048576 | tf_op jit(solution)/shard_map/all_to_all | solution.py:702
  65.4 14.2 %far_product.4 = (f32[16,128,128]{2,1,0:T(8,128)}, bf16[512,2048]{1,0:T(8,128)(2,1)}, f32[16,128,128]{2,1,0:T(8,128)}, f32[16,128,128]{2,1,0:T(8,128)}) custom-call(f32[16,128,128]{2,1,0:T(8,128)} %get-tuple-element.45.refs_0_, f32[1024,2048]{1,0:T(8,128)} %near_product.1.refs_0_.refs_1_, bf16[1024,2048]{1,0:T(8,128)(2,1)} %q_hbm.3, ...), custom_call_target="tpu_custom_call" | custom-call | flops 6710886400 | bytes 27262976 | tf_op jit(solution)/shard_map/far_product/pallas_call | solution.py:42
  79.6 0.1 collective-permute-start.6
  79.7 0.6 all-to-all-done.1
  80.3 1.7 %collective-permute-done.6.refs_7_ = bf16[256,1536]{1,0:T(8,128)(2,1)S(1)} collective-permute-done((bf16[256,1536]{1,0:T(8,128)(2,1)S(1)}, bf16[256,1536]{1,0:T(8,128)(2,1)S(1)}, u32[]{:S(2)}, u32[]{:S(2)}) %collective-permute-start.6) | collective-permute-done | bytes 786464 | tf_op jit(solution)/shard_map/ppermute | solution.py:735
  82.0 10.5 %far_product.5 = (bf16[16,128,128]{2,1,0:T(8,128)(2,1)}, bf16[256,2048]{1,0:T(8,128)(2,1)}, f32[16,128,128]{2,1,0:T(8,128)}) custom-call(f32[16,128,128]{2,1,0:T(8,128)} %get-tuple-element.49.refs_0_, f32[1024,2048]{1,0:T(8,128)} %near_product.1.refs_0_.refs_1_, bf16[1024,2048]{1,0:T(8,128)(2,1)} %q_hbm.3, ...), custom_call_target="tpu_custom_call" | custom-call | flops 3355443200 | bytes 21495808 | tf_op jit(solution)/shard_map/far_product/pallas_call | solution.py:42
  92.5 6.0 %all-to-all-start.2 = ((bf16[8,256,128]{2,1,0:T(8,128)(2,1)}), bf16[8,256,128]{2,1,0:T(8,128)(2,1)S(1)}, u32[]{:S(2)}, u32[]{:S(2)}) async-start(bf16[8,256,128]{2,1,0:T(8,128)(2,1)} %bitcast.3), calls=%async_computation.2 | async-start | bytes 1048576 | tf_op jit(solution)/shard_map/all_to_all | solution.py:702
  98.5 13.7 %block_terms.2 = (bf16[1024,2048]{1,0:T(8,128)(2,1)}, bf16[512,2048]{1,0:T(8,128)(2,1)}, bf16[512,2048]{1,0:T(8,128)(2,1)}) custom-call(bf16[1024,2048]{1,0:T(8,128)(2,1)} %q_hbm.3, bf16[1024,2048]{1,0:T(8,128)(2,1)} %k_hbm.7, bf16[1024,2048]{1,0:T(8,128)(2,1)} %v_hbm.7, bf16[256,2048]{1,0:T(8,128)(2,1)} %get-tuple-element.55.refs_0_, ...), custom_call_target="tpu_custom_call" | custom-call | flops 2952790016 | bytes 17825792 | tf_op jit(solution)/shard_map/block_terms/pallas_call | solution.py:42
  112.3 1.0 all-to-all-done.2.got_ref
  113.3 1.5 %chain_states.3 = bf16[8,256,128]{2,1,0:T(8,128)(2,1)} custom-call(bf16[8,256,128]{2,1,0:T(8,128)(2,1)S(1)} %all-to-all-done.2.got_ref, f32[8,2]{1,0:T(8,128)S(1)} %constant_dynamic-slice_fusion.weight_ref), custom_call_target="tpu_custom_call" | custom-call | flops 524288 | bytes 1048576 | tf_op jit(solution)/shard_map/chain_states/pallas_call | solution.py:42
  114.8 5.0 %all-to-all-start.3 = ((bf16[8,256,128]{2,1,0:T(8,128)(2,1)}), bf16[8,256,128]{2,1,0:T(8,128)(2,1)S(1)}, u32[]{:S(2)}, u32[]{:S(2)}) async-start(bf16[8,256,128]{2,1,0:T(8,128)(2,1)} %chain_states.3), calls=%async_computation.3 | async-start | bytes 1048576 | tf_op jit(solution)/shard_map/all_to_all | solution.py:702
  119.8 13.8 %block_terms.3 = (bf16[1024,2048]{1,0:T(8,128)(2,1)}, bf16[512,2048]{1,0:T(8,128)(2,1)}, bf16[512,2048]{1,0:T(8,128)(2,1)}) custom-call(bf16[1024,2048]{1,0:T(8,128)(2,1)} %q_hbm.3, bf16[1024,2048]{1,0:T(8,128)(2,1)} %k_hbm.7, bf16[1024,2048]{1,0:T(8,128)(2,1)} %v_hbm.7, ...), custom_call_target="tpu_custom_call", output_to_operand_aliasing={{0}: (9, {})} | custom-call | flops 2952790016 | bytes 17825792 | tf_op jit(solution)/shard_map/block_terms/pallas_call | solution.py:42
  133.6 0.5 all-to-all-done.3
  134.0 11.7 %later_terms.1 = (bf16[1024,2048]{1,0:T(8,128)(2,1)}, bf16[1024,2048]{1,0:T(8,128)(2,1)}) custom-call(bf16[1024,2048]{1,0:T(8,128)(2,1)} %k_hbm.7, bf16[1024,2048]{1,0:T(8,128)(2,1)} %v_hbm.7, f32[4,4,4,256]{3,2,1,0:T(4,128)S(1)} %get-tuple-element.60.refs_2_.cum_ref, bf16[16,128,128]{2,1,0:T(8,128)(2,1)S(1)} %bitcast.8, ...), custom_call_target="tpu_custom_call" | custom-call | flops 1073741824 | bytes 29360128 | tf_op jit(solution)/shard_map/later_terms/pallas_call | solution.py:42
  (8 shorter events, 0.0 us)
Async XLA Ops:
  0.6 23.7 %collective-permute-start = (bf16[1024,1536]{1,0:T(8,128)(2,1)}, bf16[1024,1536]{1,0:T(8,128)(2,1)}, u32[]{:S(2)}, u32[]{:S(2)}) collective-permute-start(bf16[1024,1536]{1,0:T(8,128)(2,1)} %own_hbm.1), channel_id=1, source_target_pairs={{0,1},{1,0},{2,3},{3,2},{4,5},{5,4},{6,7},{7,6},{8,9},{9,8},{10,11... | collective-permute-start | bytes 9437192 | tf_op jit(solution)/shard_map/ppermute | solution.py:721
  3.2 21.1 %collective-permute-start.1 = (bf16[256,1536]{1,0:T(8,128)(2,1)}, bf16[256,1536]{1,0:T(8,128)(2,1)S(1)}, u32[]{:S(2)}, u32[]{:S(2)}) collective-permute-start(bf16[256,1536]{1,0:T(8,128)(2,1)} %slice.9), channel_id=1, source_target_pairs={{0,2},{1,3},{2,0},{3,1},{4,6},{5,7},{6,4},{7,5},{8,10},{9,11},{10,... | collective-permute-start | bytes 2359304 | tf_op jit(solution)/shard_map/ppermute | solution.py:729
  15.2 28.6 %all-to-all-start = ((bf16[8,272,128]{2,1,0:T(8,128)(2,1)}), bf16[8,272,128]{2,1,0:T(8,128)(2,1)S(1)}, u32[]{:S(2)}, u32[]{:S(2)}) async-start(bf16[8,272,128]{2,1,0:T(8,128)(2,1)} %get-tuple-element.38), calls=%async_computation | async-start | bytes 1114112 | tf_op jit(solution)/shard_map/all_to_all | solution.py:702
  21.0 36.8 %collective-permute-start.3 = (bf16[512,1536]{1,0:T(8,128)(2,1)}, bf16[512,1536]{1,0:T(8,128)(2,1)S(1)}, u32[]{:S(2)}, u32[]{:S(2)}) collective-permute-start(bf16[512,1536]{1,0:T(8,128)(2,1)} %get-tuple-element.46), channel_id=1, source_target_pairs={{0,2},{1,3},{2,0},{3,1},{4,6},{5,7},{6,4},{7,5},{8,10},{9,11},{10,... | collective-permute-start | bytes 4718600 | tf_op jit(solution)/shard_map/ppermute | solution.py:729
  24.3 21.2 %collective-permute-start.2 = (bf16[256,1536]{1,0:T(8,128)(2,1)S(1)}, bf16[256,1536]{1,0:T(8,128)(2,1)}, u32[]{:S(2)}, u32[]{:S(2)}) collective-permute-start(bf16[256,1536]{1,0:T(8,128)(2,1)S(1)} %collective-permute-done.1.refs_5_), channel_id=1, source_target_pairs={{0,1},{1,0},{2,3},{3,2},{4,5},{5,4},{6,7},{7,6},{8,9},{9,8},{10,11... | collective-permute-start | bytes 2359304 | tf_op jit(solution)/shard_map/ppermute | solution.py:735
  57.9 7.6 %collective-permute-start.4 = (bf16[512,1536]{1,0:T(8,128)(2,1)S(1)}, bf16[512,1536]{1,0:T(8,128)(2,1)}, u32[]{:S(2)}, u32[]{:S(2)}) collective-permute-start(bf16[512,1536]{1,0:T(8,128)(2,1)S(1)} %collective-permute-done.3.refs_6_), channel_id=1, source_target_pairs={{0,1},{1,0},{2,3},{3,2},{4,5},{5,4},{6,7},{7,6},{8,9},{9,8},{10,11... | collective-permute-start | bytes 4718600 | tf_op jit(solution)/shard_map/ppermute | solution.py:735
  57.9 21.8 %collective-permute-start.5 = (bf16[256,1536]{1,0:T(8,128)(2,1)}, bf16[256,1536]{1,0:T(8,128)(2,1)S(1)}, u32[]{:S(2)}, u32[]{:S(2)}) collective-permute-start(bf16[256,1536]{1,0:T(8,128)(2,1)} %get-tuple-element.51), channel_id=1, source_target_pairs={{0,2},{1,3},{2,0},{3,1},{4,6},{5,7},{6,4},{7,5},{8,10},{9,11},{10,... | collective-permute-start | bytes 2359304 | tf_op jit(solution)/shard_map/ppermute | solution.py:729
  59.6 20.7 %all-to-all-start.1 = ((bf16[8,256,128]{2,1,0:T(8,128)(2,1)}), bf16[8,256,128]{2,1,0:T(8,128)(2,1)S(1)}, u32[]{:S(2)}, u32[]{:S(2)}) async-start(bf16[8,256,128]{2,1,0:T(8,128)(2,1)} %chain_states.2), calls=%async_computation.1 | async-start | bytes 1048576 | tf_op jit(solution)/shard_map/all_to_all | solution.py:702
  79.6 2.4 %collective-permute-start.6 = (bf16[256,1536]{1,0:T(8,128)(2,1)S(1)}, bf16[256,1536]{1,0:T(8,128)(2,1)S(1)}, u32[]{:S(2)}, u32[]{:S(2)}) collective-permute-start(bf16[256,1536]{1,0:T(8,128)(2,1)S(1)} %collective-permute-done.5.refs_6_), channel_id=1, source_target_pairs={{0,1},{1,0},{2,3},{3,2},{4,5},{5,4},{6,7},{7,6},{8,9},{9,8},{10,11... | collective-permute-start | bytes 2359304 | tf_op jit(solution)/shard_map/ppermute | solution.py:735
  92.5 20.8 %all-to-all-start.2 = ((bf16[8,256,128]{2,1,0:T(8,128)(2,1)}), bf16[8,256,128]{2,1,0:T(8,128)(2,1)S(1)}, u32[]{:S(2)}, u32[]{:S(2)}) async-start(bf16[8,256,128]{2,1,0:T(8,128)(2,1)} %bitcast.3), calls=%async_computation.2 | async-start | bytes 1048576 | tf_op jit(solution)/shard_map/all_to_all | solution.py:702
  114.8 19.2 %all-to-all-start.3 = ((bf16[8,256,128]{2,1,0:T(8,128)(2,1)}), bf16[8,256,128]{2,1,0:T(8,128)(2,1)S(1)}, u32[]{:S(2)}, u32[]{:S(2)}) async-start(bf16[8,256,128]{2,1,0:T(8,128)(2,1)} %chain_states.3), calls=%async_computation.3 | async-start | bytes 1048576 | tf_op jit(solution)/shard_map/all_to_all | solution.py:702

commit v6 on v5

--- a/solution.py
+++ b/solution.py
@@ -315,19 +315,46 @@
     return near.astype(BF16)
 
 
-def far_body(chips, blks, direct, *refs):
+def far_products(blks, held, w_ref, near_ref, q_ref, cum_ref, prior_ref, before_ref, total_ref, grad_ref, sums_ref, side, ahead, after_group, ready):
+    _, groups, group, _ = cum_ref.shape
+    wide = group * HD
+
+    def product(g):
+        ready(g)
+        return far_grad(near_ref[:, lanes_of(g, wide)], held, w_ref, g, wide, side)
+
+    def sums_of(g, grad):
+        sums_refs = [sums_ref.at[n] for n in range(len(blks))]
+        far_sums(blks, g, group, q_ref, cum_ref, prior_ref, grad, before_ref, sums_refs, total_ref)
+
+    grad_ref[:, :wide] = product(0)
+
+    def step(g):
+        ahead(g + 3)
+        mine = grad_ref[:, lanes_of(g, wide)]
+        grad = product(g + 1)
+        sums_of(g, mine)
+        grad_ref[:, lanes_of(g + 1, wide)] = grad
+        after_group(g)
+
+    loop(groups - 1, step)
+    sums_of(groups - 1, grad_ref[:, lanes_of(groups - 1, wide)])
+    after_group(groups - 1)
+
+
+def far_body(chips, blks, keep, *refs):
     count = len(blks)
     if blks[0]:
         before_hbm, refs = refs[0], refs[1:]
     near_hbm, q_hbm, cum_ref, prior_ref, w_hbm, *refs = refs
     pieces, refs = refs[: 2 * (chips - 1)], refs[2 * (chips - 1) :]
-    total_ref, grad_hbm, *sums_hbm = refs[: 2 + count]
-    refs = refs[2 + count :]
-    if direct:
-        held, total_hbm = pieces, None
-    else:
-        held, total_hbm, total_ref, refs = refs[: len(pieces)], total_ref, refs[len(pieces)], refs[len(pieces) + 1 :]
-    w_ref, near_ref, q_ref, grad_ref, before_ref, sums_ref, piece_sems, load_sems, store_sems = refs
+    (total_out, grad_hbm, *sums_hbm), refs = refs[: 2 + count], refs[2 + count :]
+    if keep:
+        (last_near_ref, last_q_ref), refs = refs[:2], refs[2:]
+    w_ref, refs = refs[0], refs[1:]
+    held, refs = refs[: len(pieces)], refs[len(pieces) :]
+    total_ref, near_ref, q_ref, grad_ref, before_ref, sums_ref, piece_sems, load_sems, store_sems = refs
+    total_ref = total_out if keep else total_ref
     rows, depth = pieces[0].shape
     _, groups, group, _ = cum_ref.shape
     wide = group * HD
@@ -352,67 +379,55 @@
         return found
 
     def piece_loads():
-        if direct:
+        return [copy_of(piece, held[n], piece_sems.at[n]) for n, piece in enumerate(pieces)]
+
+    def last_loads():
+        if not keep:
             return ()
-        return [copy_of(piece, held[n], piece_sems.at[n]) for n, piece in enumerate(pieces)]
-
-    def store(g):
-        lanes = lanes_of(g, wide)
-        return copy_of(grad_ref.at[:, lanes], grad_hbm.at[:, lanes], store_sems.at[count, g])
-
-    def sums_stores(g):
-        these = pl.ds(g * group, group)
-        found = [copy_of(sums_ref.at[n, these], sums_hbm[n].at[these], store_sems.at[n, g]) for n in range(count)]
-        if total_hbm is not None:
-            found.append(copy_of(total_ref.at[these], total_hbm.at[these], store_sems.at[count + 1, g]))
+        block = pl.ds(blks[0] * BLK + rows, BLK)
+        return (
+            copy_of(near_hbm.at[block], last_near_ref, piece_sems.at[len(pieces)]),
+            copy_of(q_hbm.at[block], last_q_ref, piece_sems.at[len(pieces) + 1]),
+        )
+
+    def stores(g):
+        these, lanes = pl.ds(g * group, group), lanes_of(g, wide)
+        found = [copy_of(grad_ref.at[:, lanes], grad_hbm.at[:, lanes], store_sems.at[count, g])]
+        found += [copy_of(sums_ref.at[n, these], sums_hbm[n].at[these], store_sems.at[n, g]) for n in range(count)]
+        if not keep:
+            found.append(copy_of(total_ref.at[these], total_out.at[these], store_sems.at[count + 1, g]))
         return found
 
-    def product(g):
-        for copy in loads(g):
+    def start(copies):
+        for copy in copies:
+            copy.start()
+
+    def wait(copies):
+        for copy in copies:
             copy.wait()
-        return far_grad(near_ref[:, lanes_of(g, wide)], held, w_ref, g, wide, side)
-
-    def sums_of(g, grad):
-        far_sums(
-            blks, g, group, q_ref, cum_ref, prior_ref, grad, before_ref if blks[0] else None,
-            [sums_ref.at[n] for n in range(count)], total_ref,
-        )
-
-    for copy in loads(0):
-        copy.start()
-    for copy in piece_loads():
-        copy.start()
-    for copy in loads(1):
-        copy.start()
-    for copy in piece_loads():
-        copy.wait()
-    for copy in loads(2) if groups > 2 else ():
-        copy.start()
-    grad_ref[:, :wide] = product(0)
-    store(0).start()
-
-    def step(g):
-        @pl.when(g + 3 < groups)
+
+    def ahead(g):
+        @pl.when(g < groups)
         def _():
-            for copy in loads(g + 3):
-                copy.start()
-
-        mine = grad_ref[:, lanes_of(g, wide)]
-        grad = product(g + 1)
-        sums_of(g, mine)
-        grad_ref[:, lanes_of(g + 1, wide)] = grad
-        store(g + 1).start()
-        for copy in sums_stores(g):
-            copy.start()
-
-    loop(groups - 1, step)
-    sums_of(groups - 1, grad_ref[:, lanes_of(groups - 1, wide)])
-    for copy in sums_stores(groups - 1):
-        copy.start()
+            start(loads(g))
+
+        @pl.when(g == groups)
+        def _():
+            start(last_loads())
+
+    start(loads(0))
+    start(piece_loads())
+    start(loads(1))
+    wait(piece_loads())
+    if groups > 2:
+        start(loads(2))
+    far_products(
+        blks, held, w_ref, near_ref, q_ref, cum_ref, prior_ref, before_ref if blks[0] else None, total_ref, grad_ref,
+        sums_ref, side, ahead, lambda g: start(stores(g)), lambda g: wait(loads(g)),
+    )
+    wait(last_loads())
     for g in range(groups):
-        store(g).wait()
-        for copy in sums_stores(g):
-            copy.wait()
+        wait(stores(g))
 
 
 def far_product(start, before, pieces, weight, near, queries, cum, prior):
@@ -423,33 +438,85 @@
     chips = len(pieces) // 2 + 1
     count = rows // BLK
     blks = list(range(start, start + count))
-    last = start + count == blk_count
+    keep = start + count == blk_count - 1
     states = (heads, HD, HD)
     far_depth = 2 * (chips - 1) * depth
-    total, grad, *sums = call(
-        functools.partial(far_body, chips, blks, last),
+    kept = [((BLK, width), F32, VMEM), ((BLK, width), BF16, VMEM), ((width, far_depth), BF16, VMEM)]
+    total, grad, *rest = call(
+        functools.partial(far_body, chips, blks, keep),
         "far_product",
         ([(before, HBM)] if start else [])
         + [(near, HBM), (queries, HBM), (cum, VMEM), (prior, SMEM), (weight, HBM)]
-        + [(piece, VMEM if last else ANY) for piece in pieces],
-        [(states, BF16 if last else F32, VMEM if last else HBM), ((rows, width), BF16, HBM)] + [(states, F32, HBM)] * count,
-        ([] if last else [pltpu.VMEM(piece.shape, BF16) for piece in pieces] + [pltpu.VMEM(states, F32)])
+        + [(piece, ANY) for piece in pieces],
+        [(states, F32, VMEM if keep else HBM), ((rows, width), BF16, HBM)]
+        + [(states, F32, HBM)] * count
+        + (kept if keep else []),
+        ([] if keep else [pltpu.VMEM((width, far_depth), BF16)])
+        + [pltpu.VMEM(piece.shape, BF16) for piece in pieces]
         + [
-            pltpu.VMEM((width, far_depth), BF16),
+            pltpu.VMEM(states, F32),
             pltpu.VMEM((rows, width), F32),
             pltpu.VMEM((rows, width), BF16),
             pltpu.VMEM((rows, width), BF16),
             pltpu.VMEM(states, F32),
             pltpu.VMEM((count, *states), F32),
-            pltpu.SemaphoreType.DMA((len(pieces),)),
+            pltpu.SemaphoreType.DMA((len(pieces) + 2,)),
             pltpu.SemaphoreType.DMA((chips + 2, groups)),
             pltpu.SemaphoreType.DMA((count + 2, groups)),
         ],
-        36,
+        24 if keep else 36,
         cost(
             2 * rows * width * (far_depth + HD),
             2 * far_depth * (rows + width) + 8 * rows * width + 12 * width * HD,
         ),
+    )
+    return grad, rest[:count], total, rest[count:]
+
+
+def last_body(blk, before_ref, near_ref, q_ref, w_ref, cum_ref, prior_ref, *refs):
+    pieces, (total_ref, grad_hbm, sums_hbm, grad_ref, sums_ref, sems) = refs[:-6], refs[-6:]
+    _, groups, group, _ = cum_ref.shape
+    wide = group * HD
+
+    def stores(g):
+        these, lanes = pl.ds(g * group, group), lanes_of(g, wide)
+        return (
+            copy_of(grad_ref.at[:, lanes], grad_hbm.at[:, lanes], sems.at[0, g]),
+            copy_of(sums_ref.at[0, these], sums_hbm.at[these], sems.at[1, g]),
+        )
+
+    def after_group(g):
+        for copy in stores(g):
+            copy.start()
+
+    far_products(
+        [blk], pieces, w_ref, near_ref, q_ref, cum_ref, prior_ref, before_ref, total_ref, grad_ref,
+        sums_ref, lax.rem(lax.axis_index("tp"), 2), lambda g: None, after_group, lambda g: None,
+    )
+    for g in range(groups):
+        for copy in stores(g):
+            copy.wait()
+
+
+def last_product(before, near, queries, weight, pieces, cum, prior):
+    rows, depth = pieces[0].shape
+    blk_count, groups, group, _ = cum.shape
+    heads = groups * group
+    width = heads * HD
+    states = (heads, HD, HD)
+    total, grad, sums = call(
+        functools.partial(last_body, blk_count - 1),
+        "last_product",
+        [(before, VMEM), (near, VMEM), (queries, VMEM), (weight, VMEM), (cum, VMEM), (prior, SMEM)]
+        + [(piece, VMEM) for piece in pieces],
+        [(states, BF16, VMEM), ((rows, width), BF16, HBM), (states, F32, HBM)],
+        [
+            pltpu.VMEM((rows, width), BF16),
+            pltpu.VMEM((1, *states), F32),
+            pltpu.SemaphoreType.DMA((2, groups)),
+        ],
+        8,
+        cost(0, 0),
     )
     return grad, sums, total
 
@@ -718,10 +785,10 @@
         return [(i, (i + 2 * hops) % tp) for i in range(tp)]
 
     own = grad_output
-    sibling = lax.ppermute(own, "tp", core)
     starts = [0, 1, blk_count - 1, blk_count]
     cuts = [(a * BLK, b * BLK) for a, b in zip(starts, starts[1:])]
     head_rows = own[: cuts[0][1]]
+    sibling = lax.ppermute(after(own, head_rows), "tp", core)
     local_enter, fwd_total, cum, pair_cum, rest = key_totals(
         key_vectors, value_vectors, after(log_decay, head_rows), own, cuts[1:], seq
     )
@@ -738,8 +805,8 @@
     end = cum[:, :, :, BLK - 1].reshape(blk_count, heads)
     prior = jnp.exp(jnp.cumsum(end, axis=0) - end).T
 
-    arrived = hand_on(0, fwd_total)
-    near = near_product(own, after(sibling, arrived[0]), out_weight)
+    near = near_product(own, sibling, out_weight)
+    arrived = hand_on(0, near)
     fwd_got = after(fwd_got, near)
 
     share = heads * HD // seq
@@ -749,14 +816,16 @@
     fwd_out = chain(fwd_got, mine, share, False)
     enter_fwd = swap(fwd_out).reshape(heads, HD, HD)
 
-    grads, sums, total, cum_now = [], [], None, after(pair_cum, fwd_out)
-    for part, start in enumerate(starts[:-1]):
-        if part:
-            arrived = hand_on(part, total)
-            cum_now = after(pair_cum, enter_fwd) if part == 2 else pair_cum
-        grad, some, total = far_product(start, total, arrived, out_weight, near, queries, cum_now, prior)
-        grads += [(j, grad) for j in range(grad.shape[0] // BLK)]
-        sums += some
+    first_grad, sums, total, _ = far_product(
+        0, None, arrived, out_weight, near, queries, after(pair_cum, fwd_out), prior
+    )
+    arrived = hand_on(1, total)
+    next_grad, next_sums, total, kept = far_product(
+        1, total, arrived, out_weight, near, queries, pair_cum, prior
+    )
+    last_grad, last_sums, total = last_product(total, *kept, hand_on(2, next_grad), pair_cum, prior)
+    grads = [(0, first_grad)] + [(j, next_grad) for j in range(blk_count - 2)] + [(0, last_grad)]
+    sums = [*sums, *next_sums, last_sums]
     gq, parts = None, []
 
     bwd_got = swap(total)

time: 146 us -> 144 us (0.986)
  Pallas kernels: 106 us -> 104 us
    pallas_call x10, Pallas kernels: 106 us -> 104 us  [call(): pl.pallas_call(body, in_specs=[spec for _, spec in ins], out_specs=[spec...]
  transfers between devices with their start and end apart: 11 -> 11, of which waited for: 6 -> 5; matrix products, arithmetic and copies ran while one was open for 2% -> 0% of each run, Pallas kernels for 57% -> 63%
where the time goes in v6:
time: 144 us; the launch traced here: 143 us
  Pallas kernels  104 us (72%)
  starting transfers between devices  28 us (19%)
  waiting for transfers between devices  7.87 us (5%)
  local copies, waits for them, and re-layouts  2.43 us (2%)
    pallas_call x10, Pallas kernels, call(): pl.pallas_call(body, in_specs=[spec for _, spec in ins], out_specs=[spec...  104 us
    all_to_all x4, starting transfers between devices, swap(): lax.all_to_all(flat, 'seq', 0, 0, tiled=True).reshape(devices, -1, HD)  22.6 us
    ppermute x3, starting transfers between devices, local(): lax.ppermute(x, 'tp', from_chip(d))  4.77 us
    ppermute x3, waiting for transfers between devices, local(): lax.ppermute(x, 'tp', from_chip(d))  3.76 us
  transfers between devices with their start and end apart: 11, of which 5 were waited for; matrix products, arithmetic and copies ran while one was open for 0% of the time, Pallas kernels for 63%

profile of v6, /device:TPU:0, one launch (start us, length us, event | category | flops | bytes accessed | tf_op | source)
XLA Modules:
  0.0 143.0 jit_solution(1932427579699999021)
XLA Ops:
  0.6 2.1 %slice.9 = bf16[256,1536]{1,0:T(8,128)(2,1)} slice(bf16[1024,1536]{1,0:T(8,128)(2,1)} %grad_hbm.1), slice={[0:256], [0:1536]} | slice | bytes 1572864 | tf_op jit(solution)/shard_map/slice | solution.py:790
  2.7 0.5 collective-permute-start
  3.1 2.5 %collective-permute-start.1 = (bf16[256,1536]{1,0:T(8,128)(2,1)}, bf16[256,1536]{1,0:T(8,128)(2,1)S(1)}, u32[]{:S(2)}, u32[]{:S(2)}) collective-permute-start(bf16[256,1536]{1,0:T(8,128)(2,1)} %slice.9), channel_id=1, source_target_pairs={{0,2},{1,3},{2,0},{3,1},{4,6},{5,7},{6,4},{7,5},{8,10},{9,11},{10,... | collective-permute-start | bytes 2359304 | tf_op jit(solution)/shard_map/ppermute | solution.py:796
  5.7 9.5 %key_totals.1 = (f32[4,16,128,128]{3,2,1,0:T(8,128)}, bf16[8,272,128]{2,1,0:T(8,128)(2,1)}, f32[4,4,4,256]{3,2,1,0:T(4,128)S(1)}, f32[4,8,2,256]{3,2,1,0:T(2,128...) custom-call(bf16[1024,2048]{1,0:T(8,128)(2,1)} %k_hbm.7, bf16[1024,2048]{1,0:T(8,128)(2,1)} %v_hbm.7, ...), custom_call_target="tpu_custom_call" | custom-call | flops 536870912 | bytes 12582912 | tf_op jit(solution)/shard_map/key_totals/pallas_call | solution.py:42
  15.1 5.8 %all-to-all-start = ((bf16[8,272,128]{2,1,0:T(8,128)(2,1)}), bf16[8,272,128]{2,1,0:T(8,128)(2,1)S(1)}, u32[]{:S(2)}, u32[]{:S(2)}) async-start(bf16[8,272,128]{2,1,0:T(8,128)(2,1)} %get-tuple-element.42), calls=%async_computation | async-start | bytes 1114112 | tf_op jit(solution)/shard_map/all_to_all | solution.py:769
  21.0 0.5 collective-permute-start.3
  21.5 0.0 collective-permute-done.sibling_hbm
  21.5 19.5 %near_product.1.refs_0_.refs_1_ = f32[1024,2048]{1,0:T(8,128)} custom-call(bf16[1024,1536]{1,0:T(8,128)(2,1)} %grad_hbm.1, bf16[1024,1536]{1,0:T(8,128)(2,1)} %collective-permute-done.sibling_hbm, bf16[2048,6144]{1,0:T(8,128)(2,1)} %refs_5_.1), custom_call_target="tpu_custom_call" | custom-call | flops 12884901888 | bytes 27262976 | tf_op jit(solution)/shard_map/near_product/pallas_call | solution.py:42
  41.0 0.1 collective-permute-start.2
  41.1 0.1 slice.11
  41.2 0.2 copy.14
  41.4 0.2 reduce_window_sum.11
  41.5 0.0 all-to-all-done.got_ref
  41.6 0.1 constant_dynamic-slice_fusion.weight_ref
  41.7 1.5 %chain_states.2 = bf16[8,256,128]{2,1,0:T(8,128)(2,1)} custom-call(bf16[8,272,128]{2,1,0:T(8,128)(2,1)S(1)} %all-to-all-done.got_ref, f32[8,2]{1,0:T(8,128)S(1)} %constant_dynamic-slice_fusion.weight_ref), custom_call_target="tpu_custom_call" | custom-call | flops 524288 | bytes 1048576 | tf_op jit(solution)/shard_map/chain_states/pallas_call | solution.py:42
  43.1 0.3 collective-permute-done.2.refs_6_
  43.5 10.6 %far_product.2 = (f32[16,128,128]{2,1,0:T(8,128)}, bf16[256,2048]{1,0:T(8,128)(2,1)}, f32[16,128,128]{2,1,0:T(8,128)}) custom-call(f32[1024,2048]{1,0:T(8,128)} %near_product.1.refs_0_.refs_1_, bf16[1024,2048]{1,0:T(8,128)(2,1)} %q_hbm.3, f32[4,8,2,256]{3,2,1,0:T(2,128)S(1)} %get-tuple-element.44.refs_2_.refs_3_.cum_ref, ...), custom_call_target="tpu_custom_call" | custom-call | flops 3355443200 | bytes 21495808 | tf_op jit(solution)/shard_map/far_product/pallas_call | solution.py:42
  54.0 3.8 %collective-permute-done.3.refs_6_ = bf16[512,1536]{1,0:T(8,128)(2,1)S(1)} collective-permute-done((bf16[512,1536]{1,0:T(8,128)(2,1)}, bf16[512,1536]{1,0:T(8,128)(2,1)S(1)}, u32[]{:S(2)}, u32[]{:S(2)}) %collective-permute-start.3) | collective-permute-done | bytes 1572896 | tf_op jit(solution)/shard_map/ppermute | solution.py:796
  57.8 1.7 %collective-permute-start.5 = (bf16[256,1536]{1,0:T(8,128)(2,1)}, bf16[256,1536]{1,0:T(8,128)(2,1)S(1)}, u32[]{:S(2)}, u32[]{:S(2)}) collective-permute-start(bf16[256,1536]{1,0:T(8,128)(2,1)} %get-tuple-element.55), channel_id=1, source_target_pairs={{0,2},{1,3},{2,0},{3,1},{4,6},{5,7},{6,4},{7,5},{8,10},{9,11},{10,... | collective-permute-start | bytes 2359304 | tf_op jit(solution)/shard_map/ppermute | solution.py:796
  59.5 5.8 %all-to-all-start.2 = ((bf16[8,256,128]{2,1,0:T(8,128)(2,1)}), bf16[8,256,128]{2,1,0:T(8,128)(2,1)S(1)}, u32[]{:S(2)}, u32[]{:S(2)}) async-start(bf16[8,256,128]{2,1,0:T(8,128)(2,1)} %chain_states.2), calls=%async_computation.2 | async-start | bytes 1048576 | tf_op jit(solution)/shard_map/all_to_all | solution.py:769
  65.4 14.2 %far_product.3 = (f32[16,128,128]{2,1,0:T(8,128)S(1)}, bf16[512,2048]{1,0:T(8,128)(2,1)}, f32[16,128,128]{2,1,0:T(8,128)}, f32[16,128,128]{2,1,0:T(8,128)}, f32[...) custom-call(f32[16,128,128]{2,1,0:T(8,128)} %get-tuple-element.47.refs_0_, ...), custom_call_target="tpu_custom_call" | custom-call | flops 6710886400 | bytes 27262976 | tf_op jit(solution)/shard_map/far_product/pallas_call | solution.py:42
  79.6 0.1 collective-permute-start.6
  79.6 2.3 %collective-permute-done.6.refs_1_ = bf16[256,1536]{1,0:T(8,128)(2,1)S(1)} collective-permute-done((bf16[256,1536]{1,0:T(8,128)(2,1)S(1)}, bf16[256,1536]{1,0:T(8,128)(2,1)S(1)}, u32[]{:S(2)}, u32[]{:S(2)}) %collective-permute-start.6) | collective-permute-done | bytes 786464 | tf_op jit(solution)/shard_map/ppermute | solution.py:802
  81.9 7.7 %last_product.1 = (bf16[16,128,128]{2,1,0:T(8,128)(2,1)}, bf16[256,2048]{1,0:T(8,128)(2,1)}, f32[16,128,128]{2,1,0:T(8,128)}) custom-call(f32[16,128,128]{2,1,0:T(8,128)S(1)} %get-tuple-element.51.before_ref, f32[256,2048]{1,0:T(8,128)S(1)} %get-tuple-element.52.near_ref, bf16[256,2048]{1,0:T(8,128)(2,1)S(1)} %get-tuple-element.53.q_ref, ...), custom_call_target="tpu_custom_call" | custom-call | tf_op jit(solution)/shard_map/last_product/pallas_call | solution.py:42
  89.6 6.0 %all-to-all-start.1 = ((bf16[8,256,128]{2,1,0:T(8,128)(2,1)}), bf16[8,256,128]{2,1,0:T(8,128)(2,1)S(1)}, u32[]{:S(2)}, u32[]{:S(2)}) async-start(bf16[8,256,128]{2,1,0:T(8,128)(2,1)} %bitcast.2), calls=%async_computation.1 | async-start | bytes 1048576 | tf_op jit(solution)/shard_map/all_to_all | solution.py:769
  95.6 13.7 %block_terms.2 = (bf16[1024,2048]{1,0:T(8,128)(2,1)}, bf16[512,2048]{1,0:T(8,128)(2,1)}, bf16[512,2048]{1,0:T(8,128)(2,1)}) custom-call(bf16[1024,2048]{1,0:T(8,128)(2,1)} %q_hbm.3, bf16[1024,2048]{1,0:T(8,128)(2,1)} %k_hbm.7, bf16[1024,2048]{1,0:T(8,128)(2,1)} %v_hbm.7, bf16[256,2048]{1,0:T(8,128)(2,1)} %get-tuple-element.59.refs_0_, ...), custom_call_target="tpu_custom_call" | custom-call | flops 2952790016 | bytes 17825792 | tf_op jit(solution)/shard_map/block_terms/pallas_call | solution.py:42
  109.4 1.0 all-to-all-done.1.got_ref
  110.4 1.5 %chain_states.3 = bf16[8,256,128]{2,1,0:T(8,128)(2,1)} custom-call(bf16[8,256,128]{2,1,0:T(8,128)(2,1)S(1)} %all-to-all-done.1.got_ref, f32[8,2]{1,0:T(8,128)S(1)} %constant_dynamic-slice_fusion.weight_ref), custom_call_target="tpu_custom_call" | custom-call | flops 524288 | bytes 1048576 | tf_op jit(solution)/shard_map/chain_states/pallas_call | solution.py:42
  111.9 5.0 %all-to-all-start.3 = ((bf16[8,256,128]{2,1,0:T(8,128)(2,1)}), bf16[8,256,128]{2,1,0:T(8,128)(2,1)S(1)}, u32[]{:S(2)}, u32[]{:S(2)}) async-start(bf16[8,256,128]{2,1,0:T(8,128)(2,1)} %chain_states.3), calls=%async_computation.3 | async-start | bytes 1048576 | tf_op jit(solution)/shard_map/all_to_all | solution.py:769
  116.9 13.8 %block_terms.3 = (bf16[1024,2048]{1,0:T(8,128)(2,1)}, bf16[512,2048]{1,0:T(8,128)(2,1)}, bf16[512,2048]{1,0:T(8,128)(2,1)}) custom-call(bf16[1024,2048]{1,0:T(8,128)(2,1)} %q_hbm.3, bf16[1024,2048]{1,0:T(8,128)(2,1)} %k_hbm.7, bf16[1024,2048]{1,0:T(8,128)(2,1)} %v_hbm.7, ...), custom_call_target="tpu_custom_call", output_to_operand_aliasing={{0}: (9, {})} | custom-call | flops 2952790016 | bytes 17825792 | tf_op jit(solution)/shard_map/block_terms/pallas_call | solution.py:42
  130.7 0.5 all-to-all-done.3
  131.2 11.7 %later_terms.1 = (bf16[1024,2048]{1,0:T(8,128)(2,1)}, bf16[1024,2048]{1,0:T(8,128)(2,1)}) custom-call(bf16[1024,2048]{1,0:T(8,128)(2,1)} %k_hbm.7, bf16[1024,2048]{1,0:T(8,128)(2,1)} %v_hbm.7, f32[4,4,4,256]{3,2,1,0:T(4,128)S(1)} %get-tuple-element.64.refs_2_.cum_ref, bf16[16,128,128]{2,1,0:T(8,128)(2,1)S(1)} %bitcast.8, ...), custom_call_target="tpu_custom_call" | custom-call | flops 1073741824 | bytes 29360128 | tf_op jit(solution)/shard_map/later_terms/pallas_call | solution.py:42
  (8 shorter events, 0.0 us)
Async XLA Ops:
  2.7 18.8 %collective-permute-start = (bf16[1024,1536]{1,0:T(8,128)(2,1)}, bf16[1024,1536]{1,0:T(8,128)(2,1)}, u32[]{:S(2)}, u32[]{:S(2)}) collective-permute-start(bf16[1024,1536]{1,0:T(8,128)(2,1)} %grad_hbm.1), channel_id=1, source_target_pairs={{0,1},{1,0},{2,3},{3,2},{4,5},{5,4},{6,7},{7,6},{8,9},{9,8},{10,11... | collective-permute-start | bytes 9437192 | tf_op jit(solution)/shard_map/ppermute | solution.py:791
  3.1 37.8 %collective-permute-start.1 = (bf16[256,1536]{1,0:T(8,128)(2,1)}, bf16[256,1536]{1,0:T(8,128)(2,1)S(1)}, u32[]{:S(2)}, u32[]{:S(2)}) collective-permute-start(bf16[256,1536]{1,0:T(8,128)(2,1)} %slice.9), channel_id=1, source_target_pairs={{0,2},{1,3},{2,0},{3,1},{4,6},{5,7},{6,4},{7,5},{8,10},{9,11},{10,... | collective-permute-start | bytes 2359304 | tf_op jit(solution)/shard_map/ppermute | solution.py:796
  15.1 26.4 %all-to-all-start = ((bf16[8,272,128]{2,1,0:T(8,128)(2,1)}), bf16[8,272,128]{2,1,0:T(8,128)(2,1)S(1)}, u32[]{:S(2)}, u32[]{:S(2)}) async-start(bf16[8,272,128]{2,1,0:T(8,128)(2,1)} %get-tuple-element.42), calls=%async_computation | async-start | bytes 1114112 | tf_op jit(solution)/shard_map/all_to_all | solution.py:769
  21.0 36.8 %collective-permute-start.3 = (bf16[512,1536]{1,0:T(8,128)(2,1)}, bf16[512,1536]{1,0:T(8,128)(2,1)S(1)}, u32[]{:S(2)}, u32[]{:S(2)}) collective-permute-start(bf16[512,1536]{1,0:T(8,128)(2,1)} %get-tuple-element.48), channel_id=1, source_target_pairs={{0,2},{1,3},{2,0},{3,1},{4,6},{5,7},{6,4},{7,5},{8,10},{9,11},{10,... | collective-permute-start | bytes 4718600 | tf_op jit(solution)/shard_map/ppermute | solution.py:796
  41.0 2.5 %collective-permute-start.2 = (bf16[256,1536]{1,0:T(8,128)(2,1)S(1)}, bf16[256,1536]{1,0:T(8,128)(2,1)}, u32[]{:S(2)}, u32[]{:S(2)}) collective-permute-start(bf16[256,1536]{1,0:T(8,128)(2,1)S(1)} %collective-permute-done.1.refs_5_), channel_id=1, source_target_pairs={{0,1},{1,0},{2,3},{3,2},{4,5},{5,4},{6,7},{7,6},{8,9},{9,8},{10,11... | collective-permute-start | bytes 2359304 | tf_op jit(solution)/shard_map/ppermute | solution.py:802
  57.8 7.6 %collective-permute-start.4 = (bf16[512,1536]{1,0:T(8,128)(2,1)S(1)}, bf16[512,1536]{1,0:T(8,128)(2,1)}, u32[]{:S(2)}, u32[]{:S(2)}) collective-permute-start(bf16[512,1536]{1,0:T(8,128)(2,1)S(1)} %collective-permute-done.3.refs_6_), channel_id=1, source_target_pairs={{0,1},{1,0},{2,3},{3,2},{4,5},{5,4},{6,7},{7,6},{8,9},{9,8},{10,11... | collective-permute-start | bytes 4718600 | tf_op jit(solution)/shard_map/ppermute | solution.py:802
  57.8 21.8 %collective-permute-start.5 = (bf16[256,1536]{1,0:T(8,128)(2,1)}, bf16[256,1536]{1,0:T(8,128)(2,1)S(1)}, u32[]{:S(2)}, u32[]{:S(2)}) collective-permute-start(bf16[256,1536]{1,0:T(8,128)(2,1)} %get-tuple-element.55), channel_id=1, source_target_pairs={{0,2},{1,3},{2,0},{3,1},{4,6},{5,7},{6,4},{7,5},{8,10},{9,11},{10,... | collective-permute-start | bytes 2359304 | tf_op jit(solution)/shard_map/ppermute | solution.py:796
  59.5 30.1 %all-to-all-start.2 = ((bf16[8,256,128]{2,1,0:T(8,128)(2,1)}), bf16[8,256,128]{2,1,0:T(8,128)(2,1)S(1)}, u32[]{:S(2)}, u32[]{:S(2)}) async-start(bf16[8,256,128]{2,1,0:T(8,128)(2,1)} %chain_states.2), calls=%async_computation.2 | async-start | bytes 1048576 | tf_op jit(solution)/shard_map/all_to_all | solution.py:769
  79.6 2.4 %collective-permute-start.6 = (bf16[256,1536]{1,0:T(8,128)(2,1)S(1)}, bf16[256,1536]{1,0:T(8,128)(2,1)S(1)}, u32[]{:S(2)}, u32[]{:S(2)}) collective-permute-start(bf16[256,1536]{1,0:T(8,128)(2,1)S(1)} %collective-permute-done.5.refs_0_), channel_id=1, source_target_pairs={{0,1},{1,0},{2,3},{3,2},{4,5},{5,4},{6,7},{7,6},{8,9},{9,8},{10,11... | collective-permute-start | bytes 2359304 | tf_op jit(solution)/shard_map/ppermute | solution.py:802
  89.6 20.8 %all-to-all-start.1 = ((bf16[8,256,128]{2,1,0:T(8,128)(2,1)}), bf16[8,256,128]{2,1,0:T(8,128)(2,1)S(1)}, u32[]{:S(2)}, u32[]{:S(2)}) async-start(bf16[8,256,128]{2,1,0:T(8,128)(2,1)} %bitcast.2), calls=%async_computation.1 | async-start | bytes 1048576 | tf_op jit(solution)/shard_map/all_to_all | solution.py:769
  111.9 19.3 %all-to-all-start.3 = ((bf16[8,256,128]{2,1,0:T(8,128)(2,1)}), bf16[8,256,128]{2,1,0:T(8,128)(2,1)S(1)}, u32[]{:S(2)}, u32[]{:S(2)}) async-start(bf16[8,256,128]{2,1,0:T(8,128)(2,1)} %chain_states.3), calls=%async_computation.3 | async-start | bytes 1048576 | tf_op jit(solution)/shard_map/all_to_all | solution.py:769

commit v7 on v6

--- a/solution.py
+++ b/solution.py
@@ -69,6 +69,25 @@
 
 def head_in(h):
     return slice(h * HD, (h + 1) * HD)
+
+
+def take_body(grad_hbm, out_ref, sems):
+    copy = copy_of(grad_hbm.at[pl.ds(0, out_ref.shape[0])], out_ref, sems.at[0])
+    copy.start()
+    copy.wait()
+
+
+def take_rows(grad, rows):
+    (out,) = call(
+        take_body,
+        "take_rows",
+        [(grad, HBM)],
+        [((rows, grad.shape[1]), BF16, VMEM)],
+        [pltpu.SemaphoreType.DMA((1,))],
+        1,
+        cost(0, 4 * rows * grad.shape[1]),
+    )
+    return out
 
 
 def prefix_sums(x):
@@ -787,7 +806,7 @@
     own = grad_output
     starts = [0, 1, blk_count - 1, blk_count]
     cuts = [(a * BLK, b * BLK) for a, b in zip(starts, starts[1:])]
-    head_rows = own[: cuts[0][1]]
+    head_rows = take_rows(own, cuts[0][1])
     sibling = lax.ppermute(after(own, head_rows), "tp", core)
     local_enter, fwd_total, cum, pair_cum, rest = key_totals(
         key_vectors, value_vectors, after(log_decay, head_rows), own, cuts[1:], seq

time: 144 us -> 143 us (level)
  local copies, waits for them, and re-layouts: 2.43 us -> 0.36 us
    slice x1 -> x0, local copies, waits for them, and re-layouts: 2.06 us -> none  [local(): head_rows = own[:cuts[0][1]]]
    pallas_call x10 -> x11, Pallas kernels: 104 us -> 104 us  [call(): pl.pallas_call(body, in_specs=[spec for _, spec in ins], out_specs=[spec...]
where the time goes in v7:
time: 143 us; the launch traced here: 142 us
  Pallas kernels  104 us (73%)
  starting transfers between devices  28.1 us (20%)
  waiting for transfers between devices  8.26 us (6%)
    pallas_call x11, Pallas kernels, call(): pl.pallas_call(body, in_specs=[spec for _, spec in ins], out_specs=[spec...  104 us
    all_to_all x4, starting transfers between devices, swap(): lax.all_to_all(flat, 'seq', 0, 0, tiled=True).reshape(devices, -1, HD)  22.6 us
    ppermute x3, starting transfers between devices, local(): lax.ppermute(x, 'tp', from_chip(d))  4.86 us
    ppermute x3, waiting for transfers between devices, local(): lax.ppermute(x, 'tp', from_chip(d))  4.08 us
  transfers between devices with their start and end apart: 11, of which 5 were waited for; matrix products, arithmetic and copies ran while one was open for 0% of the time, Pallas kernels for 63%

profile of v7, /device:TPU:0, one launch (start us, length us, event | category | flops | bytes accessed | tf_op | source)
XLA Modules:
  0.0 142.0 jit_solution(14699574253341921241)
XLA Ops:
  0.6 1.1 take_rows.1
  1.8 0.5 collective-permute-start
  2.3 2.6 %collective-permute-start.1 = (bf16[256,1536]{1,0:T(8,128)(2,1)S(1)}, bf16[256,1536]{1,0:T(8,128)(2,1)}, u32[]{:S(2)}, u32[]{:S(2)}) collective-permute-start(bf16[256,1536]{1,0:T(8,128)(2,1)S(1)} %take_rows.1), channel_id=1, source_target_pairs={{0,2},{1,3},{2,0},{3,1},{4,6},{5,7},{6,4},{7,5},{8,10},{9,11},{10,... | collective-permute-start | bytes 2359304 | tf_op jit(solution)/shard_map/ppermute | solution.py:815
  4.9 9.5 %key_totals.1 = (f32[4,16,128,128]{3,2,1,0:T(8,128)}, bf16[8,272,128]{2,1,0:T(8,128)(2,1)}, f32[4,4,4,256]{3,2,1,0:T(4,128)S(1)}, f32[4,8,2,256]{3,2,1,0:T(2,128...) custom-call(bf16[1024,2048]{1,0:T(8,128)(2,1)} %k_hbm.7, bf16[1024,2048]{1,0:T(8,128)(2,1)} %v_hbm.7, ...), custom_call_target="tpu_custom_call" | custom-call | flops 536870912 | bytes 12582912 | tf_op jit(solution)/shard_map/key_totals/pallas_call | solution.py:42
  14.4 5.8 %all-to-all-start = ((bf16[8,272,128]{2,1,0:T(8,128)(2,1)}), bf16[8,272,128]{2,1,0:T(8,128)(2,1)S(1)}, u32[]{:S(2)}, u32[]{:S(2)}) async-start(bf16[8,272,128]{2,1,0:T(8,128)(2,1)} %get-tuple-element.42), calls=%async_computation | async-start | bytes 1114112 | tf_op jit(solution)/shard_map/all_to_all | solution.py:788
  20.2 0.5 collective-permute-start.3
  20.7 19.5 %near_product.1.refs_0_.refs_1_ = f32[1024,2048]{1,0:T(8,128)} custom-call(bf16[1024,1536]{1,0:T(8,128)(2,1)} %grad_hbm.3, bf16[1024,1536]{1,0:T(8,128)(2,1)} %collective-permute-done.sibling_hbm, bf16[2048,6144]{1,0:T(8,128)(2,1)} %refs_5_.1), custom_call_target="tpu_custom_call" | custom-call | flops 12884901888 | bytes 27262976 | tf_op jit(solution)/shard_map/near_product/pallas_call | solution.py:42
  40.2 0.0 collective-permute-done.1.refs_5_
  40.2 0.1 collective-permute-start.2
  40.3 0.1 slice.7
  40.4 0.2 copy.14
  40.6 0.2 reduce_window_sum.11
  40.7 0.0 all-to-all-done.got_ref
  40.8 0.1 constant_dynamic-slice_fusion.weight_ref
  40.9 1.5 %chain_states.2 = bf16[8,256,128]{2,1,0:T(8,128)(2,1)} custom-call(bf16[8,272,128]{2,1,0:T(8,128)(2,1)S(1)} %all-to-all-done.got_ref, f32[8,2]{1,0:T(8,128)S(1)} %constant_dynamic-slice_fusion.weight_ref), custom_call_target="tpu_custom_call" | custom-call | flops 524288 | bytes 1048576 | tf_op jit(solution)/shard_map/chain_states/pallas_call | solution.py:42
  42.4 0.4 collective-permute-done.2.refs_6_
  42.8 9.9 %far_product.2 = (f32[16,128,128]{2,1,0:T(8,128)}, bf16[256,2048]{1,0:T(8,128)(2,1)}, f32[16,128,128]{2,1,0:T(8,128)}) custom-call(f32[1024,2048]{1,0:T(8,128)} %near_product.1.refs_0_.refs_1_, bf16[1024,2048]{1,0:T(8,128)(2,1)} %q_hbm.3, f32[4,8,2,256]{3,2,1,0:T(2,128)S(1)} %get-tuple-element.44.refs_2_.refs_3_.cum_ref, ...), custom_call_target="tpu_custom_call" | custom-call | flops 3355443200 | bytes 21495808 | tf_op jit(solution)/shard_map/far_product/pallas_call | solution.py:42
  52.7 4.1 %collective-permute-done.3.refs_6_ = bf16[512,1536]{1,0:T(8,128)(2,1)S(1)} collective-permute-done((bf16[512,1536]{1,0:T(8,128)(2,1)}, bf16[512,1536]{1,0:T(8,128)(2,1)S(1)}, u32[]{:S(2)}, u32[]{:S(2)}) %collective-permute-start.3) | collective-permute-done | bytes 1572896 | tf_op jit(solution)/shard_map/ppermute | solution.py:815
  56.7 1.8 %collective-permute-start.5 = (bf16[256,1536]{1,0:T(8,128)(2,1)}, bf16[256,1536]{1,0:T(8,128)(2,1)S(1)}, u32[]{:S(2)}, u32[]{:S(2)}) collective-permute-start(bf16[256,1536]{1,0:T(8,128)(2,1)} %get-tuple-element.55), channel_id=1, source_target_pairs={{0,2},{1,3},{2,0},{3,1},{4,6},{5,7},{6,4},{7,5},{8,10},{9,11},{10,... | collective-permute-start | bytes 2359304 | tf_op jit(solution)/shard_map/ppermute | solution.py:815
  58.5 5.8 %all-to-all-start.2 = ((bf16[8,256,128]{2,1,0:T(8,128)(2,1)}), bf16[8,256,128]{2,1,0:T(8,128)(2,1)S(1)}, u32[]{:S(2)}, u32[]{:S(2)}) async-start(bf16[8,256,128]{2,1,0:T(8,128)(2,1)} %chain_states.2), calls=%async_computation.2 | async-start | bytes 1048576 | tf_op jit(solution)/shard_map/all_to_all | solution.py:788
  64.3 14.2 %far_product.3 = (f32[16,128,128]{2,1,0:T(8,128)S(1)}, bf16[512,2048]{1,0:T(8,128)(2,1)}, f32[16,128,128]{2,1,0:T(8,128)}, f32[16,128,128]{2,1,0:T(8,128)}, f32[...) custom-call(f32[16,128,128]{2,1,0:T(8,128)} %get-tuple-element.47.refs_0_, ...), custom_call_target="tpu_custom_call" | custom-call | flops 6710886400 | bytes 27262976 | tf_op jit(solution)/shard_map/far_product/pallas_call | solution.py:42
  78.5 0.1 collective-permute-start.6
  78.6 2.3 %collective-permute-done.6.refs_1_ = bf16[256,1536]{1,0:T(8,128)(2,1)S(1)} collective-permute-done((bf16[256,1536]{1,0:T(8,128)(2,1)S(1)}, bf16[256,1536]{1,0:T(8,128)(2,1)S(1)}, u32[]{:S(2)}, u32[]{:S(2)}) %collective-permute-start.6) | collective-permute-done | bytes 786464 | tf_op jit(solution)/shard_map/ppermute | solution.py:821
  80.9 7.7 %last_product.1 = (bf16[16,128,128]{2,1,0:T(8,128)(2,1)}, bf16[256,2048]{1,0:T(8,128)(2,1)}, f32[16,128,128]{2,1,0:T(8,128)}) custom-call(f32[16,128,128]{2,1,0:T(8,128)S(1)} %get-tuple-element.51.before_ref, f32[256,2048]{1,0:T(8,128)S(1)} %get-tuple-element.52.near_ref, bf16[256,2048]{1,0:T(8,128)(2,1)S(1)} %get-tuple-element.53.q_ref, ...), custom_call_target="tpu_custom_call" | custom-call | tf_op jit(solution)/shard_map/last_product/pallas_call | solution.py:42
  88.6 6.0 %all-to-all-start.1 = ((bf16[8,256,128]{2,1,0:T(8,128)(2,1)}), bf16[8,256,128]{2,1,0:T(8,128)(2,1)S(1)}, u32[]{:S(2)}, u32[]{:S(2)}) async-start(bf16[8,256,128]{2,1,0:T(8,128)(2,1)} %bitcast.2), calls=%async_computation.1 | async-start | bytes 1048576 | tf_op jit(solution)/shard_map/all_to_all | solution.py:788
  94.6 13.7 %block_terms.2 = (bf16[1024,2048]{1,0:T(8,128)(2,1)}, bf16[512,2048]{1,0:T(8,128)(2,1)}, bf16[512,2048]{1,0:T(8,128)(2,1)}) custom-call(bf16[1024,2048]{1,0:T(8,128)(2,1)} %q_hbm.3, bf16[1024,2048]{1,0:T(8,128)(2,1)} %k_hbm.7, bf16[1024,2048]{1,0:T(8,128)(2,1)} %v_hbm.7, bf16[256,2048]{1,0:T(8,128)(2,1)} %get-tuple-element.59.refs_0_, ...), custom_call_target="tpu_custom_call" | custom-call | flops 2952790016 | bytes 17825792 | tf_op jit(solution)/shard_map/block_terms/pallas_call | solution.py:42
  108.3 1.0 all-to-all-done.1.got_ref
  109.4 1.5 %chain_states.3 = bf16[8,256,128]{2,1,0:T(8,128)(2,1)} custom-call(bf16[8,256,128]{2,1,0:T(8,128)(2,1)S(1)} %all-to-all-done.1.got_ref, f32[8,2]{1,0:T(8,128)S(1)} %constant_dynamic-slice_fusion.weight_ref), custom_call_target="tpu_custom_call" | custom-call | flops 524288 | bytes 1048576 | tf_op jit(solution)/shard_map/chain_states/pallas_call | solution.py:42
  110.9 5.0 %all-to-all-start.3 = ((bf16[8,256,128]{2,1,0:T(8,128)(2,1)}), bf16[8,256,128]{2,1,0:T(8,128)(2,1)S(1)}, u32[]{:S(2)}, u32[]{:S(2)}) async-start(bf16[8,256,128]{2,1,0:T(8,128)(2,1)} %chain_states.3), calls=%async_computation.3 | async-start | bytes 1048576 | tf_op jit(solution)/shard_map/all_to_all | solution.py:788
  115.8 13.8 %block_terms.3 = (bf16[1024,2048]{1,0:T(8,128)(2,1)}, bf16[512,2048]{1,0:T(8,128)(2,1)}, bf16[512,2048]{1,0:T(8,128)(2,1)}) custom-call(bf16[1024,2048]{1,0:T(8,128)(2,1)} %q_hbm.3, bf16[1024,2048]{1,0:T(8,128)(2,1)} %k_hbm.7, bf16[1024,2048]{1,0:T(8,128)(2,1)} %v_hbm.7, ...), custom_call_target="tpu_custom_call", output_to_operand_aliasing={{0}: (9, {})} | custom-call | flops 2952790016 | bytes 17825792 | tf_op jit(solution)/shard_map/block_terms/pallas_call | solution.py:42
  129.6 0.5 all-to-all-done.3
  130.1 11.7 %later_terms.1 = (bf16[1024,2048]{1,0:T(8,128)(2,1)}, bf16[1024,2048]{1,0:T(8,128)(2,1)}) custom-call(bf16[1024,2048]{1,0:T(8,128)(2,1)} %k_hbm.7, bf16[1024,2048]{1,0:T(8,128)(2,1)} %v_hbm.7, f32[4,4,4,256]{3,2,1,0:T(4,128)S(1)} %get-tuple-element.64.refs_2_.cum_ref, bf16[16,128,128]{2,1,0:T(8,128)(2,1)S(1)} %bitcast.8, ...), custom_call_target="tpu_custom_call" | custom-call | flops 1073741824 | bytes 29360128 | tf_op jit(solution)/shard_map/later_terms/pallas_call | solution.py:42
  (8 shorter events, 0.0 us)
Async XLA Ops:
  1.8 18.9 %collective-permute-start = (bf16[1024,1536]{1,0:T(8,128)(2,1)}, bf16[1024,1536]{1,0:T(8,128)(2,1)}, u32[]{:S(2)}, u32[]{:S(2)}) collective-permute-start(bf16[1024,1536]{1,0:T(8,128)(2,1)} %grad_hbm.3), channel_id=1, source_target_pairs={{0,1},{1,0},{2,3},{3,2},{4,5},{5,4},{6,7},{7,6},{8,9},{9,8},{10,11... | collective-permute-start | bytes 9437192 | tf_op jit(solution)/shard_map/ppermute | solution.py:810
  2.3 37.9 %collective-permute-start.1 = (bf16[256,1536]{1,0:T(8,128)(2,1)S(1)}, bf16[256,1536]{1,0:T(8,128)(2,1)}, u32[]{:S(2)}, u32[]{:S(2)}) collective-permute-start(bf16[256,1536]{1,0:T(8,128)(2,1)S(1)} %take_rows.1), channel_id=1, source_target_pairs={{0,2},{1,3},{2,0},{3,1},{4,6},{5,7},{6,4},{7,5},{8,10},{9,11},{10,... | collective-permute-start | bytes 2359304 | tf_op jit(solution)/shard_map/ppermute | solution.py:815
  14.4 26.4 %all-to-all-start = ((bf16[8,272,128]{2,1,0:T(8,128)(2,1)}), bf16[8,272,128]{2,1,0:T(8,128)(2,1)S(1)}, u32[]{:S(2)}, u32[]{:S(2)}) async-start(bf16[8,272,128]{2,1,0:T(8,128)(2,1)} %get-tuple-element.42), calls=%async_computation | async-start | bytes 1114112 | tf_op jit(solution)/shard_map/all_to_all | solution.py:788
  20.2 36.6 %collective-permute-start.3 = (bf16[512,1536]{1,0:T(8,128)(2,1)}, bf16[512,1536]{1,0:T(8,128)(2,1)S(1)}, u32[]{:S(2)}, u32[]{:S(2)}) collective-permute-start(bf16[512,1536]{1,0:T(8,128)(2,1)} %get-tuple-element.48), channel_id=1, source_target_pairs={{0,2},{1,3},{2,0},{3,1},{4,6},{5,7},{6,4},{7,5},{8,10},{9,11},{10,... | collective-permute-start | bytes 4718600 | tf_op jit(solution)/shard_map/ppermute | solution.py:815
  40.2 2.6 %collective-permute-start.2 = (bf16[256,1536]{1,0:T(8,128)(2,1)}, bf16[256,1536]{1,0:T(8,128)(2,1)S(1)}, u32[]{:S(2)}, u32[]{:S(2)}) collective-permute-start(bf16[256,1536]{1,0:T(8,128)(2,1)} %collective-permute-done.1.refs_5_), channel_id=1, source_target_pairs={{0,1},{1,0},{2,3},{3,2},{4,5},{5,4},{6,7},{7,6},{8,9},{9,8},{10,11... | collective-permute-start | bytes 2359304 | tf_op jit(solution)/shard_map/ppermute | solution.py:821
  56.7 7.6 %collective-permute-start.4 = (bf16[512,1536]{1,0:T(8,128)(2,1)S(1)}, bf16[512,1536]{1,0:T(8,128)(2,1)}, u32[]{:S(2)}, u32[]{:S(2)}) collective-permute-start(bf16[512,1536]{1,0:T(8,128)(2,1)S(1)} %collective-permute-done.3.refs_6_), channel_id=1, source_target_pairs={{0,1},{1,0},{2,3},{3,2},{4,5},{5,4},{6,7},{7,6},{8,9},{9,8},{10,11... | collective-permute-start | bytes 4718600 | tf_op jit(solution)/shard_map/ppermute | solution.py:821
  56.7 21.8 %collective-permute-start.5 = (bf16[256,1536]{1,0:T(8,128)(2,1)}, bf16[256,1536]{1,0:T(8,128)(2,1)S(1)}, u32[]{:S(2)}, u32[]{:S(2)}) collective-permute-start(bf16[256,1536]{1,0:T(8,128)(2,1)} %get-tuple-element.55), channel_id=1, source_target_pairs={{0,2},{1,3},{2,0},{3,1},{4,6},{5,7},{6,4},{7,5},{8,10},{9,11},{10,... | collective-permute-start | bytes 2359304 | tf_op jit(solution)/shard_map/ppermute | solution.py:815
  58.5 30.1 %all-to-all-start.2 = ((bf16[8,256,128]{2,1,0:T(8,128)(2,1)}), bf16[8,256,128]{2,1,0:T(8,128)(2,1)S(1)}, u32[]{:S(2)}, u32[]{:S(2)}) async-start(bf16[8,256,128]{2,1,0:T(8,128)(2,1)} %chain_states.2), calls=%async_computation.2 | async-start | bytes 1048576 | tf_op jit(solution)/shard_map/all_to_all | solution.py:788
  78.5 2.4 %collective-permute-start.6 = (bf16[256,1536]{1,0:T(8,128)(2,1)S(1)}, bf16[256,1536]{1,0:T(8,128)(2,1)S(1)}, u32[]{:S(2)}, u32[]{:S(2)}) collective-permute-start(bf16[256,1536]{1,0:T(8,128)(2,1)S(1)} %collective-permute-done.5.refs_0_), channel_id=1, source_target_pairs={{0,1},{1,0},{2,3},{3,2},{4,5},{5,4},{6,7},{7,6},{8,9},{9,8},{10,11... | collective-permute-start | bytes 2359304 | tf_op jit(solution)/shard_map/ppermute | solution.py:821
  88.6 20.8 %all-to-all-start.1 = ((bf16[8,256,128]{2,1,0:T(8,128)(2,1)}), bf16[8,256,128]{2,1,0:T(8,128)(2,1)S(1)}, u32[]{:S(2)}, u32[]{:S(2)}) async-start(bf16[8,256,128]{2,1,0:T(8,128)(2,1)} %bitcast.2), calls=%async_computation.1 | async-start | bytes 1048576 | tf_op jit(solution)/shard_map/all_to_all | solution.py:788
  110.9 19.3 %all-to-all-start.3 = ((bf16[8,256,128]{2,1,0:T(8,128)(2,1)}), bf16[8,256,128]{2,1,0:T(8,128)(2,1)S(1)}, u32[]{:S(2)}, u32[]{:S(2)}) async-start(bf16[8,256,128]{2,1,0:T(8,128)(2,1)} %chain_states.3), calls=%async_computation.3 | async-start | bytes 1048576 | tf_op jit(solution)/shard_map/all_to_all | solution.py:788

commit v8 on v7

--- a/solution.py
+++ b/solution.py
@@ -326,21 +326,21 @@
     total_ref[these] = jnp.stack(chained).astype(total_ref.dtype)
 
 
-def far_grad(near, pieces, w_ref, g, wide, side):
+def far_grad(near, pieces, places, w_ref, g, wide, side):
     part = pl.ds(pl.multiple_of(g * wide, wide), wide)
-    for n, piece in enumerate(pieces):
+    for n, piece in zip(places, pieces):
         at = 2 * (n // 2) + (side if n % 2 == 0 else 1 - side)
         near += mm(piece[...], w_ref[part, lanes_of(at, piece.shape[1])], NT)
     return near.astype(BF16)
 
 
-def far_products(blks, held, w_ref, near_ref, q_ref, cum_ref, prior_ref, before_ref, total_ref, grad_ref, sums_ref, side, ahead, after_group, ready):
+def far_products(blks, held, places, w_ref, near_ref, q_ref, cum_ref, prior_ref, before_ref, total_ref, grad_ref, sums_ref, side, ahead, after_group, ready):
     _, groups, group, _ = cum_ref.shape
     wide = group * HD
 
     def product(g):
         ready(g)
-        return far_grad(near_ref[:, lanes_of(g, wide)], held, w_ref, g, wide, side)
+        return far_grad(near_ref[:, lanes_of(g, wide)], held, places, w_ref, g, wide, side)
 
     def sums_of(g, grad):
         sums_refs = [sums_ref.at[n] for n in range(len(blks))]
@@ -441,7 +441,7 @@
     if groups > 2:
         start(loads(2))
     far_products(
-        blks, held, w_ref, near_ref, q_ref, cum_ref, prior_ref, before_ref if blks[0] else None, total_ref, grad_ref,
+        blks, held, range(len(held)), w_ref, near_ref, q_ref, cum_ref, prior_ref, before_ref if blks[0] else None, total_ref, grad_ref,
         sums_ref, side, ahead, lambda g: start(stores(g)), lambda g: wait(loads(g)),
     )
     wait(last_loads())
@@ -492,6 +492,36 @@
     return grad, rest[:count], total, rest[count:]
 
 
+def part_body(near_ref, w_ref, *refs):
+    pieces, out_ref = refs[:-1], refs[-1]
+    wide = PAIR * HD
+    side = lax.rem(lax.axis_index("tp"), 2)
+
+    def product(g):
+        part, lanes = pl.ds(pl.multiple_of(g * wide, wide), wide), lanes_of(g, wide)
+        total = near_ref[:, lanes]
+        for n, piece in enumerate(pieces):
+            total += mm(piece[...], w_ref[part, lanes_of(2 * n + side, piece.shape[1])], NT)
+        out_ref[:, lanes] = total
+
+    loop(near_ref.shape[1] // wide, product)
+
+
+def part_product(near, weight, pieces):
+    rows, width = near.shape
+    depth = pieces[0].shape[1]
+    (out,) = call(
+        part_body,
+        "part_product",
+        [(near, VMEM), (weight, VMEM)] + [(piece, VMEM) for piece in pieces],
+        [((rows, width), F32, VMEM)],
+        [],
+        4,
+        cost(2 * rows * width * len(pieces) * depth, 8 * rows * width),
+    )
+    return out
+
+
 def last_body(blk, before_ref, near_ref, q_ref, w_ref, cum_ref, prior_ref, *refs):
     pieces, (total_ref, grad_hbm, sums_hbm, grad_ref, sums_ref, sems) = refs[:-6], refs[-6:]
     _, groups, group, _ = cum_ref.shape
@@ -509,7 +539,7 @@
             copy.start()
 
     far_products(
-        [blk], pieces, w_ref, near_ref, q_ref, cum_ref, prior_ref, before_ref, total_ref, grad_ref,
+        [blk], pieces, range(1, 2 * len(pieces), 2), w_ref, near_ref, q_ref, cum_ref, prior_ref, before_ref, total_ref, grad_ref,
         sums_ref, lax.rem(lax.axis_index("tp"), 2), lambda g: None, after_group, lambda g: None,
     )
     for g in range(groups):
@@ -842,7 +872,12 @@
     next_grad, next_sums, total, kept = far_product(
         1, total, arrived, out_weight, near, queries, pair_cum, prior
     )
-    last_grad, last_sums, total = last_product(total, *kept, hand_on(2, next_grad), pair_cum, prior)
+    last_near, last_queries, far_weight = kept
+    arrived = hand_on(2, next_grad)
+    last_near = part_product(last_near, far_weight, arrived[::2])
+    last_grad, last_sums, total = last_product(
+        total, last_near, last_queries, far_weight, arrived[1::2], pair_cum, prior
+    )
     grads = [(0, first_grad)] + [(j, next_grad) for j in range(blk_count - 2)] + [(0, last_grad)]
     sums = [*sums, *next_sums, last_sums]
     gq, parts = None, []

time: 143 us -> 142 us (level)
  Pallas kernels: 104 us -> 106 us
  waiting for transfers between devices: 8.26 us -> 6.72 us
    ppermute x3, waiting for transfers between devices: 2.66 us -> 0.39 us  [hand_on(): arrived += [x, lax.ppermute(x, 'tp', core)]]
    pallas_call x11 -> x12, Pallas kernels: 104 us -> 106 us  [call(): pl.pallas_call(body, in_specs=[spec for _, spec in ins], out_specs=[spec...]
  transfers between devices with their start and end apart: 11 -> 11, of which waited for: 5 -> 4; matrix products, arithmetic and copies ran while one was open for 0% -> 0% of each run, Pallas kernels for 63% -> 65%
where the time goes in v8:
time: 142 us
  Pallas kernels  106 us (75%)
  starting transfers between devices  27.7 us (20%)
  waiting for transfers between devices  6.72 us (5%)
    pallas_call x12, Pallas kernels, call(): pl.pallas_call(body, in_specs=[spec for _, spec in ins], out_specs=[spec...  106 us
    all_to_all x4, starting transfers between devices, swap(): lax.all_to_all(flat, 'seq', 0, 0, tiled=True).reshape(devices, -1, HD)  22.2 us
    ppermute x3, starting transfers between devices, local(): lax.ppermute(x, 'tp', from_chip(d))  4.86 us
    ppermute x3, waiting for transfers between devices, local(): lax.ppermute(x, 'tp', from_chip(d))  4.08 us
  transfers between devices with their start and end apart: 11, of which 4 were waited for; matrix products, arithmetic and copies ran while one was open for 0% of the time, Pallas kernels for 65%

profile of v8, /device:TPU:0, one launch (start us, length us, event | category | flops | bytes accessed | tf_op | source)
XLA Modules:
  0.0 141.7 jit_solution(12584437965728548245)
XLA Ops:
  0.6 1.1 take_rows.1
  1.8 0.5 collective-permute-start
  2.3 2.6 %collective-permute-start.1 = (bf16[256,1536]{1,0:T(8,128)(2,1)S(1)}, bf16[256,1536]{1,0:T(8,128)(2,1)}, u32[]{:S(2)}, u32[]{:S(2)}) collective-permute-start(bf16[256,1536]{1,0:T(8,128)(2,1)S(1)} %take_rows.1), channel_id=1, source_target_pairs={{0,2},{1,3},{2,0},{3,1},{4,6},{5,7},{6,4},{7,5},{8,10},{9,11},{10,... | collective-permute-start | bytes 2359304 | tf_op jit(solution)/shard_map/ppermute | solution.py:845
  4.9 9.5 %key_totals.1 = (f32[4,16,128,128]{3,2,1,0:T(8,128)}, bf16[8,272,128]{2,1,0:T(8,128)(2,1)}, f32[4,4,4,256]{3,2,1,0:T(4,128)S(1)}, f32[4,8,2,256]{3,2,1,0:T(2,128...) custom-call(bf16[1024,2048]{1,0:T(8,128)(2,1)} %k_hbm.7, bf16[1024,2048]{1,0:T(8,128)(2,1)} %v_hbm.7, ...), custom_call_target="tpu_custom_call" | custom-call | flops 536870912 | bytes 12582912 | tf_op jit(solution)/shard_map/key_totals/pallas_call | solution.py:42
  14.4 5.8 %all-to-all-start = ((bf16[8,272,128]{2,1,0:T(8,128)(2,1)}), bf16[8,272,128]{2,1,0:T(8,128)(2,1)S(1)}, u32[]{:S(2)}, u32[]{:S(2)}) async-start(bf16[8,272,128]{2,1,0:T(8,128)(2,1)} %get-tuple-element.42), calls=%async_computation | async-start | bytes 1114112 | tf_op jit(solution)/shard_map/all_to_all | solution.py:818
  20.2 0.5 collective-permute-start.3
  20.7 19.5 %near_product.1.refs_0_.refs_1_ = f32[1024,2048]{1,0:T(8,128)} custom-call(bf16[1024,1536]{1,0:T(8,128)(2,1)} %grad_hbm.3, bf16[1024,1536]{1,0:T(8,128)(2,1)} %collective-permute-done.sibling_hbm, bf16[2048,6144]{1,0:T(8,128)(2,1)} %refs_5_.1), custom_call_target="tpu_custom_call" | custom-call | flops 12884901888 | bytes 27262976 | tf_op jit(solution)/shard_map/near_product/pallas_call | solution.py:42
  40.2 0.1 collective-permute-start.2
  40.3 0.1 slice.7
  40.4 0.2 copy.14
  40.6 0.2 reduce_window_sum.11
  40.7 0.0 all-to-all-done.got_ref
  40.8 0.1 constant_dynamic-slice_fusion.weight_ref
  40.9 1.5 %chain_states.2 = bf16[8,256,128]{2,1,0:T(8,128)(2,1)} custom-call(bf16[8,272,128]{2,1,0:T(8,128)(2,1)S(1)} %all-to-all-done.got_ref, f32[8,2]{1,0:T(8,128)S(1)} %constant_dynamic-slice_fusion.weight_ref), custom_call_target="tpu_custom_call" | custom-call | flops 524288 | bytes 1048576 | tf_op jit(solution)/shard_map/chain_states/pallas_call | solution.py:42
  42.4 0.4 collective-permute-done.2.refs_6_
  42.8 9.9 %far_product.2 = (f32[16,128,128]{2,1,0:T(8,128)}, bf16[256,2048]{1,0:T(8,128)(2,1)}, f32[16,128,128]{2,1,0:T(8,128)}) custom-call(f32[1024,2048]{1,0:T(8,128)} %near_product.1.refs_0_.refs_1_, bf16[1024,2048]{1,0:T(8,128)(2,1)} %q_hbm.3, f32[4,8,2,256]{3,2,1,0:T(2,128)S(1)} %get-tuple-element.44.refs_2_.refs_3_.cum_ref, ...), custom_call_target="tpu_custom_call" | custom-call | flops 3355443200 | bytes 21495808 | tf_op jit(solution)/shard_map/far_product/pallas_call | solution.py:42
  52.7 4.1 %collective-permute-done.3.refs_6_ = bf16[512,1536]{1,0:T(8,128)(2,1)S(1)} collective-permute-done((bf16[512,1536]{1,0:T(8,128)(2,1)}, bf16[512,1536]{1,0:T(8,128)(2,1)S(1)}, u32[]{:S(2)}, u32[]{:S(2)}) %collective-permute-start.3) | collective-permute-done | bytes 1572896 | tf_op jit(solution)/shard_map/ppermute | solution.py:845
  56.7 0.0 collective-permute-start.4
  56.7 1.8 %collective-permute-start.5 = (bf16[256,1536]{1,0:T(8,128)(2,1)}, bf16[256,1536]{1,0:T(8,128)(2,1)S(1)}, u32[]{:S(2)}, u32[]{:S(2)}) collective-permute-start(bf16[256,1536]{1,0:T(8,128)(2,1)} %get-tuple-element.54), channel_id=1, source_target_pairs={{0,2},{1,3},{2,0},{3,1},{4,6},{5,7},{6,4},{7,5},{8,10},{9,11},{10,... | collective-permute-start | bytes 2359304 | tf_op jit(solution)/shard_map/ppermute | solution.py:845
  58.5 5.8 %all-to-all-start.2 = ((bf16[8,256,128]{2,1,0:T(8,128)(2,1)}), bf16[8,256,128]{2,1,0:T(8,128)(2,1)S(1)}, u32[]{:S(2)}, u32[]{:S(2)}) async-start(bf16[8,256,128]{2,1,0:T(8,128)(2,1)} %chain_states.2), calls=%async_computation.2 | async-start | bytes 1048576 | tf_op jit(solution)/shard_map/all_to_all | solution.py:818
  64.3 14.2 %far_product.3 = (f32[16,128,128]{2,1,0:T(8,128)S(1)}, bf16[512,2048]{1,0:T(8,128)(2,1)}, f32[16,128,128]{2,1,0:T(8,128)}, f32[16,128,128]{2,1,0:T(8,128)}, f32[...) custom-call(f32[16,128,128]{2,1,0:T(8,128)} %get-tuple-element.47.refs_0_, ...), custom_call_target="tpu_custom_call" | custom-call | flops 6710886400 | bytes 27262976 | tf_op jit(solution)/shard_map/far_product/pallas_call | solution.py:42
  78.5 0.1 collective-permute-start.6
  78.6 3.3 %part_product.1.near_ref = f32[256,2048]{1,0:T(8,128)S(1)} custom-call(f32[256,2048]{1,0:T(8,128)S(1)} %get-tuple-element.52.near_ref, bf16[2048,3072]{1,0:T(8,128)(2,1)S(1)} %get-tuple-element.53.w_ref, bf16[256,1536]{1,0:T(8,128)(2,1)S(1)} %collective-permute-done.5.refs_0_), custom_call_target="tpu_custom_call" | custom-call | flops 1610612736 | bytes 4194304 | tf_op jit(solution)/shard_map/part_product/pallas_call | solution.py:42
  81.9 6.1 %last_product.1 = (bf16[16,128,128]{2,1,0:T(8,128)(2,1)}, bf16[256,2048]{1,0:T(8,128)(2,1)}, f32[16,128,128]{2,1,0:T(8,128)}) custom-call(f32[16,128,128]{2,1,0:T(8,128)S(1)} %get-tuple-element.51.before_ref, f32[256,2048]{1,0:T(8,128)S(1)} %part_product.1.near_ref, bf16[256,2048]{1,0:T(8,128)(2,1)S(1)} %get-tuple-element.56.q_ref, ...), custom_call_target="tpu_custom_call" | custom-call | tf_op jit(solution)/shard_map/last_product/pallas_call | solution.py:42
  88.0 6.0 %all-to-all-start.1 = ((bf16[8,256,128]{2,1,0:T(8,128)(2,1)}), bf16[8,256,128]{2,1,0:T(8,128)(2,1)S(1)}, u32[]{:S(2)}, u32[]{:S(2)}) async-start(bf16[8,256,128]{2,1,0:T(8,128)(2,1)} %bitcast.2), calls=%async_computation.1 | async-start | bytes 1048576 | tf_op jit(solution)/shard_map/all_to_all | solution.py:818
  94.0 13.7 %block_terms.2 = (bf16[1024,2048]{1,0:T(8,128)(2,1)}, bf16[512,2048]{1,0:T(8,128)(2,1)}, bf16[512,2048]{1,0:T(8,128)(2,1)}) custom-call(bf16[1024,2048]{1,0:T(8,128)(2,1)} %q_hbm.3, bf16[1024,2048]{1,0:T(8,128)(2,1)} %k_hbm.7, bf16[1024,2048]{1,0:T(8,128)(2,1)} %v_hbm.7, bf16[256,2048]{1,0:T(8,128)(2,1)} %get-tuple-element.59.refs_0_, ...), custom_call_target="tpu_custom_call" | custom-call | flops 2952790016 | bytes 17825792 | tf_op jit(solution)/shard_map/block_terms/pallas_call | solution.py:42
  107.7 1.4 all-to-all-done.1.got_ref
  109.1 1.5 %chain_states.3 = bf16[8,256,128]{2,1,0:T(8,128)(2,1)} custom-call(bf16[8,256,128]{2,1,0:T(8,128)(2,1)S(1)} %all-to-all-done.1.got_ref, f32[8,2]{1,0:T(8,128)S(1)} %constant_dynamic-slice_fusion.weight_ref), custom_call_target="tpu_custom_call" | custom-call | flops 524288 | bytes 1048576 | tf_op jit(solution)/shard_map/chain_states/pallas_call | solution.py:42
  110.7 4.6 %all-to-all-start.3 = ((bf16[8,256,128]{2,1,0:T(8,128)(2,1)}), bf16[8,256,128]{2,1,0:T(8,128)(2,1)S(1)}, u32[]{:S(2)}, u32[]{:S(2)}) async-start(bf16[8,256,128]{2,1,0:T(8,128)(2,1)} %chain_states.3), calls=%async_computation.3 | async-start | bytes 1048576 | tf_op jit(solution)/shard_map/all_to_all | solution.py:818
  115.3 13.8 %block_terms.3 = (bf16[1024,2048]{1,0:T(8,128)(2,1)}, bf16[512,2048]{1,0:T(8,128)(2,1)}, bf16[512,2048]{1,0:T(8,128)(2,1)}) custom-call(bf16[1024,2048]{1,0:T(8,128)(2,1)} %q_hbm.3, bf16[1024,2048]{1,0:T(8,128)(2,1)} %k_hbm.7, bf16[1024,2048]{1,0:T(8,128)(2,1)} %v_hbm.7, ...), custom_call_target="tpu_custom_call", output_to_operand_aliasing={{0}: (9, {})} | custom-call | flops 2952790016 | bytes 17825792 | tf_op jit(solution)/shard_map/block_terms/pallas_call | solution.py:42
  129.0 0.8 all-to-all-done.3
  129.9 11.7 %later_terms.1 = (bf16[1024,2048]{1,0:T(8,128)(2,1)}, bf16[1024,2048]{1,0:T(8,128)(2,1)}) custom-call(bf16[1024,2048]{1,0:T(8,128)(2,1)} %k_hbm.7, bf16[1024,2048]{1,0:T(8,128)(2,1)} %v_hbm.7, f32[4,4,4,256]{3,2,1,0:T(4,128)S(1)} %get-tuple-element.64.refs_2_.cum_ref, bf16[16,128,128]{2,1,0:T(8,128)(2,1)S(1)} %bitcast.8, ...), custom_call_target="tpu_custom_call" | custom-call | flops 1073741824 | bytes 29360128 | tf_op jit(solution)/shard_map/later_terms/pallas_call | solution.py:42
  (9 shorter events, 0.0 us)
Async XLA Ops:
  1.8 18.9 %collective-permute-start = (bf16[1024,1536]{1,0:T(8,128)(2,1)}, bf16[1024,1536]{1,0:T(8,128)(2,1)}, u32[]{:S(2)}, u32[]{:S(2)}) collective-permute-start(bf16[1024,1536]{1,0:T(8,128)(2,1)} %grad_hbm.3), channel_id=1, source_target_pairs={{0,1},{1,0},{2,3},{3,2},{4,5},{5,4},{6,7},{7,6},{8,9},{9,8},{10,11... | collective-permute-start | bytes 9437192 | tf_op jit(solution)/shard_map/ppermute | solution.py:840
  2.3 37.9 %collective-permute-start.1 = (bf16[256,1536]{1,0:T(8,128)(2,1)S(1)}, bf16[256,1536]{1,0:T(8,128)(2,1)}, u32[]{:S(2)}, u32[]{:S(2)}) collective-permute-start(bf16[256,1536]{1,0:T(8,128)(2,1)S(1)} %take_rows.1), channel_id=1, source_target_pairs={{0,2},{1,3},{2,0},{3,1},{4,6},{5,7},{6,4},{7,5},{8,10},{9,11},{10,... | collective-permute-start | bytes 2359304 | tf_op jit(solution)/shard_map/ppermute | solution.py:845
  14.4 26.4 %all-to-all-start = ((bf16[8,272,128]{2,1,0:T(8,128)(2,1)}), bf16[8,272,128]{2,1,0:T(8,128)(2,1)S(1)}, u32[]{:S(2)}, u32[]{:S(2)}) async-start(bf16[8,272,128]{2,1,0:T(8,128)(2,1)} %get-tuple-element.42), calls=%async_computation | async-start | bytes 1114112 | tf_op jit(solution)/shard_map/all_to_all | solution.py:818
  20.2 36.6 %collective-permute-start.3 = (bf16[512,1536]{1,0:T(8,128)(2,1)}, bf16[512,1536]{1,0:T(8,128)(2,1)S(1)}, u32[]{:S(2)}, u32[]{:S(2)}) collective-permute-start(bf16[512,1536]{1,0:T(8,128)(2,1)} %get-tuple-element.48), channel_id=1, source_target_pairs={{0,2},{1,3},{2,0},{3,1},{4,6},{5,7},{6,4},{7,5},{8,10},{9,11},{10,... | collective-permute-start | bytes 4718600 | tf_op jit(solution)/shard_map/ppermute | solution.py:845
  40.2 2.6 %collective-permute-start.2 = (bf16[256,1536]{1,0:T(8,128)(2,1)}, bf16[256,1536]{1,0:T(8,128)(2,1)S(1)}, u32[]{:S(2)}, u32[]{:S(2)}) collective-permute-start(bf16[256,1536]{1,0:T(8,128)(2,1)} %collective-permute-done.1.refs_5_), channel_id=1, source_target_pairs={{0,1},{1,0},{2,3},{3,2},{4,5},{5,4},{6,7},{7,6},{8,9},{9,8},{10,11... | collective-permute-start | bytes 2359304 | tf_op jit(solution)/shard_map/ppermute | solution.py:851
  56.7 7.6 %collective-permute-start.4 = (bf16[512,1536]{1,0:T(8,128)(2,1)S(1)}, bf16[512,1536]{1,0:T(8,128)(2,1)}, u32[]{:S(2)}, u32[]{:S(2)}) collective-permute-start(bf16[512,1536]{1,0:T(8,128)(2,1)S(1)} %collective-permute-done.3.refs_6_), channel_id=1, source_target_pairs={{0,1},{1,0},{2,3},{3,2},{4,5},{5,4},{6,7},{7,6},{8,9},{9,8},{10,11... | collective-permute-start | bytes 4718600 | tf_op jit(solution)/shard_map/ppermute | solution.py:851
  56.7 21.8 %collective-permute-start.5 = (bf16[256,1536]{1,0:T(8,128)(2,1)}, bf16[256,1536]{1,0:T(8,128)(2,1)S(1)}, u32[]{:S(2)}, u32[]{:S(2)}) collective-permute-start(bf16[256,1536]{1,0:T(8,128)(2,1)} %get-tuple-element.54), channel_id=1, source_target_pairs={{0,2},{1,3},{2,0},{3,1},{4,6},{5,7},{6,4},{7,5},{8,10},{9,11},{10,... | collective-permute-start | bytes 2359304 | tf_op jit(solution)/shard_map/ppermute | solution.py:845
  58.5 29.5 %all-to-all-start.2 = ((bf16[8,256,128]{2,1,0:T(8,128)(2,1)}), bf16[8,256,128]{2,1,0:T(8,128)(2,1)S(1)}, u32[]{:S(2)}, u32[]{:S(2)}) async-start(bf16[8,256,128]{2,1,0:T(8,128)(2,1)} %chain_states.2), calls=%async_computation.2 | async-start | bytes 1048576 | tf_op jit(solution)/shard_map/all_to_all | solution.py:818
  78.5 3.4 %collective-permute-start.6 = (bf16[256,1536]{1,0:T(8,128)(2,1)S(1)}, bf16[256,1536]{1,0:T(8,128)(2,1)S(1)}, u32[]{:S(2)}, u32[]{:S(2)}) collective-permute-start(bf16[256,1536]{1,0:T(8,128)(2,1)S(1)} %collective-permute-done.5.refs_0_), channel_id=1, source_target_pairs={{0,1},{1,0},{2,3},{3,2},{4,5},{5,4},{6,7},{7,6},{8,9},{9,8},{10,11... | collective-permute-start | bytes 2359304 | tf_op jit(solution)/shard_map/ppermute | solution.py:851
  88.0 21.2 %all-to-all-start.1 = ((bf16[8,256,128]{2,1,0:T(8,128)(2,1)}), bf16[8,256,128]{2,1,0:T(8,128)(2,1)S(1)}, u32[]{:S(2)}, u32[]{:S(2)}) async-start(bf16[8,256,128]{2,1,0:T(8,128)(2,1)} %bitcast.2), calls=%async_computation.1 | async-start | bytes 1048576 | tf_op jit(solution)/shard_map/all_to_all | solution.py:818
  110.7 19.2 %all-to-all-start.3 = ((bf16[8,256,128]{2,1,0:T(8,128)(2,1)}), bf16[8,256,128]{2,1,0:T(8,128)(2,1)S(1)}, u32[]{:S(2)}, u32[]{:S(2)}) async-start(bf16[8,256,128]{2,1,0:T(8,128)(2,1)} %chain_states.3), calls=%async_computation.3 | async-start | bytes 1048576 | tf_op jit(solution)/shard_map/all_to_all | solution.py:818
